TPU v7x, 32 devices: a whole 2x2x4 slice. The times are simulated.
32 devices in a mesh: fsdp: 32 (over z, y, x, core).
Axes of the slice: x: 2, y: 2, z: 4, core: 2. Of those that a mesh axis runs over, the one named last changes fastest.
Arguments:
- slow_in: bfloat16 [512, 14, 14, 1024], P('fsdp'), may hold values from -6 to 6
- fast_in: bfloat16 [2048, 14, 14, 128], P('fsdp'), may hold values from -6 to 6
- clip_ids: int32 [32, 16], P('fsdp'), may hold values from 0 to 7, never falling along the last dimension, each value on 1 to 8 neighbouring positions
- lateral_weight: bfloat16 [640, 256], P(None, 'fsdp'), may hold values from -0.25 to 0.25
- first_weight: bfloat16 [3840, 256], P('fsdp'), may hold values from -0.09375 to 0.09375
- middle_weight: bfloat16 [2304, 256], P('fsdp'), may hold values from -0.125 to 0.125
- last_weight: bfloat16 [256, 1024], P('fsdp'), may hold values from -0.375 to 0.375
- proj_weight: bfloat16 [1280, 1024], P('fsdp'), may hold values from -0.15625 to 0.15625
- lat_norm: bfloat16 [2, 256], P(None, 'fsdp'), may hold values from 0.099609375 to 1.8984375
- one_norm: bfloat16 [2, 256], P(None, 'fsdp'), may hold values from 0.099609375 to 1.8984375
- two_norm: bfloat16 [2, 256], P(None, 'fsdp'), may hold values from 0.099609375 to 1.8984375
- out_norm: bfloat16 [2, 1024], P(None, 'fsdp'), may hold values from 0.099609375 to 1.8984375
- proj_norm: bfloat16 [2, 1024], P(None, 'fsdp'), may hold values from 0.099609375 to 1.8984375
- fast_first: bfloat16 [384, 32], replicated, may hold values from -0.3125 to 0.3125
- fast_middle: bfloat16 [288, 32], replicated, may hold values from -0.375 to 0.375
- fast_last: bfloat16 [32, 128], replicated, may hold values from -1 to 1
- fast_proj: bfloat16 [128, 128], replicated, may hold values from -0.5 to 0.5
- fast_mid_norm: bfloat16 [2, 2, 32], replicated, may hold values from 0.099609375 to 1.8984375
- fast_out_norm: bfloat16 [2, 2, 128], replicated, may hold values from 0.099609375 to 1.8984375
- slow_cot: bfloat16 [512, 14, 14, 1024], P('fsdp'), may hold values from -6 to 6
- fast_cot: bfloat16 [2048, 14, 14, 128], P('fsdp'), may hold values from -6 to 6
Outputs:
- slow_out: bfloat16 [512, 14, 14, 1024], P('fsdp')
- fast_out: bfloat16 [2048, 14, 14, 128], P('fsdp')
- slow_in_grad: bfloat16 [512, 14, 14, 1024], P('fsdp')
- fast_in_grad: bfloat16 [2048, 14, 14, 128], P('fsdp')
- lateral_grad: float32 [640, 256], P(None, 'fsdp')
- first_grad: float32 [3840, 256], P('fsdp')
- middle_grad: float32 [2304, 256], P('fsdp')
- last_grad: float32 [256, 1024], P('fsdp')
- proj_grad: float32 [1280, 1024], P('fsdp')
- lat_norm_grad: float32 [2, 256], P(None, 'fsdp')
- one_norm_grad: float32 [2, 256], P(None, 'fsdp')
- two_norm_grad: float32 [2, 256], P(None, 'fsdp')
- out_norm_grad: float32 [2, 1024], P(None, 'fsdp')
- proj_norm_grad: float32 [2, 1024], P(None, 'fsdp')
- fast_first_grad: float32 [384, 32], replicated
- fast_middle_grad: float32 [288, 32], replicated
- fast_last_grad: float32 [32, 128], replicated
- fast_proj_grad: float32 [128, 128], replicated
- fast_mid_norm_grad: float32 [2, 2, 32], replicated
- fast_out_norm_grad: float32 [2, 2, 128], replicated
Inputs may be any that keep to these rules, and one draw needn't show every extreme that they name: `clip_ids`: each row holds the slow frames of one device in 8 clips; clip numbers never fall along a row and a clip never continues into the next row; each clip has 1 to 8 frames, and every row holds at least one clip of exactly 8 frames.
All inputs are finite; a program needn't handle non-finite values.
Results may differ from a plain program's by a relative error of at most 0.0089.
Values may be sent and summed in bfloat16 or wider, within the bound.
A program may use at most 384 MiB of HBM per device.

v0:
```python
import jax
import jax.numpy as jnp
from jax import lax
from jax.sharding import PartitionSpec as P

EPSILON = 1e-05


def product(operand, weight):
    return jnp.einsum("fhwc,cd->fhwd", operand, weight, preferred_element_type=jnp.float32)


def back_product(gradient, weight):
    return jnp.einsum("fhwd,cd->fhwc", gradient, weight, preferred_element_type=jnp.float32)


def weight_term(columns, gradient):
    return jnp.einsum("fhwc,fhwd->cd", columns, gradient, preferred_element_type=jnp.float32)


def clip_edges(clip_ids):
    same = clip_ids[:, 1:] == clip_ids[:, :-1]
    closed = jnp.zeros((clip_ids.shape[0], 1), dtype=bool)
    has_prev = jnp.concatenate([closed, same], axis=1).reshape(-1)
    has_next = jnp.concatenate([same, closed], axis=1).reshape(-1)
    return (has_prev, has_next)


def fast_edges(has_prev, has_next):
    within = jnp.arange(4)
    fast_prev = ((within[None, :] != 0) | has_prev[:, None]).reshape(-1)
    fast_next = ((within[None, :] != 3) | has_next[:, None]).reshape(-1)
    return (fast_prev, fast_next)


def masked(field, keep_mask):
    return jnp.where(keep_mask[:, None, None, None], field, jnp.zeros_like(field))


def shift_down(field):
    return jnp.concatenate([jnp.zeros_like(field[:1]), field[:-1]], axis=0)


def shift_up(field):
    return jnp.concatenate([field[1:], jnp.zeros_like(field[:1])], axis=0)


def temporal_cols(field, has_prev, has_next):
    return jnp.concatenate(
        [masked(shift_down(field), has_prev), field, masked(shift_up(field), has_next)], axis=-1
    )


def temporal_back(grad_cols, has_prev, has_next):
    width = grad_cols.shape[-1] // 3
    before = masked(grad_cols[..., :width], has_prev)
    after = masked(grad_cols[..., 2 * width :], has_next)
    return grad_cols[..., width : 2 * width] + shift_up(before) + shift_down(after)


def spatial_cols(field):
    extent = field.shape[1]
    padded = jnp.pad(field, ((0, 0), (1, 1), (1, 1), (0, 0)))
    pieces = []
    for row_off in range(3):
        for col_off in range(3):
            pieces.append(padded[:, row_off : row_off + extent, col_off : col_off + extent, :])
    return jnp.concatenate(pieces, axis=-1)


def spatial_back(grad_cols):
    width = grad_cols.shape[-1] // 9
    extent = grad_cols.shape[1]
    total = None
    for position in range(9):
        row_off = position // 3
        col_off = position % 3
        piece = grad_cols[..., position * width : (position + 1) * width]
        placed = jnp.pad(piece, ((0, 0), (row_off, 2 - row_off), (col_off, 2 - col_off), (0, 0)))
        total = placed if total is None else total + placed
    return total[:, 1 : 1 + extent, 1 : 1 + extent, :]


def lateral_cols(fast, has_prev):
    frames = fast.shape[0] // 4
    grouped = fast.reshape((frames, 4) + fast.shape[1:])
    return jnp.concatenate(
        [
            masked(shift_down(grouped[:, 2]), has_prev),
            masked(shift_down(grouped[:, 3]), has_prev),
            grouped[:, 0],
            grouped[:, 1],
            grouped[:, 2],
        ],
        axis=-1,
    )


def lateral_back(grad_cols, has_prev):
    width = grad_cols.shape[-1] // 5
    parts = [grad_cols[..., tap * width : (tap + 1) * width] for tap in range(5)]
    from_two = shift_up(masked(parts[0], has_prev))
    from_three = shift_up(masked(parts[1], has_prev))
    grouped = jnp.stack([parts[2], parts[3], parts[4] + from_two, from_three], axis=1)
    return grouped.reshape((grouped.shape[0] * 4,) + grouped.shape[2:])


def split_channels(joined_sums, widths, counts):
    pieces = []
    offset = 0
    for width, count in zip(widths, counts):
        pieces.append(joined_sums[offset : offset + width] / count)
        offset += width
    return pieces


def gather_stats(fields):
    devices = lax.axis_size("fsdp")
    widths = [field.shape[-1] for field in fields]
    counts = [field.shape[0] * field.shape[1] * field.shape[2] * devices for field in fields]
    local_sums = jnp.concatenate([jnp.sum(field, axis=(0, 1, 2)) for field in fields])
    totals = lax.psum(local_sums, "fsdp")
    averages = split_channels(totals, widths, counts)
    local_spread = jnp.concatenate(
        [
            jnp.sum(jnp.square(field - average), axis=(0, 1, 2))
            for field, average in zip(fields, averages)
        ]
    )
    spreads = lax.psum(local_spread, "fsdp")
    variances = split_channels(spreads, widths, counts)
    return [
        (average, lax.rsqrt(variance + EPSILON)) for average, variance in zip(averages, variances)
    ]


def reduce_norms(pairs):
    firsts = jnp.concatenate([jnp.sum(grad_out, axis=(0, 1, 2)) for grad_out, normed in pairs])
    seconds = jnp.concatenate(
        [jnp.sum(grad_out * normed, axis=(0, 1, 2)) for grad_out, normed in pairs]
    )
    sum_all, cross_all = lax.psum((firsts, seconds), "fsdp")
    result = []
    offset = 0
    for grad_out, normed in pairs:
        width = grad_out.shape[-1]
        result.append((sum_all[offset : offset + width], cross_all[offset : offset + width]))
        offset += width
    return result


def normalize(field, stats):
    average, inverse = stats
    return (field - average) * inverse


def affine(normed, norm_pair):
    pair = norm_pair.astype(jnp.float32)
    return normed * pair[0] + pair[1]


def silu_slope(field):
    sigma = jax.nn.sigmoid(field)
    return sigma * (1.0 + field * (1.0 - sigma))


def norm_input_grad(grad_out, normed, norm_pair, inverse, totals, count):
    sum_grad, sum_cross = totals
    gain = norm_pair[0].astype(jnp.float32)
    return (gain * inverse * (grad_out - sum_grad / count - normed * (sum_cross / count))).astype(
        jnp.bfloat16
    )


def pair_grad(totals):
    return jnp.stack([totals[1], totals[0]])


def own_columns(full_grad):
    share = full_grad.shape[1] // lax.axis_size("fsdp")
    return lax.dynamic_slice_in_dim(full_grad, lax.axis_index("fsdp") * share, share, 1)


def shards(
    slow_in,
    fast_in,
    clip_ids,
    lateral_weight,
    first_weight,
    middle_weight,
    last_weight,
    proj_weight,
    lat_norm,
    one_norm,
    two_norm,
    out_norm,
    proj_norm,
    fast_first,
    fast_middle,
    fast_last,
    fast_proj,
    fast_mid_norm,
    fast_out_norm,
    slow_cot,
    fast_cot,
):
    gathered = (
        lax.all_gather(lateral_weight, "fsdp", axis=1, tiled=True),
        lax.all_gather(first_weight, "fsdp", axis=0, tiled=True),
        lax.all_gather(middle_weight, "fsdp", axis=0, tiled=True),
        lax.all_gather(last_weight, "fsdp", axis=0, tiled=True),
        lax.all_gather(proj_weight, "fsdp", axis=0, tiled=True),
        lax.all_gather(lat_norm, "fsdp", axis=1, tiled=True),
        lax.all_gather(one_norm, "fsdp", axis=1, tiled=True),
        lax.all_gather(two_norm, "fsdp", axis=1, tiled=True),
        lax.all_gather(out_norm, "fsdp", axis=1, tiled=True),
        lax.all_gather(proj_norm, "fsdp", axis=1, tiled=True),
    )
    (
        lateral_full,
        first_full,
        middle_full,
        last_full,
        proj_full,
        gain_lat,
        gain_one,
        gain_two,
        gain_out,
        gain_proj,
    ) = gathered
    has_prev, has_next = clip_edges(clip_ids)
    fast_prev, fast_next = fast_edges(has_prev, has_next)
    devices = lax.axis_size("fsdp")
    slow_count = slow_in.shape[0] * slow_in.shape[1] * slow_in.shape[2] * devices
    fast_count = 4 * slow_count
    lat_cols = lateral_cols(fast_in, has_prev)
    lat_pre = product(lat_cols, lateral_full)
    fone_cols = temporal_cols(fast_in, fast_prev, fast_next)
    fone_pre = product(fone_cols, fast_first)
    fproj_pre = product(fast_in, fast_proj)
    lat_stats, fone_stats, fproj_stats = gather_stats([lat_pre, fone_pre, fproj_pre])
    lat_hat = normalize(lat_pre, lat_stats)
    lat_act = affine(lat_hat, gain_lat)
    lateral = jax.nn.silu(lat_act).astype(jnp.bfloat16)
    fone_hat = normalize(fone_pre, fone_stats)
    fone_act = affine(fone_hat, fast_mid_norm[0])
    fone = jax.nn.silu(fone_act).astype(jnp.bfloat16)
    fproj_hat = normalize(fproj_pre, fproj_stats)
    joined = jnp.concatenate([slow_in, lateral], axis=-1)
    one_cols = temporal_cols(joined, has_prev, has_next)
    one_pre = product(one_cols, first_full)
    proj_pre = product(joined, proj_full)
    ftwo_cols = spatial_cols(fone)
    ftwo_pre = product(ftwo_cols, fast_middle)
    one_stats, proj_stats, ftwo_stats = gather_stats([one_pre, proj_pre, ftwo_pre])
    one_hat = normalize(one_pre, one_stats)
    one_act = affine(one_hat, gain_one)
    one = jax.nn.silu(one_act).astype(jnp.bfloat16)
    proj_hat = normalize(proj_pre, proj_stats)
    ftwo_hat = normalize(ftwo_pre, ftwo_stats)
    ftwo_act = affine(ftwo_hat, fast_mid_norm[1])
    ftwo = jax.nn.silu(ftwo_act).astype(jnp.bfloat16)
    two_cols = spatial_cols(one)
    two_pre = product(two_cols, middle_full)
    fthree_pre = product(ftwo, fast_last)
    two_stats, fthree_stats = gather_stats([two_pre, fthree_pre])
    two_hat = normalize(two_pre, two_stats)
    two_act = affine(two_hat, gain_two)
    two = jax.nn.silu(two_act).astype(jnp.bfloat16)
    fthree_hat = normalize(fthree_pre, fthree_stats)
    three_pre = product(two, last_full)
    three_stats = gather_stats([three_pre])[0]
    three_hat = normalize(three_pre, three_stats)
    slow_sum = affine(three_hat, gain_out) + affine(proj_hat, gain_proj)
    slow_out = jax.nn.silu(slow_sum).astype(jnp.bfloat16)
    fast_sum = affine(fthree_hat, fast_out_norm[0]) + affine(fproj_hat, fast_out_norm[1])
    fast_out = jax.nn.silu(fast_sum).astype(jnp.bfloat16)
    slow_delta = slow_cot.astype(jnp.float32) * silu_slope(slow_sum)
    fast_delta = fast_cot.astype(jnp.float32) * silu_slope(fast_sum)
    outer = reduce_norms(
        [
            (slow_delta, three_hat),
            (slow_delta, proj_hat),
            (fast_delta, fthree_hat),
            (fast_delta, fproj_hat),
        ]
    )
    three_d = norm_input_grad(slow_delta, three_hat, gain_out, three_stats[1], outer[0], slow_count)
    proj_d = norm_input_grad(slow_delta, proj_hat, gain_proj, proj_stats[1], outer[1], slow_count)
    fthree_d = norm_input_grad(
        fast_delta, fthree_hat, fast_out_norm[0], fthree_stats[1], outer[2], fast_count
    )
    fproj_d = norm_input_grad(
        fast_delta, fproj_hat, fast_out_norm[1], fproj_stats[1], outer[3], fast_count
    )
    last_term = weight_term(two, three_d)
    proj_term = weight_term(joined, proj_d)
    fthree_term = weight_term(ftwo, fthree_d)
    fproj_term = weight_term(fast_in, fproj_d)
    two_delta = back_product(three_d, last_full) * silu_slope(two_act)
    ftwo_delta = back_product(fthree_d, fast_last) * silu_slope(ftwo_act)
    middle_sums = reduce_norms([(two_delta, two_hat), (ftwo_delta, ftwo_hat)])
    two_d = norm_input_grad(two_delta, two_hat, gain_two, two_stats[1], middle_sums[0], slow_count)
    ftwo_d = norm_input_grad(
        ftwo_delta, ftwo_hat, fast_mid_norm[1], ftwo_stats[1], middle_sums[1], fast_count
    )
    middle_term = weight_term(two_cols, two_d)
    fmiddle_term = weight_term(ftwo_cols, ftwo_d)
    one_delta = spatial_back(back_product(two_d, middle_full)) * silu_slope(one_act)
    fone_delta = spatial_back(back_product(ftwo_d, fast_middle)) * silu_slope(fone_act)
    inner_sums = reduce_norms([(one_delta, one_hat), (fone_delta, fone_hat)])
    one_d = norm_input_grad(one_delta, one_hat, gain_one, one_stats[1], inner_sums[0], slow_count)
    fone_d = norm_input_grad(
        fone_delta, fone_hat, fast_mid_norm[0], fone_stats[1], inner_sums[1], fast_count
    )
    first_term = weight_term(one_cols, one_d)
    ffirst_term = weight_term(fone_cols, fone_d)
    joined_grad = temporal_back(back_product(one_d, first_full), has_prev, has_next) + back_product(
        proj_d, proj_full
    )
    width_in = slow_in.shape[-1]
    slow_in_grad = joined_grad[..., :width_in].astype(jnp.bfloat16)
    lat_delta = joined_grad[..., width_in:] * silu_slope(lat_act)
    lat_sums = reduce_norms([(lat_delta, lat_hat)])
    lat_d = norm_input_grad(lat_delta, lat_hat, gain_lat, lat_stats[1], lat_sums[0], slow_count)
    lateral_term = weight_term(lat_cols, lat_d)
    fast_in_grad = (
        lateral_back(back_product(lat_d, lateral_full), has_prev)
        + temporal_back(back_product(fone_d, fast_first), fast_prev, fast_next)
        + back_product(fproj_d, fast_proj)
    ).astype(jnp.bfloat16)
    shares = (
        lax.psum_scatter(lateral_term, "fsdp", scatter_dimension=1, tiled=True),
        lax.psum_scatter(first_term, "fsdp", scatter_dimension=0, tiled=True),
        lax.psum_scatter(middle_term, "fsdp", scatter_dimension=0, tiled=True),
        lax.psum_scatter(last_term, "fsdp", scatter_dimension=0, tiled=True),
        lax.psum_scatter(proj_term, "fsdp", scatter_dimension=0, tiled=True),
    )
    lateral_grad, first_grad, middle_grad, last_grad, proj_grad = shares
    fast_shares = lax.psum((ffirst_term, fmiddle_term, fthree_term, fproj_term), "fsdp")
    lat_norm_grad = own_columns(pair_grad(lat_sums[0]))
    one_norm_grad = own_columns(pair_grad(inner_sums[0]))
    two_norm_grad = own_columns(pair_grad(middle_sums[0]))
    out_norm_grad = own_columns(pair_grad(outer[0]))
    proj_norm_grad = own_columns(pair_grad(outer[1]))
    fast_mid_norm_grad = jnp.stack([pair_grad(inner_sums[1]), pair_grad(middle_sums[1])])
    fast_out_norm_grad = jnp.stack([pair_grad(outer[2]), pair_grad(outer[3])])
    return (
        slow_out,
        fast_out,
        slow_in_grad,
        fast_in_grad,
        lateral_grad,
        first_grad,
        middle_grad,
        last_grad,
        proj_grad,
        lat_norm_grad,
        one_norm_grad,
        two_norm_grad,
        out_norm_grad,
        proj_norm_grad,
        fast_shares[0],
        fast_shares[1],
        fast_shares[2],
        fast_shares[3],
        fast_mid_norm_grad,
        fast_out_norm_grad,
    )


def solution(mesh):
    in_specs = (
        P("fsdp", None, None, None),
        P("fsdp", None, None, None),
        P("fsdp", None),
        P(None, "fsdp"),
        P("fsdp", None),
        P("fsdp", None),
        P("fsdp", None),
        P("fsdp", None),
        P(None, "fsdp"),
        P(None, "fsdp"),
        P(None, "fsdp"),
        P(None, "fsdp"),
        P(None, "fsdp"),
        P(),
        P(),
        P(),
        P(),
        P(),
        P(),
        P("fsdp", None, None, None),
        P("fsdp", None, None, None),
    )
    out_specs = (
        P("fsdp", None, None, None),
        P("fsdp", None, None, None),
        P("fsdp", None, None, None),
        P("fsdp", None, None, None),
        P(None, "fsdp"),
        P("fsdp", None),
        P("fsdp", None),
        P("fsdp", None),
        P("fsdp", None),
        P(None, "fsdp"),
        P(None, "fsdp"),
        P(None, "fsdp"),
        P(None, "fsdp"),
        P(None, "fsdp"),
        P(),
        P(),
        P(),
        P(),
        P(),
        P(),
    )
    return jax.shard_map(shards, mesh=mesh, in_specs=in_specs, out_specs=out_specs, check_vma=False)
```

profile of v0, /device:TPU:0, one launch (start us, length us, event | category | flops | bytes accessed | tf_op | source)
XLA Modules:
  0.0 1946.9 jit_solution(17432601938069787687)
XLA Ops:
  27.0 44.6 %all_gather.30 = bf16[640,256]{0,1:T(8,128)(2,1)S(1)} all-gather(bf16[640,8]{0,1:T(8,128)(2,1)S(1)} %copy-done.82), channel_id=1, replica_groups=mesh['fsdp'=32] {'fsdp'}, dimensions={1}, use_global_device_ids=true | all-gather | bytes 337920 | tf_op jit(solution)/shard_map/all_gather | solution.py:208
  97.0 37.4 %psum.140 = f32[416]{0:T(512)S(1)} all-reduce(f32[416]{0:T(512)S(1)} %pad_maximum_fusion.18), channel_id=1, replica_groups=mesh['fsdp'=32] {'fsdp'}, use_global_device_ids=true, to_apply=%region_3.4 | all-reduce | flops 416 | bytes 3328 | tf_op jit(solution)/shard_map/psum | solution.py:122
  134.6 40.2 %all-gather = bf16[32,8,2]{1,2,0:T(2,128)(2,1)S(1)} all-gather(bf16[1,8,2]{1,2,0:T(2,128)(2,1)S(1)} %bitcast.348), channel_id=1, replica_groups=mesh['fsdp'=32] {'fsdp'}, dimensions={0}, use_global_device_ids=true | all-gather | bytes 1056 | tf_op jit(solution)/shard_map/all_gather | solution.py:213
  174.9 36.4 %all-gather.1 = bf16[32,8,2]{1,2,0:T(2,128)(2,1)S(1)} all-gather(bf16[1,8,2]{1,2,0:T(2,128)(2,1)S(1)} %bitcast.349), channel_id=1, replica_groups=mesh['fsdp'=32] {'fsdp'}, dimensions={0}, use_global_device_ids=true | all-gather | bytes 1056 | tf_op jit(solution)/shard_map/all_gather | solution.py:214
  211.5 37.8 %all-gather.2 = bf16[32,8,2]{1,2,0:T(2,128)(2,1)S(1)} all-gather(bf16[1,8,2]{1,2,0:T(2,128)(2,1)S(1)} %bitcast.350), channel_id=1, replica_groups=mesh['fsdp'=32] {'fsdp'}, dimensions={0}, use_global_device_ids=true | all-gather | bytes 1056 | tf_op jit(solution)/shard_map/all_gather | solution.py:215
  249.5 36.4 %all-gather.3 = bf16[32,32,2]{1,2,0:T(2,128)(2,1)S(1)} all-gather(bf16[1,32,2]{1,2,0:T(2,128)(2,1)S(1)} %bitcast.351), channel_id=1, replica_groups=mesh['fsdp'=32] {'fsdp'}, dimensions={0}, use_global_device_ids=true | all-gather | bytes 4224 | tf_op jit(solution)/shard_map/all_gather | solution.py:216
  286.0 37.8 %all-gather.4 = bf16[32,32,2]{1,2,0:T(2,128)(2,1)S(1)} all-gather(bf16[1,32,2]{1,2,0:T(2,128)(2,1)S(1)} %bitcast.352), channel_id=1, replica_groups=mesh['fsdp'=32] {'fsdp'}, dimensions={0}, use_global_device_ids=true | all-gather | bytes 4224 | tf_op jit(solution)/shard_map/all_gather | solution.py:217
  324.0 41.1 %all_gather.37 = bf16[256,1024]{1,0:T(8,128)(2,1)} all-gather(bf16[8,1024]{1,0:T(8,128)(2,1)S(1)} %copy-done.64), channel_id=1, replica_groups=mesh['fsdp'=32] {'fsdp'}, dimensions={0}, use_global_device_ids=true | all-gather | bytes 540672 | tf_op jit(solution)/shard_map/all_gather | solution.py:211
  371.0 37.0 %psum.141 = f32[416]{0:T(512)S(1)} all-reduce(f32[416]{0:T(512)S(1)} %pad_maximum_fusion.19), channel_id=1, replica_groups=mesh['fsdp'=32] {'fsdp'}, use_global_device_ids=true, to_apply=%region_7.8 | all-reduce | flops 416 | bytes 3328 | tf_op jit(solution)/shard_map/psum | solution.py:130
  487.1 42.5 %psum.142 = f32[1312]{0:T(1024)S(1)} all-reduce(f32[1312]{0:T(1024)S(1)} %pad_maximum_fusion.16), channel_id=1, replica_groups=mesh['fsdp'=32] {'fsdp'}, use_global_device_ids=true, to_apply=%region_11.12 | all-reduce | flops 1312 | bytes 10496 | tf_op jit(solution)/shard_map/psum | solution.py:122
  538.6 38.8 %psum.143 = f32[1312]{0:T(1024)S(1)} all-reduce(f32[1312]{0:T(1024)S(1)} %pad_maximum_fusion.17), channel_id=1, replica_groups=mesh['fsdp'=32] {'fsdp'}, use_global_device_ids=true, to_apply=%region_15.16 | all-reduce | flops 1312 | bytes 10496 | tf_op jit(solution)/shard_map/psum | solution.py:130
  602.2 42.0 %psum.144 = f32[384]{0:T(512)S(1)} all-reduce(f32[384]{0:T(512)S(1)} %pad_maximum_fusion.20), channel_id=1, replica_groups=mesh['fsdp'=32] {'fsdp'}, use_global_device_ids=true, to_apply=%region_18.19 | all-reduce | flops 384 | bytes 3072 | tf_op jit(solution)/shard_map/psum | solution.py:122
  649.3 38.4 %psum.145 = f32[384]{0:T(512)S(1)} all-reduce(f32[384]{0:T(512)S(1)} %pad_maximum_fusion.21), channel_id=1, replica_groups=mesh['fsdp'=32] {'fsdp'}, use_global_device_ids=true, to_apply=%region_21.22 | all-reduce | flops 384 | bytes 3072 | tf_op jit(solution)/shard_map/psum | solution.py:130
  696.5 41.6 %psum.146 = f32[1024]{0:T(1024)S(1)} all-reduce(f32[1024]{0:T(1024)S(1)} %get-tuple-element.249), channel_id=1, replica_groups=mesh['fsdp'=32] {'fsdp'}, use_global_device_ids=true, to_apply=%region_23.24 | all-reduce | flops 1024 | bytes 8192 | tf_op jit(solution)/shard_map/psum | solution.py:122
  744.1 38.5 %psum.147 = f32[1024]{0:T(1024)S(1)} all-reduce(f32[1024]{0:T(1024)S(1)} %multiply_reduce_fusion.2), channel_id=1, replica_groups=mesh['fsdp'=32] {'fsdp'}, use_global_device_ids=true, to_apply=%region_25.26 | all-reduce | flops 1024 | bytes 8192 | tf_op jit(solution)/shard_map/psum | solution.py:130
  814.1 42.3 %all-reduce.36 = (f32[2304]{0:T(1024)S(1)}, f32[2304]{0:T(1024)S(1)}) all-reduce(f32[2304]{0:T(1024)S(1)} %pad_maximum_fusion.15, f32[2304]{0:T(1024)S(1)} %pad_maximum_fusion.14), channel_id=1, replica_groups=mesh['fsdp'=32] {'fsdp'}, use_global_device_ids=true, to_apply=%region_33.34 | all-reduce | flops 4608 | bytes 36864 | tf_op jit(solution)/shard_map/psum | solution.py:142
  900.5 38.7 %all-reduce.35 = (f32[288]{0:T(512)S(1)}, f32[288]{0:T(512)S(1)}) all-reduce(f32[288]{0:T(512)S(1)} %pad_maximum_fusion.23, f32[288]{0:T(512)S(1)} %pad_maximum_fusion.22), channel_id=1, replica_groups=mesh['fsdp'=32] {'fsdp'}, use_global_device_ids=true, to_apply=%region_39.40 | all-reduce | flops 576 | bytes 4608 | tf_op jit(solution)/shard_map/psum | solution.py:142
  1043.3 41.9 %all-reduce.34 = (f32[288]{0:T(512)S(1)}, f32[288]{0:T(512)S(1)}) all-reduce(f32[288]{0:T(512)S(1)} %pad_maximum_fusion.25, f32[288]{0:T(512)S(1)} %pad_maximum_fusion.24), channel_id=1, replica_groups=mesh['fsdp'=32] {'fsdp'}, use_global_device_ids=true, to_apply=%region_45.46 | all-reduce | flops 576 | bytes 4608 | tf_op jit(solution)/shard_map/psum | solution.py:142
  1147.0 28.1 %convolution_add_fusion = f32[16,14,14,1280]{3,0,2,1:T(8,128)} fusion(bf16[16,14,14,1024]{3,0,2,1:T(8,128)(2,1)} %get-tuple-element.139, f32[16,14,14,3840]{3,0,2,1:T(8,128)} %fusion.17, f32[15,14,14,1280]{3,0,2,1:T(8,128)} %slice_select_fusion, f32[15,14,14,1280]{3,0,2,1:T(8,128)} %slice_select_fusion.1, bf16[1280,1024]{1,0:T(8,128)(2,1)S(1)} %copy-done.137), kind=kOutput, calls=%fused_computation.1 | convolution fusion | flops 8232878080 | bytes 71262208 | tf_op jit(solution)/shard_map/fhwd,cd->fhwc/dot_general | solution.py:14
  1190.3 118.5 %all-reduce.41.cloned.1.call-done = (f32[256]{0:T(256)}, f32[256]{0:T(256)}, f32[384,32]{0,1:T(8,128)}, f32[288,32]{0,1:T(8,128)}, f32[32,128]{1,0:T(8,128)}) async-done(((f32[256]{0:T(256)}, f32[256]{0:T(256)}, f32[384,32]{0,1:T(8,128)}, f32[288,32]{0,1:T(8,128)}, f32[32,128]{1,0:T(8,128)}), (f32[256]{0:T(256)}, f32[256]{0:T(256)}, f32[384,32]{0,1:T(8,128)}, f32[288,32]{0,1:T(8,128)}, ...) | async-done | bytes 104464 | tf_op jit(solution)/shard_map/psum | solution.py:142
  1447.8 134.9 %reduce-scatter.9.cloned.1.call-done = f32[8,1024]{1,0:T(8,128)} async-done(((f32[256,1024]{1,0:T(8,128)}), f32[8,1024]{1,0:T(8,128)}) %reduce-scatter.9.cloned.1.call-update) | async-done | bytes 32784 | tf_op jit(solution)/shard_map/reduce_scatter | solution.py:336
  1582.7 100.9 %reduce-scatter.7.cloned.1.call-done = f32[72,256]{1,0:T(8,128)} async-done(((f32[2304,256]{1,0:T(8,128)}), f32[72,256]{1,0:T(8,128)}) %reduce-scatter.7.cloned.1.call-update) | async-done | bytes 73744 | tf_op jit(solution)/shard_map/reduce_scatter | solution.py:335
  1683.6 109.8 %reduce-scatter.5.cloned.1.call-done = f32[120,256]{1,0:T(8,128)} async-done(((f32[3840,256]{1,0:T(8,128)}), f32[120,256]{1,0:T(8,128)}) %reduce-scatter.5.cloned.1.call-update) | async-done | bytes 122896 | tf_op jit(solution)/shard_map/reduce_scatter | solution.py:334
  1793.4 144.8 %reduce-scatter.11.cloned.1.call-done = f32[40,1024]{1,0:T(8,128)} async-done(((f32[1280,1024]{1,0:T(8,128)}), f32[40,1024]{1,0:T(8,128)}) %reduce-scatter.11.cloned.1.call-update) | async-done | bytes 163856 | tf_op jit(solution)/shard_map/reduce_scatter | solution.py:337
  (534 shorter events, 580.4 us)
Async XLA Ops:
  7.2 452.7 %all-gather.9.cloned.1.call-start = ((), (), s32[]{:S(2)}) async-start(), calls=%async_computation.4 | async-start | bytes 2027520 | tf_op jit(solution)/shard_map/all_gather | solution.py:209
  8.0 463.6 %all-gather.11.cloned.1.call-start = ((), (), s32[]{:S(2)}) async-start(), calls=%async_computation.5 | async-start | bytes 2703360 | tf_op jit(solution)/shard_map/all_gather | solution.py:212
  8.7 582.5 %all-gather.13.cloned.1.call-start = ((), (), s32[]{:S(2)}) async-start(), calls=%async_computation.6 | async-start | bytes 1216512 | tf_op jit(solution)/shard_map/all_gather | solution.py:210
  9.4 1299.4 %all-reduce.41.cloned.1.call-start = ((), (), s32[]{:S(2)}) async-start(), calls=%async_computation.11 | async-start | bytes 233472 | tf_op jit(solution)/shard_map/psum | solution.py:142
  26.1 415.7 %copy-start.89 = (pred[16]{0:T(512)(128)(4,1)}, pred[16]{0:T(512)(128)(4,1)S(1)}, u32[]{:S(2)}) copy-start(pred[16]{0:T(512)(128)(4,1)S(1)} %get-tuple-element.232) | copy-start | bytes 52
  82.9 340.4 %copy-start.2 = (f32[16,14,14,256]{3,0,2,1:T(8,128)}, f32[16,14,14,256]{3,0,2,1:T(8,128)S(1)}, u32[]{:S(2)}) copy-start(f32[16,14,14,256]{3,0,2,1:T(8,128)S(1)} %get-tuple-element.238) | copy-start | bytes 9633796
  134.4 279.6 %copy-start.76 = (f32[32]{0:T(128)}, f32[32]{0:T(128)S(1)}, u32[]{:S(2)}) copy-start(f32[32]{0:T(128)S(1)} %slice_multiply_fusion.11) | copy-start | bytes 388
  134.5 288.8 %copy-start.58 = (f32[256]{0:T(256)}, f32[256]{0:T(256)S(1)}, u32[]{:S(2)}) copy-start(f32[256]{0:T(256)S(1)} %slice_multiply_fusion.6) | copy-start | bytes 3076
  134.5 279.4 %copy-start.92 = (f32[32]{0:T(128)}, f32[32]{0:T(128)S(1)}, u32[]{:S(2)}) copy-start(f32[32]{0:T(128)S(1)} %get-tuple-element.227) | copy-start | bytes 388
  134.5 279.4 %copy-start.94 = (f32[32]{0:T(128)}, f32[32]{0:T(128)S(1)}, u32[]{:S(2)}) copy-start(f32[32]{0:T(128)S(1)} %get-tuple-element.228) | copy-start | bytes 388
  211.4 368.1 %copy-start.70 = (f32[1,256]{1,0:T(1,128)}, f32[1,256]{1,0:T(1,128)S(1)}, u32[]{:S(2)}) copy-start(f32[1,256]{1,0:T(1,128)S(1)} %get-tuple-element.211) | copy-start | bytes 3076
  211.5 368.1 %copy-start.72 = (f32[1,256]{1,0:T(1,128)}, f32[1,256]{1,0:T(1,128)S(1)}, u32[]{:S(2)}) copy-start(f32[1,256]{1,0:T(1,128)S(1)} %get-tuple-element.212) | copy-start | bytes 3076
  249.4 642.3 %copy-start.120 = (f32[1,256]{1,0:T(1,128)}, f32[1,256]{1,0:T(1,128)S(1)}, u32[]{:S(2)}) copy-start(f32[1,256]{1,0:T(1,128)S(1)} %get-tuple-element.209) | copy-start | bytes 3076
  249.5 642.3 %copy-start.122 = (f32[1,256]{1,0:T(1,128)}, f32[1,256]{1,0:T(1,128)S(1)}, u32[]{:S(2)}) copy-start(f32[1,256]{1,0:T(1,128)S(1)} %get-tuple-element.210) | copy-start | bytes 3076
  644.2 319.9 %copy-start.87 = (f32[256]{0:T(256)}, f32[256]{0:T(256)S(1)}, u32[]{:S(2)}) copy-start(f32[256]{0:T(256)S(1)} %slice_multiply_fusion.5) | copy-start | bytes 3076
  687.8 276.3 %copy-start.107 = (f32[256]{0:T(256)}, f32[256]{0:T(256)S(1)}, u32[]{:S(2)}) copy-start(f32[256]{0:T(256)S(1)} %get-tuple-element.206) | copy-start | bytes 3076
  1185.5 259.4 %all-reduce.43.cloned.1.call-start = ((), (), s32[]{:S(2)}) async-start(), calls=%async_computation.12 | async-start | bytes 1441792
  1316.8 266.0 %reduce-scatter.9.cloned.1.call-start = ((), (), s32[]{:S(2)}) async-start(), calls=%async_computation.9 | async-start | bytes 1081344 | tf_op jit(solution)/shard_map/reduce_scatter | solution.py:336
  1322.8 360.8 %reduce-scatter.7.cloned.1.call-start = ((), (), s32[]{:S(2)}) async-start(), calls=%async_computation.8 | async-start | bytes 2433024 | tf_op jit(solution)/shard_map/reduce_scatter | solution.py:335
  1334.3 459.2 %reduce-scatter.5.cloned.1.call-start = ((), (), s32[]{:S(2)}) async-start(), calls=%async_computation.7 | async-start | bytes 4055040 | tf_op jit(solution)/shard_map/reduce_scatter | solution.py:334
  1349.1 589.2 %reduce-scatter.11.cloned.1.call-start = ((), (), s32[]{:S(2)}) async-start(), calls=%async_computation.10 | async-start | bytes 5406720 | tf_op jit(solution)/shard_map/reduce_scatter | solution.py:337
  1424.0 514.2 %copy-start.55 = (f32[384,32]{0,1:T(8,128)S(1)}, f32[384,32]{0,1:T(8,128)}, u32[]{:S(2)}) copy-start(f32[384,32]{0,1:T(8,128)} %get-tuple-element.273) | copy-start | bytes 147460
  1424.0 514.9 %copy-start.54 = (f32[288,32]{0,1:T(8,128)S(1)}, f32[288,32]{0,1:T(8,128)}, u32[]{:S(2)}) copy-start(f32[288,32]{0,1:T(8,128)} %get-tuple-element.274) | copy-start | bytes 110596
  1424.0 515.5 %copy-start.65 = (f32[32,128]{1,0:T(8,128)S(1)}, f32[32,128]{1,0:T(8,128)}, u32[]{:S(2)}) copy-start(f32[32,128]{1,0:T(8,128)} %get-tuple-element.275) | copy-start | bytes 49156
  (140 other events, 3240.3 us)
Sparse Core Ops, SparseCore 0:
  11.0 59.1 all-gather.8
  73.0 57.2 all-gather.10
  133.2 52.9 all-gather.12
  1185.6 123.1 all-reduce.40
  1316.9 128.0 all-reduce.42
  1447.7 134.9 reduce-scatter.8
  1588.6 94.9 reduce-scatter.6
  1690.4 102.9 reduce-scatter.4
  1796.4 141.7 reduce-scatter.10
where the time goes:
time: 1950 us
  blocking collectives  713 us (37%)
  waiting for transfers between devices  625 us (32%)
  matrix products  249 us (13%)
  other arithmetic  193 us (10%)
  local copies, waits for them, and re-layouts  150 us (8%)
    psum x4, blocking collectives, gather_stats(): totals = lax.psum(local_sums, 'fsdp')  164 us
    psum x4, blocking collectives, gather_stats(): spreads = lax.psum(local_spread, 'fsdp')  153 us
    reduce_scatter x1, waiting for transfers between devices, shards(): lax.psum_scatter(proj_term, 'fsdp', scatter_dimension=0, tiled=True)  145 us
    reduce_scatter x1, waiting for transfers between devices, shards(): lax.psum_scatter(last_term, 'fsdp', scatter_dimension=0, tiled=True)  135 us
    psum x3, blocking collectives, reduce_norms(): sum_all, cross_all = lax.psum((firsts, seconds), 'fsdp')  123 us
    psum x1, waiting for transfers between devices, reduce_norms(): sum_all, cross_all = lax.psum((firsts, seconds), 'fsdp')  118 us
    reduce_scatter x1, waiting for transfers between devices, shards(): lax.psum_scatter(first_term, 'fsdp', scatter_dimension=0, tiled=True)  110 us
    dot_general x9, matrix products, back_product(): jnp.einsum('fhwd,cd->fhwc', gradient, weight, preferred_element_type=jnp....  108 us
  transfers between devices with their start and end apart: 9, of which 6 were waited for; matrix products, arithmetic and copies ran while one was open for 13% of the time, Pallas kernels for 0%

commit v1 on v0

--- a/solution.py
+++ b/solution.py
@@ -1,9 +1,239 @@
+import functools
+
 import jax
 import jax.numpy as jnp
 from jax import lax
+from jax.experimental import pallas as pl
+from jax.experimental.pallas import tpu as pltpu
 from jax.sharding import PartitionSpec as P
 
 EPSILON = 1e-05
+
+MESH = pl.DeviceIdType.MESH
+
+def exch_kernel(n, inner, count, centred, x_ref, o_ref, near, far, mid, near_send, near_recv, far_send, far_recv):
+    me = lax.axis_index("fsdp")
+    outer = n // inner
+    mi = lax.rem(me, inner)
+    mo = lax.div(me, inner)
+    barrier = pltpu.get_barrier_semaphore()
+    for k in range(1, inner):
+        pl.semaphore_signal(barrier, inc=1, device_id=(mo * inner + lax.rem(mi + k, inner),), device_id_type=MESH)
+    for k in range(1, outer):
+        pl.semaphore_signal(barrier, inc=1, device_id=(lax.rem(mo + k, outer) * inner + mi,), device_id_type=MESH)
+    pl.semaphore_wait(barrier, inner - 1 + outer - 1)
+
+    def swap(src, slots, sends, recvs, mine, size, peer):
+        copies = []
+        for k in range(1, size):
+            c = pltpu.make_async_remote_copy(src_ref=src, dst_ref=slots.at[mine], send_sem=sends.at[k], recv_sem=recvs.at[k],
+                device_id=(peer(k),), device_id_type=MESH)
+            c.start()
+            copies.append(c)
+        slots[mine] = src[...]
+        for c in copies:
+            c.wait()
+
+    def merge(slots, size, weight):
+        if not centred:
+            t = slots[0]
+            for k in range(1, size):
+                t = t + slots[k]
+            return t
+        m = slots[0, 0:1]
+        for k in range(1, size):
+            m = m + slots[k, 0:1]
+        m = m * (1.0 / size)
+        s = None
+        for k in range(size):
+            d = slots[k, 0:1] - m
+            v = slots[k, 1:2] + d * d * weight
+            s = v if s is None else s + v
+        return jnp.concatenate([m, s], axis=0)
+
+    swap(x_ref, near, near_send, near_recv, mi, inner, lambda k: mo * inner + lax.rem(mi + k, inner))
+    mid[...] = merge(near, inner, float(count))
+    if outer > 1:
+        swap(mid, far, far_send, far_recv, mo, outer, lambda k: lax.rem(mo + k, outer) * inner + mi)
+        o_ref[...] = merge(far, outer, float(count * inner))
+    else:
+        o_ref[...] = mid[...]
+
+def exchange(x, n, inner, cid, count=1.0, centred=False):
+    outer = n // inner
+    return pl.pallas_call(
+        functools.partial(exch_kernel, n, inner, count, centred),
+        out_shape=jax.ShapeDtypeStruct(x.shape, x.dtype),
+        in_specs=[pl.BlockSpec(memory_space=pltpu.VMEM)],
+        out_specs=pl.BlockSpec(memory_space=pltpu.VMEM),
+        scratch_shapes=[pltpu.VMEM((inner,) + x.shape, x.dtype), pltpu.VMEM((outer,) + x.shape, x.dtype), pltpu.VMEM(x.shape, x.dtype),
+            pltpu.SemaphoreType.DMA((inner,)), pltpu.SemaphoreType.DMA((inner,)),
+            pltpu.SemaphoreType.DMA((outer,)), pltpu.SemaphoreType.DMA((outer,))],
+        compiler_params=pltpu.CompilerParams(collective_id=cid, has_side_effects=True),
+    )(x)
+
+def places(n):
+    me = lax.axis_index("fsdp")
+    z = lax.div(me, 8)
+    y = lax.rem(lax.div(me, 4), 2)
+    x = lax.rem(lax.div(me, 2), 2)
+    c = lax.rem(me, 2)
+    return z, y, x, c
+
+def flat(z, y, x, c):
+    return ((z * 2 + y) * 2 + x) * 2 + c
+
+def meet(n):
+    z, y, x, c = places(n)
+    depth = n // 8
+    barrier = pltpu.get_barrier_semaphore()
+    peers = [flat(lax.rem(z + k, depth), y, x, c) for k in range(1, depth)]
+    peers += [flat(z, y, x, 1 - c), flat(z, y, 1 - x, c), flat(z, 1 - y, x, c)]
+    for peer in peers:
+        pl.semaphore_signal(barrier, inc=1, device_id=(peer,), device_id_type=MESH)
+    pl.semaphore_wait(barrier, len(peers))
+
+def gather_kernel(n, turns, *refs):
+    k = len(turns)
+    ins, outs = refs[:k], refs[k:2 * k]
+    own_sem, z_send, z_recv, p_send, p_recv, c_send, c_recv = refs[2 * k:]
+    depth = n // 8
+    z, y, x, c = places(n)
+    meet(n)
+    def start(src, dst, ss, rs, dev):
+        d = pltpu.make_async_remote_copy(src_ref=src, dst_ref=dst, send_sem=ss, recv_sem=rs, device_id=(dev,), device_id_type=MESH)
+        d.start()
+        return d
+    core = flat(z, y, x, 1 - c)
+    tail = []
+    zc, own = [], []
+    for i in range(k):
+        o = pltpu.make_async_copy(ins[i], outs[i].at[z, y, x, c], own_sem.at[i])
+        o.start()
+        own.append(o)
+        zc.append([start(ins[i], outs[i].at[z, y, x, c], z_send.at[i, s], z_recv.at[i, s], flat(lax.rem(z + s, depth), y, x, c)) for s in range(1, depth)])
+    pc = []
+    for i in range(k):
+        own[i].wait()
+        for d in zc[i]:
+            d.wait()
+        dev = flat(z, y, 1 - x, c) if turns[i] == 0 else flat(z, 1 - y, x, c)
+        part = outs[i].at[:, y, x, c]
+        pc.append(start(part, part, p_send.at[i, 0], p_recv.at[i, 0], dev))
+        tail.append(start(part, part, c_send.at[i, 0], c_recv.at[i, 0], core))
+    qc = []
+    for i in range(k):
+        pc[i].wait()
+        if turns[i] == 0:
+            part, new, dev = outs[i].at[:, y, :, c], outs[i].at[:, y, 1 - x, c], flat(z, 1 - y, x, c)
+        else:
+            part, new, dev = outs[i].at[:, :, x, c], outs[i].at[:, 1 - y, x, c], flat(z, y, 1 - x, c)
+        qc.append(start(part, part, p_send.at[i, 1], p_recv.at[i, 1], dev))
+        tail.append(start(new, new, c_send.at[i, 1], c_recv.at[i, 1], core))
+    for i in range(k):
+        qc[i].wait()
+        new = outs[i].at[:, 1 - y, :, c] if turns[i] == 0 else outs[i].at[:, :, 1 - x, c]
+        tail.append(start(new, new, c_send.at[i, 2], c_recv.at[i, 2], core))
+    for d in tail:
+        d.wait()
+
+def gather_all(arrays, turns, n, cid):
+    k = len(arrays)
+    depth = n // 8
+    DS = pltpu.SemaphoreType.DMA
+    outs = pl.pallas_call(
+        functools.partial(gather_kernel, n, turns),
+        out_shape=[jax.ShapeDtypeStruct((depth, 2, 2, 2) + a.shape, a.dtype) for a in arrays],
+        in_specs=[pl.BlockSpec(memory_space=pl.ANY)] * k,
+        out_specs=[pl.BlockSpec(memory_space=pl.ANY)] * k,
+        scratch_shapes=[DS((k,)), DS((k, depth)), DS((k, depth)), DS((k, 2)), DS((k, 2)), DS((k, 3)), DS((k, 3))],
+        compiler_params=pltpu.CompilerParams(collective_id=cid, has_side_effects=True),
+    )(*arrays)
+    return [o.reshape((n,) + a.shape) for o, a in zip(outs, arrays)]
+
+def scatter_kernel(n, turns, *refs):
+    k = len(turns)
+    ins, outs = refs[:k], refs[k:2 * k]
+    rest = refs[2 * k:]
+    half, r1, r2, r3, r4 = (rest[j * k:(j + 1) * k] for j in range(5))
+    own_sem, c_sem, p_sem, q_sem, z_send, z_recv = rest[5 * k:]
+    depth = n // 8
+    z, y, x, c = places(n)
+    meet(n)
+    def start(src, dst, ss, rs, dev):
+        d = pltpu.make_async_remote_copy(src_ref=src, dst_ref=dst, send_sem=ss, recv_sem=rs, device_id=(dev,), device_id_type=MESH)
+        d.start()
+        return d
+    def add(target, other):
+        target[...] = (target[...].astype(jnp.float32) + other[...].astype(jnp.float32)).astype(target.dtype)
+    def pairs(i):
+        if turns[i] == 0:
+            return (lambda zz, o: half[i].at[zz, o, x]), (lambda zz: half[i].at[zz, y, x])
+        return (lambda zz, o: half[i].at[zz, y, o]), (lambda zz: half[i].at[zz, y, x])
+    own, cc, pc, qc, zc = [], [], [], [], []
+    for i in range(k):
+        o = pltpu.make_async_copy(ins[i].at[:, :, :, c], half[i], own_sem.at[i])
+        o.start()
+        own.append(o)
+        cc.append(start(ins[i].at[:, :, :, 1 - c], r1[i], c_sem.at[i, 0], c_sem.at[i, 1], flat(z, y, x, 1 - c)))
+    for i in range(k):
+        own[i].wait()
+        cc[i].wait()
+        @pl.loop(0, depth)
+        def _(zz):
+            for a in range(2):
+                for b in range(2):
+                    add(half[i].at[zz, a, b], r1[i].at[zz, a, b])
+        if turns[i] == 0:
+            src, dev = half[i].at[:, :, 1 - x], flat(z, y, 1 - x, c)
+        else:
+            src, dev = half[i].at[:, 1 - y], flat(z, 1 - y, x, c)
+        pc.append(start(src, r2[i], p_sem.at[i, 0], p_sem.at[i, 1], dev))
+    for i in range(k):
+        pc[i].wait()
+        view, last = pairs(i)
+        @pl.loop(0, depth)
+        def _(zz):
+            for o in range(2):
+                add(view(zz, o), r2[i].at[zz, o])
+        if turns[i] == 0:
+            src, dev = half[i].at[:, 1 - y, x], flat(z, 1 - y, x, c)
+        else:
+            src, dev = half[i].at[:, y, 1 - x], flat(z, y, 1 - x, c)
+        qc.append(start(src, r3[i], q_sem.at[i, 0], q_sem.at[i, 1], dev))
+    for i in range(k):
+        qc[i].wait()
+        view, last = pairs(i)
+        @pl.loop(0, depth)
+        def _(zz):
+            add(last(zz), r3[i].at[zz])
+        for s in range(1, depth):
+            zz = lax.rem(z + s, depth)
+            zc.append((i, s, start(last(zz), r4[i].at[s], z_send.at[i, s], z_recv.at[i, s], flat(zz, y, x, c))))
+    for i in range(k):
+        view, last = pairs(i)
+        outs[i][...] = last(z)[...].astype(jnp.float32)
+        for j, s, d in zc:
+            if j == i:
+                d.wait()
+                outs[i][...] += r4[i][s].astype(jnp.float32)
+
+def scatter_all(arrays, turns, n, cid):
+    k = len(arrays)
+    depth = n // 8
+    DS = pltpu.SemaphoreType.DMA
+    six = [a.reshape((depth, 2, 2, 2) + a.shape[1:]) for a in arrays]
+    def buf(lead):
+        return [pltpu.VMEM(lead + a.shape[1:], a.dtype) for a in arrays]
+    return pl.pallas_call(
+        functools.partial(scatter_kernel, n, turns),
+        out_shape=[jax.ShapeDtypeStruct(a.shape[1:], jnp.float32) for a in arrays],
+        in_specs=[pl.BlockSpec(memory_space=pl.ANY)] * k,
+        out_specs=[pl.BlockSpec(memory_space=pltpu.VMEM)] * k,
+        scratch_shapes=buf((depth, 2, 2)) + buf((depth, 2, 2)) + buf((depth, 2)) + buf((depth,)) + buf((depth,))
+        + [DS((k,)), DS((k, 2)), DS((k, 2)), DS((k, 2)), DS((k, depth)), DS((k, depth))],
+        compiler_params=pltpu.CompilerParams(collective_id=cid, has_side_effects=True, vmem_limit_bytes=60 * 1024 * 1024),
+    )(*six)
 
 
 def product(operand, weight):
@@ -105,47 +335,39 @@
     return grouped.reshape((grouped.shape[0] * 4,) + grouped.shape[2:])
 
 
-def split_channels(joined_sums, widths, counts):
-    pieces = []
-    offset = 0
-    for width, count in zip(widths, counts):
-        pieces.append(joined_sums[offset : offset + width] / count)
-        offset += width
-    return pieces
-
-
-def gather_stats(fields):
+def widen(row):
+    short = -row.shape[-1] % 128
+    return jnp.pad(row, ((0, 0), (0, short)))
+
+
+def gather_stats(fields, call):
     devices = lax.axis_size("fsdp")
     widths = [field.shape[-1] for field in fields]
-    counts = [field.shape[0] * field.shape[1] * field.shape[2] * devices for field in fields]
-    local_sums = jnp.concatenate([jnp.sum(field, axis=(0, 1, 2)) for field in fields])
-    totals = lax.psum(local_sums, "fsdp")
-    averages = split_channels(totals, widths, counts)
-    local_spread = jnp.concatenate(
-        [
-            jnp.sum(jnp.square(field - average), axis=(0, 1, 2))
-            for field, average in zip(fields, averages)
-        ]
-    )
-    spreads = lax.psum(local_spread, "fsdp")
-    variances = split_channels(spreads, widths, counts)
-    return [
-        (average, lax.rsqrt(variance + EPSILON)) for average, variance in zip(averages, variances)
+    rows = []
+    for field in fields:
+        own = jnp.mean(field, axis=(0, 1, 2))
+        rows.append(widen(jnp.stack([own, jnp.mean(jnp.square(field - own), axis=(0, 1, 2))])))
+    merged = exchange(jnp.concatenate(rows, axis=1), devices, 8, call, 1.0, True) / jnp.array([[1.0], [devices]])
+    result, offset = [], 0
+    for width, row in zip(widths, rows):
+        part = merged[:, offset : offset + width]
+        result.append((part[0], lax.rsqrt(part[1] + EPSILON)))
+        offset += row.shape[1]
+    return result
+
+
+def reduce_norms(pairs, call):
+    devices = lax.axis_size("fsdp")
+    rows = [
+        widen(jnp.stack([jnp.sum(grad_out, axis=(0, 1, 2)), jnp.sum(grad_out * normed, axis=(0, 1, 2))]))
+        for grad_out, normed in pairs
     ]
-
-
-def reduce_norms(pairs):
-    firsts = jnp.concatenate([jnp.sum(grad_out, axis=(0, 1, 2)) for grad_out, normed in pairs])
-    seconds = jnp.concatenate(
-        [jnp.sum(grad_out * normed, axis=(0, 1, 2)) for grad_out, normed in pairs]
-    )
-    sum_all, cross_all = lax.psum((firsts, seconds), "fsdp")
-    result = []
-    offset = 0
-    for grad_out, normed in pairs:
+    merged = exchange(jnp.concatenate(rows, axis=1), devices, 8, call)
+    result, offset = [], 0
+    for (grad_out, normed), row in zip(pairs, rows):
         width = grad_out.shape[-1]
-        result.append((sum_all[offset : offset + width], cross_all[offset : offset + width]))
-        offset += width
+        result.append((merged[0, offset : offset + width], merged[1, offset : offset + width]))
+        offset += row.shape[1]
     return result
 
 
@@ -204,33 +426,25 @@
     slow_cot,
     fast_cot,
 ):
-    gathered = (
-        lax.all_gather(lateral_weight, "fsdp", axis=1, tiled=True),
-        lax.all_gather(first_weight, "fsdp", axis=0, tiled=True),
-        lax.all_gather(middle_weight, "fsdp", axis=0, tiled=True),
-        lax.all_gather(last_weight, "fsdp", axis=0, tiled=True),
-        lax.all_gather(proj_weight, "fsdp", axis=0, tiled=True),
-        lax.all_gather(lat_norm, "fsdp", axis=1, tiled=True),
-        lax.all_gather(one_norm, "fsdp", axis=1, tiled=True),
-        lax.all_gather(two_norm, "fsdp", axis=1, tiled=True),
-        lax.all_gather(out_norm, "fsdp", axis=1, tiled=True),
-        lax.all_gather(proj_norm, "fsdp", axis=1, tiled=True),
-    )
-    (
-        lateral_full,
-        first_full,
-        middle_full,
-        last_full,
-        proj_full,
-        gain_lat,
-        gain_one,
-        gain_two,
-        gain_out,
-        gain_proj,
-    ) = gathered
+    devices = lax.axis_size("fsdp")
+    norms = jnp.concatenate([lat_norm, one_norm, two_norm, out_norm, proj_norm], axis=1).astype(jnp.float32)
+    norms = jnp.pad(norms, ((0, 6), (0, 128 - norms.shape[1])))
+    lateral_full, first_full, middle_full, last_full, proj_full, norms_full = gather_all(
+        [lateral_weight.T, first_weight, middle_weight, last_weight, proj_weight, norms], (0, 1, 1, 0, 0, 0), devices, 1
+    )
+    lateral_full = lateral_full.reshape(-1, lateral_weight.shape[0]).T
+    first_full = first_full.reshape(-1, first_weight.shape[1])
+    middle_full = middle_full.reshape(-1, middle_weight.shape[1])
+    last_full = last_full.reshape(-1, last_weight.shape[1])
+    proj_full = proj_full.reshape(-1, proj_weight.shape[1])
+    gains, offset = [], 0
+    for pair in (lat_norm, one_norm, two_norm, out_norm, proj_norm):
+        width = pair.shape[1]
+        gains.append(norms_full[:, :2, offset : offset + width].transpose(1, 0, 2).reshape(2, -1))
+        offset += width
+    gain_lat, gain_one, gain_two, gain_out, gain_proj = gains
     has_prev, has_next = clip_edges(clip_ids)
     fast_prev, fast_next = fast_edges(has_prev, has_next)
-    devices = lax.axis_size("fsdp")
     slow_count = slow_in.shape[0] * slow_in.shape[1] * slow_in.shape[2] * devices
     fast_count = 4 * slow_count
     lat_cols = lateral_cols(fast_in, has_prev)
@@ -238,7 +452,7 @@
     fone_cols = temporal_cols(fast_in, fast_prev, fast_next)
     fone_pre = product(fone_cols, fast_first)
     fproj_pre = product(fast_in, fast_proj)
-    lat_stats, fone_stats, fproj_stats = gather_stats([lat_pre, fone_pre, fproj_pre])
+    lat_stats, fone_stats, fproj_stats = gather_stats([lat_pre, fone_pre, fproj_pre], 2)
     lat_hat = normalize(lat_pre, lat_stats)
     lat_act = affine(lat_hat, gain_lat)
     lateral = jax.nn.silu(lat_act).astype(jnp.bfloat16)
@@ -252,7 +466,7 @@
     proj_pre = product(joined, proj_full)
     ftwo_cols = spatial_cols(fone)
     ftwo_pre = product(ftwo_cols, fast_middle)
-    one_stats, proj_stats, ftwo_stats = gather_stats([one_pre, proj_pre, ftwo_pre])
+    one_stats, proj_stats, ftwo_stats = gather_stats([one_pre, proj_pre, ftwo_pre], 3)
     one_hat = normalize(one_pre, one_stats)
     one_act = affine(one_hat, gain_one)
     one = jax.nn.silu(one_act).astype(jnp.bfloat16)
@@ -263,13 +477,13 @@
     two_cols = spatial_cols(one)
     two_pre = product(two_cols, middle_full)
     fthree_pre = product(ftwo, fast_last)
-    two_stats, fthree_stats = gather_stats([two_pre, fthree_pre])
+    two_stats, fthree_stats = gather_stats([two_pre, fthree_pre], 4)
     two_hat = normalize(two_pre, two_stats)
     two_act = affine(two_hat, gain_two)
     two = jax.nn.silu(two_act).astype(jnp.bfloat16)
     fthree_hat = normalize(fthree_pre, fthree_stats)
     three_pre = product(two, last_full)
-    three_stats = gather_stats([three_pre])[0]
+    three_stats = gather_stats([three_pre], 5)[0]
     three_hat = normalize(three_pre, three_stats)
     slow_sum = affine(three_hat, gain_out) + affine(proj_hat, gain_proj)
     slow_out = jax.nn.silu(slow_sum).astype(jnp.bfloat16)
@@ -283,7 +497,8 @@
             (slow_delta, proj_hat),
             (fast_delta, fthree_hat),
             (fast_delta, fproj_hat),
-        ]
+        ],
+        6,
     )
     three_d = norm_input_grad(slow_delta, three_hat, gain_out, three_stats[1], outer[0], slow_count)
     proj_d = norm_input_grad(slow_delta, proj_hat, gain_proj, proj_stats[1], outer[1], slow_count)
@@ -299,7 +514,7 @@
     fproj_term = weight_term(fast_in, fproj_d)
     two_delta = back_product(three_d, last_full) * silu_slope(two_act)
     ftwo_delta = back_product(fthree_d, fast_last) * silu_slope(ftwo_act)
-    middle_sums = reduce_norms([(two_delta, two_hat), (ftwo_delta, ftwo_hat)])
+    middle_sums = reduce_norms([(two_delta, two_hat), (ftwo_delta, ftwo_hat)], 7)
     two_d = norm_input_grad(two_delta, two_hat, gain_two, two_stats[1], middle_sums[0], slow_count)
     ftwo_d = norm_input_grad(
         ftwo_delta, ftwo_hat, fast_mid_norm[1], ftwo_stats[1], middle_sums[1], fast_count
@@ -308,7 +523,7 @@
     fmiddle_term = weight_term(ftwo_cols, ftwo_d)
     one_delta = spatial_back(back_product(two_d, middle_full)) * silu_slope(one_act)
     fone_delta = spatial_back(back_product(ftwo_d, fast_middle)) * silu_slope(fone_act)
-    inner_sums = reduce_norms([(one_delta, one_hat), (fone_delta, fone_hat)])
+    inner_sums = reduce_norms([(one_delta, one_hat), (fone_delta, fone_hat)], 8)
     one_d = norm_input_grad(one_delta, one_hat, gain_one, one_stats[1], inner_sums[0], slow_count)
     fone_d = norm_input_grad(
         fone_delta, fone_hat, fast_mid_norm[0], fone_stats[1], inner_sums[1], fast_count
@@ -321,7 +536,7 @@
     width_in = slow_in.shape[-1]
     slow_in_grad = joined_grad[..., :width_in].astype(jnp.bfloat16)
     lat_delta = joined_grad[..., width_in:] * silu_slope(lat_act)
-    lat_sums = reduce_norms([(lat_delta, lat_hat)])
+    lat_sums = reduce_norms([(lat_delta, lat_hat)], 9)
     lat_d = norm_input_grad(lat_delta, lat_hat, gain_lat, lat_stats[1], lat_sums[0], slow_count)
     lateral_term = weight_term(lat_cols, lat_d)
     fast_in_grad = (
@@ -329,15 +544,27 @@
         + temporal_back(back_product(fone_d, fast_first), fast_prev, fast_next)
         + back_product(fproj_d, fast_proj)
     ).astype(jnp.bfloat16)
-    shares = (
-        lax.psum_scatter(lateral_term, "fsdp", scatter_dimension=1, tiled=True),
-        lax.psum_scatter(first_term, "fsdp", scatter_dimension=0, tiled=True),
-        lax.psum_scatter(middle_term, "fsdp", scatter_dimension=0, tiled=True),
-        lax.psum_scatter(last_term, "fsdp", scatter_dimension=0, tiled=True),
-        lax.psum_scatter(proj_term, "fsdp", scatter_dimension=0, tiled=True),
+    shares = scatter_all(
+        [
+            lateral_term.T.astype(jnp.bfloat16).reshape(devices, -1, lateral_weight.shape[0]),
+            first_term.astype(jnp.bfloat16).reshape(devices, -1, first_weight.shape[1]),
+            middle_term.astype(jnp.bfloat16).reshape(devices, -1, middle_weight.shape[1]),
+            last_term.astype(jnp.bfloat16).reshape(devices, -1, last_weight.shape[1]),
+            proj_term.astype(jnp.bfloat16).reshape(devices, -1, proj_weight.shape[1]),
+        ],
+        (0, 1, 1, 0, 0),
+        devices,
+        10,
     )
     lateral_grad, first_grad, middle_grad, last_grad, proj_grad = shares
-    fast_shares = lax.psum((ffirst_term, fmiddle_term, fthree_term, fproj_term), "fsdp")
+    lateral_grad = lateral_grad.T
+    terms = (ffirst_term, fmiddle_term, fthree_term, fproj_term)
+    fast_total = exchange(jnp.concatenate([term.reshape(-1, 128) for term in terms]), devices, 8, 11)
+    fast_shares, offset = [], 0
+    for term in terms:
+        rows = term.size // 128
+        fast_shares.append(fast_total[offset : offset + rows].reshape(term.shape))
+        offset += rows
     lat_norm_grad = own_columns(pair_grad(lat_sums[0]))
     one_norm_grad = own_columns(pair_grad(inner_sums[0]))
     two_norm_grad = own_columns(pair_grad(middle_sums[0]))

time: 1950 us -> 792 us (0.41)
  blocking collectives: 713 us -> 0 us
  waiting for transfers between devices: 625 us -> 0 us
  Pallas kernels: 0 us -> 220 us
  matrix products: 249 us -> 209 us
    reduce_scatter x4 -> x0, waiting for transfers between devices: 490 us -> none  [the longest x1 145 us: shards(): lax.psum_scatter(proj_term, 'fsdp', scatter_dimension=0, tiled=True)]
    psum x11 -> x0, blocking collectives: 439 us -> none  [the longest x4 164 us: gather_stats(): totals = lax.psum(local_sums, 'fsdp')]
    all_gather x7 -> x0, blocking collectives: 274 us -> none  [the longest x1 44.6 us: shards(): lax.all_gather(lateral_weight, 'fsdp', axis=1, tiled=True)]
    pallas_call x0 -> x11, Pallas kernels: none -> 220 us  [the longest x9 118 us: exchange(): pl.pallas_call(functools.partial(exch_kernel, n, inner, count, centred),...]
    psum x1 -> x0, waiting for transfers between devices: 118 us -> none  [reduce_norms(): sum_all, cross_all = lax.psum((firsts, seconds), 'fsdp')]
    reduce_sum x5 -> x3, other arithmetic: 47.9 us -> 17.8 us  [reduce_norms(): jnp.sum(grad_out, axis=(0, 1, 2))]
    dot_general x9, matrix products: 74.3 us -> 47.8 us  [product(): jnp.einsum('fhwc,cd->fhwd', operand, weight, preferred_element_type=jnp.f...]
    reduce_sum x9 -> x11, other arithmetic: 25.9 us -> 40.9 us  [the longest x2 32 us: reduce_norms(): jnp.sum(grad_out * normed, axis=(0, 1, 2))]
  transfers between devices with their start and end apart: 9 -> 0, of which waited for: 6 -> 0; matrix products, arithmetic and copies ran while one was open for 13% -> 0% of each run, Pallas kernels for 0% -> 0%
where the time goes in v1:
time: 792 us; the launch traced here: 785 us
  Pallas kernels  220 us (28%)
  matrix products  209 us (26%)
  other arithmetic  202 us (26%)
  local copies, waits for them, and re-layouts  151 us (19%)
    pallas_call x9, Pallas kernels, exchange(): pl.pallas_call(functools.partial(exch_kernel, n, inner, count, centred),...  118 us
    dot_general x9, matrix products, back_product(): jnp.einsum('fhwd,cd->fhwc', gradient, weight, preferred_element_type=jnp....  99.7 us
    dot_general x9, matrix products, weight_term(): jnp.einsum('fhwc,fhwd->cd', columns, gradient, preferred_element_type=jnp...  61.7 us
    pallas_call x1, Pallas kernels, gather_all(): pl.pallas_call(functools.partial(gather_kernel, n, turns), out_shape=[jax...  52.9 us
    select_n x8, other arithmetic, masked(): jnp.where(keep_mask[:, None, None, None], field, jnp.zeros_like(field))  50.7 us
    pallas_call x1, Pallas kernels, scatter_all(): pl.pallas_call(functools.partial(scatter_kernel, n, turns), out_shape=[ja...  49.9 us
    dot_general x9, matrix products, product(): jnp.einsum('fhwc,cd->fhwd', operand, weight, preferred_element_type=jnp.f...  47.8 us
    unnamed x260, local copies, waits for them, and re-layouts  39.8 us

profile of v1, /device:TPU:0, one launch (start us, length us, event | category | flops | bytes accessed | tf_op | source)
XLA Modules:
  0.0 785.0 jit_solution(17379272466423668865)
XLA Ops:
  40.5 52.9 %shard_map.392 = (bf16[4,2,2,2,8,640]{5,4,3,2,1,0:T(8,128)(2,1)}, bf16[4,2,2,2,120,256]{5,4,3,2,1,0:T(8,128)(2,1)}, bf16[4,2,2,2,72,256]{5,4,3,2,1,0:T(8,128)(2,...) custom-call(bf16[8,640]{1,0:T(8,128)(2,1)} %bitcast.397, ...), custom_call_target="tpu_custom_call" | custom-call | tf_op jit(solution)/shard_map/pallas_call | solution.py:144
  102.0 11.1 %shard_map.393 = f32[2,512]{1,0:T(2,128)} custom-call(f32[2,512]{1,0:T(2,128)} %maximum_maximum_fusion.1.x_ref), custom_call_target="tpu_custom_call" | custom-call | tf_op jit(solution)/shard_map/pallas_call | solution.py:64
  119.3 11.6 %fusion.115 = (f32[1024]{0:T(1024)S(1)}, f32[16,14,14,1024]{3,0,2,1:T(8,128)S(1)}) fusion(bf16[1280,1024,1,1]{1,0,3,2:T(8,128)(2,1)S(1)} %bitcast.434, bf16[16,14,14,256]{3,0,2,1:T(8,128)(2,1)S(1)} %multiply_convert_fusion.15, bf16[16,14,14,1024]{3,0,2,1:T(8,128)(2,1)} %param.25), kind=kOutput, calls=%fused_computation.362 | convolution fusion | flops 8240102400 | bytes 23498752 | tf_op jit(solution)/shard_map/fhwc,cd->fhwd/dot_general | solution.py:240
  176.7 12.2 %fusion.116 = (f32[256]{0:T(256)S(1)}, f32[16,14,14,256]{3,0,2,1:T(8,128)S(1)}) fusion(bf16[3840,256,1,1]{1,0,3,2:T(8,128)(2,1)S(1)} %bitcast.347, bf16[16,14,14,1280]{3,0,2,1:T(8,128)(2,1)} %pad_select_fusion, bf16[16,14,14,256]{3,0,2,1:T(8,128)(2,1)S(1)} %copy-done.42, bf16[16,14,14,1024]{3,0,2,1:T(8,128)(2,1)} %param.25, ...), kind=kOutput, calls=%fused_computation.363 | convolution fusion | flops 6262767616 | bytes 29262848 | tf_op jit(solution)/shard_map/fhwc,cd->fhwd/dot_general | solution.py:240
  190.4 10.5 %shard_map.394 = f32[2,1408]{1,0:T(2,128)} custom-call(f32[2,1408]{1,0:T(2,128)} %pad_maximum_fusion.15.x_ref), custom_call_target="tpu_custom_call" | custom-call | tf_op jit(solution)/shard_map/pallas_call | solution.py:64
  230.6 11.2 %multiply_reduce_fusion.5 = (f32[128]{0:T(128)S(1)}, f32[128]{0:T(128)S(1)}, f32[128]{0:T(128)S(1)}, f32[64,14,14,128]{3,0,2,1:T(8,128)}, bf16[64,14,14,128]{3,0,2,1:T(8,128)(2,1)}) fusion(f32[64,14,14,128]{3,0,2,1:T(8,128)} %copy-done.9, f32[128]{0:T(128)S(1)} %get-tuple-element.206, f32[128]{0:T(128)S(1)} %get-tuple-element.205, ...), kind=kLoop, calls=%fused_computation.38 | loop fusion | flops 40140416 | bytes 25695744 | tf_op jit(solution)/shard_map/reduce_sum | solution.py:362
  260.3 20.8 %multiply_reduce_fusion.1 = (f32[1024]{0:T(1024)S(1)}, f32[1024]{0:T(1024)S(1)}, f32[1024]{0:T(1024)S(1)}, f32[16,14,14,1024]{3,0,2,1:T(8,128)}, bf16[16,14,14,1024]{3,0,2,1:T(8,128)(2,1)}) fusion(f32[16,14,14,1024]{3,0,2,1:T(8,128)} %copy-done.5, f32[1024]{0:T(1024)S(1)} %bitcast.363, f32[1024]{0:T(1024)S(1)} %bitcast.367, f32[1024]{0:T(1024)S(1)} %bitcast.360, ...), kind=kLoop, calls=%fused_computation.10 | loop fusion | flops 80278528 | bytes 51425280 | tf_op jit(solution)/shard_map/reduce_sum | solution.py:362
  281.7 11.0 %shard_map.397 = f32[2,2304]{1,0:T(2,128)} custom-call(f32[2,2304]{1,0:T(2,128)} %maximum_maximum_fusion.x_ref), custom_call_target="tpu_custom_call" | custom-call | tf_op jit(solution)/shard_map/pallas_call | solution.py:64
  306.1 14.9 %multiply_convert_fusion.1 = (bf16[16,14,14,1024]{3,0,2,1:T(8,128)(2,1)}, bf16[16,14,14,1024]{3,0,2,1:T(8,128)(2,1)}) fusion(f32[16,14,14,1024]{3,0,2,1:T(8,128)} %get-tuple-element.105, f32[16,14,14,1024]{3,0,2,1:T(8,128)} %copy-done.5, f32[1024]{0:T(1024)S(1)} %bitcast.386, f32[1024]{0:T(1024)S(1)} %bitcast.385, f32[1024]{0:T(1024)S(1)} %mul.549, ...), kind=kLoop, calls=%fused_computation.8 | loop fusion | flops 44957696 | bytes 51421184 | tf_op jit(solution)/shard_map/convert_element_type | solution.py:392
  331.6 10.8 %bitcast_convert_fusion = bf16[1280,1024]{1,0:T(8,128)(2,1)} fusion(bf16[16,14,14,1024]{3,0,2,1:T(8,128)(2,1)S(1)} %bitcast.340, bf16[16,14,14,256]{3,0,2,1:T(8,128)(2,1)S(1)} %copy-done.43, bf16[16,14,14,1024]{3,0,2,1:T(8,128)(2,1)S(1)} %bitcast.344), kind=kOutput, calls=%fused_computation.48 | convolution fusion | flops 8238202880 | bytes 17072128 | tf_op jit(solution)/shard_map/fhwc,fhwd->cd/dot_general | solution.py:248
  384.5 11.5 %fusion.120 = f32[16,14,14,2304]{3,0,2,1:T(8,128)} fusion(bf16[16,14,14,256]{3,0,2,1:T(8,128)(2,1)S(1)} %multiply_convert_fusion.10, bf16[2304,256,1,1]{1,0,3,2:T(8,128)(2,1)S(1)} %bitcast.353), kind=kOutput, calls=%fused_computation.367 | convolution fusion | flops 3699376128 | bytes 31686656 | tf_op jit(solution)/shard_map/fhwd,cd->fhwc/dot_general | solution.py:244
  396.0 19.6 %fusion.90 = (f32[16,14,14,256]{3,0,2,1:T(8,128)S(1)}, f32[16,14,14,256]{3,0,2,1:T(8,128)}, f32[16,14,14,256]{3,0,2,1:T(8,128)}, f32[16,14,14,256]{3,0,2,1:T(8,1...) fusion(f32[16,14,14,2304]{3,0,2,1:T(8,128)} %fusion.120), kind=kLoop, calls=%fused_computation.337 | loop fusion | bytes 57802752 | tf_op jit(solution)/shard_map/slice | solution.py:308
  428.6 11.5 %fusion.45 = f32[64,14,14,288]{0,3,2,1:T(8,128)} fusion(bf16[64,14,14,32]{0,3,2,1:T(8,128)(2,1)S(1)} %copy-done.26, bf16[288,32]{0,1:T(8,128)(2,1)S(1)} %copy-done.57), kind=kOutput, calls=%fused_computation.184 | convolution fusion | flops 231211008 | bytes 15271936 | tf_op jit(solution)/shard_map/fhwd,cd->fhwc/dot_general | solution.py:244
  440.1 19.8 %fusion.89 = (f32[64,14,14,32]{0,3,2,1:T(8,128)S(1)}, f32[64,14,14,32]{0,3,2,1:T(8,128)}, f32[64,14,14,32]{0,3,2,1:T(8,128)}, f32[64,14,14,32]{0,3,2,1:T(8,128)}...) fusion(f32[64,14,14,288]{0,3,2,1:T(8,128)} %fusion.45), kind=kLoop, calls=%fused_computation.336 | loop fusion | bytes 28901376 | tf_op jit(solution)/shard_map/slice | solution.py:308
  497.8 31.4 %shard_map.402 = f32[328,128]{1,0:T(8,128)} custom-call(f32[328,128]{1,0:T(8,128)} %pad_maximum_fusion.14.x_ref), custom_call_target="tpu_custom_call" | custom-call | tf_op jit(solution)/shard_map/pallas_call | solution.py:64
  536.5 13.3 %fusion.7 = bf16[3840,256]{1,0:T(8,128)(2,1)} fusion(bf16[16,14,14,256]{3,0,2,1:T(8,128)(2,1)S(1)} %multiply_convert_fusion.8, bf16[16,14,14,1280]{3,0,2,1:T(8,128)(2,1)} %pad_select_fusion, bf16[16,14,14,256]{3,0,2,1:T(8,128)(2,1)S(1)} %copy-done.44, bf16[16,14,14,1024]{3,0,2,1:T(8,128)(2,1)} %param.25, bf16[16,14,14,1280]{3,0,2,1:T(8,128)(2,1)} %pad_select_fusion.1), kind=kOutput, calls=%fused_computation.49 | convolution fusion | flops 6262947840 | bytes 27656192 | tf_op jit(solution)/shard_map/fhwc,fhwd->cd/dot_general | solution.py:248
  552.8 11.3 %fusion.42 = f32[64,14,14,384]{3,0,2,1:T(8,128)} fusion(bf16[384,32]{0,1:T(8,128)(2,1)S(1)} %copy-done.69, f32[64,14,14,32]{0,3,2,1:T(8,128)} %get-tuple-element.104, f32[64,14,14,32]{0,3,2,1:T(8,128)S(1)} %copy-done.14, f32[32]{0:T(128)} %copy-done.97, f32[32]{0:T(128)} %copy-done.96, f32[32]{0:T(128)} %get-tuple-element.215, f32[32]{0:T(128)} %copy-done.78, ...), kind=kOutput, calls=%fused_computation.181 | convolution fusion | flops 311091200 | bytes 22504064 | tf_op jit(solution)/shard_map/fhwd,cd->fhwc/dot_general | solution.py:244
  564.0 12.3 %fusion.91 = (f32[64,14,14,128]{3,0,2,1:T(8,128)}, f32[64,14,14,128]{3,0,2,1:T(8,128)}) fusion(f32[64,14,14,384]{3,0,2,1:T(8,128)} %fusion.42), kind=kLoop, calls=%fused_computation.338 | loop fusion | bytes 25690112 | tf_op jit(solution)/shard_map/slice | solution.py:286
  587.0 20.1 %fusion.121 = f32[16,14,14,3840]{3,0,2,1:T(8,128)} fusion(bf16[16,14,14,256]{3,0,2,1:T(8,128)(2,1)S(1)} %copy-done.38, bf16[3840,256,1,1]{1,0,3,2:T(8,128)(2,1)} %bitcast.346), kind=kOutput, calls=%fused_computation.368 | convolution fusion | flops 6165626880 | bytes 51740672 | tf_op jit(solution)/shard_map/fhwd,cd->fhwc/dot_general | solution.py:244
  607.1 17.3 %fusion.88 = (f32[16,14,14,1280]{3,0,2,1:T(8,128)}, f32[16,14,14,1280]{3,0,2,1:T(8,128)S(1)}) fusion(f32[16,14,14,3840]{3,0,2,1:T(8,128)} %fusion.121), kind=kLoop, calls=%fused_computation.335 | loop fusion | bytes 64225280 | tf_op jit(solution)/shard_map/slice | solution.py:286
  624.4 11.8 %slice_select_fusion.1 = f32[15,14,14,1280]{3,0,2,1:T(8,128)} fusion(f32[16,14,14,1280]{3,0,2,1:T(8,128)} %get-tuple-element.107, pred[15]{0:T(512)(128)(4,1)S(1)} %copy-done.98), kind=kLoop, calls=%fused_computation.3 | loop fusion | flops 3763200 | bytes 30105616 | tf_op jit(solution)/shard_map/jit(_where)/select_n | solution.py:267
  642.2 27.2 %convolution_add_fusion = f32[16,14,14,1280]{3,0,2,1:T(8,128)} fusion(bf16[16,14,14,1024]{3,0,2,1:T(8,128)(2,1)} %get-tuple-element.132, bf16[1280,1024,1,1]{1,0,3,2:T(8,128)(2,1)S(1)} %bitcast.435, f32[16,14,14,3840]{3,0,2,1:T(8,128)} %fusion.121, f32[15,14,14,1280]{3,0,2,1:T(8,128)} %slice_select_fusion, f32[15,14,14,1280]{3,0,2,1:T(8,128)} %slice_select_fusion.1), kind=kOutput, calls=%fused_computation.1 | convolution fusion | flops 8232878080 | bytes 71262208 | tf_op jit(solution)/shard_map/fhwd,cd->fhwc/dot_general | solution.py:244
  682.7 12.9 %shard_map.400 = f32[2,256]{1,0:T(2,128)} custom-call(f32[2,256]{1,0:T(2,128)} %pad_maximum_fusion.19.x_ref), custom_call_target="tpu_custom_call" | custom-call | tf_op jit(solution)/shard_map/pallas_call | solution.py:64
  704.8 49.9 %shard_map.401 = (f32[8,640]{1,0:T(8,128)}, f32[120,256]{1,0:T(8,128)}, f32[72,256]{1,0:T(8,128)}, f32[8,1024]{1,0:T(8,128)}, f32[40,1024]{1,0:T(8,128)}) custom-call(bf16[4,2,2,2,8,640]{5,4,3,2,1,0:T(8,128)(2,1)} %bitcast.351, bf16[4,2,2,2,120,256]{5,4,3,2,1,0:T(8,128)(2,1)} %bitcast.348, bf16[4,2,2,2,72,256]{5,4,3,2,1,0:T(8,128)(2,1)} %bitcast.354, ...), custom_call_target="tpu_custom_call" | custom-call | tf_op jit(solution)/shard_map/pallas_call | solution.py:228
  (448 shorter events, 345.6 us)
Async XLA Ops:
  0.7 35.4 %copy-start = (bf16[128,128]{1,0:T(8,128)(2,1)S(1)}, bf16[128,128]{1,0:T(8,128)(2,1)}, u32[]{:S(2)}) copy-start(bf16[128,128]{1,0:T(8,128)(2,1)} %param.41) | copy-start | bytes 98308
  2.4 165.7 %copy-start.83 = (pred[16]{0:T(512)(128)(4,1)}, pred[16]{0:T(512)(128)(4,1)S(1)}, u32[]{:S(2)}) copy-start(pred[16]{0:T(512)(128)(4,1)S(1)} %get-tuple-element.240) | copy-start | bytes 52
  3.2 21.4 %copy-start.91 = (pred[64]{0:T(512)(128)(4,1)}, pred[64]{0:T(512)(128)(4,1)S(1)}, u32[]{:S(2)}) copy-start(pred[64]{0:T(512)(128)(4,1)S(1)} %or.50) | copy-start | bytes 196
  4.7 132.7 %copy-start.86 = (f32[32]{0:T(128)}, f32[32]{0:T(128)S(1)}, u32[]{:S(2)}) copy-start(f32[32]{0:T(128)S(1)} %get-tuple-element.263) | copy-start | bytes 388
  4.7 132.7 %copy-start.88 = (f32[32]{0:T(128)}, f32[32]{0:T(128)S(1)}, u32[]{:S(2)}) copy-start(f32[32]{0:T(128)S(1)} %get-tuple-element.264) | copy-start | bytes 388
  96.5 21.0 %copy-start.70 = (f32[256]{0:T(256)}, f32[256]{0:T(256)S(1)}, u32[]{:S(2)}) copy-start(f32[256]{0:T(256)S(1)} %mul.495) | copy-start | bytes 3076
  96.6 21.0 %copy-start.81 = (f32[256]{0:T(256)}, f32[256]{0:T(256)S(1)}, u32[]{:S(2)}) copy-start(f32[256]{0:T(256)S(1)} %add.404) | copy-start | bytes 3076
  96.7 113.7 %copy-start.62 = (f32[256]{0:T(256)}, f32[256]{0:T(256)S(1)}, u32[]{:S(2)}) copy-start(f32[256]{0:T(256)S(1)} %mul.507) | copy-start | bytes 3076
  96.8 113.6 %copy-start.72 = (f32[256]{0:T(256)}, f32[256]{0:T(256)S(1)}, u32[]{:S(2)}) copy-start(f32[256]{0:T(256)S(1)} %add.414) | copy-start | bytes 3076
  113.9 23.5 %copy-start.76 = (f32[32]{0:T(128)}, f32[32]{0:T(128)S(1)}, u32[]{:S(2)}) copy-start(f32[32]{0:T(128)S(1)} %get-tuple-element.187) | copy-start | bytes 388
  113.9 23.6 %copy-start.78 = (f32[32]{0:T(128)}, f32[32]{0:T(128)S(1)}, u32[]{:S(2)}) copy-start(f32[32]{0:T(128)S(1)} %get-tuple-element.188) | copy-start | bytes 388
  188.8 21.6 %copy-start.15 = (f32[16,14,14,256]{3,0,2,1:T(8,128)}, f32[16,14,14,256]{3,0,2,1:T(8,128)S(1)}, u32[]{:S(2)}) copy-start(f32[16,14,14,256]{3,0,2,1:T(8,128)S(1)} %get-tuple-element.252) | copy-start | bytes 9633796
  218.2 108.7 %copy-start.35 = (f32[16,14,14,256]{3,0,2,1:T(8,128)}, f32[16,14,14,256]{3,0,2,1:T(8,128)S(1)}, u32[]{:S(2)}) copy-start(f32[16,14,14,256]{3,0,2,1:T(8,128)S(1)} %get-tuple-element.256) | copy-start | bytes 9633796
  302.0 19.0 %copy-start.20 = (bf16[64,14,14,128]{3,0,2,1:T(8,128)(2,1)}, bf16[64,14,14,128]{3,0,2,1:T(8,128)(2,1)S(1)}, u32[]{:S(2)}) copy-start(bf16[64,14,14,128]{3,0,2,1:T(8,128)(2,1)S(1)} %get-tuple-element.139) | copy-start | bytes 9633796
  466.6 19.6 %copy-start.3 = (bf16[64,14,14,128]{3,0,2,1:T(8,128)(2,1)S(1)}, bf16[64,14,14,128]{3,0,2,1:T(8,128)(2,1)}, u32[]{:S(2)}) copy-start(bf16[64,14,14,128]{3,0,2,1:T(8,128)(2,1)} %param.26) | copy-start | bytes 9633796
  607.1 17.3 %copy-start.98 = (pred[15]{0:T(512)(128)(4,1)S(1)}, pred[15]{0:T(512)(128)(4,1)}, u32[]{:S(2)}) copy-start(pred[15]{0:T(512)(128)(4,1)} %slice.686) | copy-start | bytes 49
  642.1 27.2 %copy-start.7 = (f32[16,14,14,256]{3,0,2,1:T(8,128)S(1)}, f32[16,14,14,256]{3,0,2,1:T(8,128)}, u32[]{:S(2)}) copy-start(f32[16,14,14,256]{3,0,2,1:T(8,128)} %copy-done.6) | copy-start | bytes 9633796
  642.1 27.2 %copy-start.65 = (f32[1,256]{1,0:T(1,128)S(1)}, f32[1,256]{1,0:T(1,128)}, u32[]{:S(2)}) copy-start(f32[1,256]{1,0:T(1,128)} %copy-done.64) | copy-start | bytes 3076
  642.1 27.2 %copy-start.71 = (f32[256]{0:T(256)S(1)}, f32[256]{0:T(256)}, u32[]{:S(2)}) copy-start(f32[256]{0:T(256)} %copy-done.70) | copy-start | bytes 3076
  642.1 27.2 %copy-start.75 = (f32[1,256]{1,0:T(1,128)S(1)}, f32[1,256]{1,0:T(1,128)}, u32[]{:S(2)}) copy-start(f32[1,256]{1,0:T(1,128)} %copy-done.74) | copy-start | bytes 3076
  642.1 27.2 %copy-start.82 = (f32[256]{0:T(256)S(1)}, f32[256]{0:T(256)}, u32[]{:S(2)}) copy-start(f32[256]{0:T(256)} %copy-done.81) | copy-start | bytes 3076
  673.7 23.3 %copy-start.95 = (f32[256]{0:T(256)S(1)}, f32[256]{0:T(256)}, u32[]{:S(2)}) copy-start(f32[256]{0:T(256)} %mul.601) | copy-start | bytes 3076
  704.8 49.9 %copy-start.24 = (bf16[16,14,14,256]{3,0,2,1:T(8,128)(2,1)S(1)}, bf16[16,14,14,256]{3,0,2,1:T(8,128)(2,1)}, u32[]{:S(2)}) copy-start(bf16[16,14,14,256]{3,0,2,1:T(8,128)(2,1)} %copy-done.23) | copy-start | bytes 4816900
  704.8 49.9 %copy-start.48 = (bf16[4,2,2,2,8,640]{5,4,3,2,1,0:T(8,128)(2,1)S(1)}, bf16[4,2,2,2,8,640]{5,4,3,2,1,0:T(8,128)(2,1)}, u32[]{:S(2)}) copy-start(bf16[4,2,2,2,8,640]{5,4,3,2,1,0:T(8,128)(2,1)} %get-tuple-element.31) | copy-start | bytes 983044
  (96 other events, 717.2 us)

commit v2 on v0

v2 whole, which is shorter than its diff:
```python
import functools

import jax
import jax.numpy as jnp
import numpy as np
from jax import lax
from jax.experimental import pallas as pl
from jax.experimental.pallas import tpu as pltpu
from jax.sharding import PartitionSpec as P

EPSILON = 1e-05


MESH = pl.DeviceIdType.MESH


f32 = jnp.float32
bf16 = jnp.bfloat16
STEPS = 7
STRIP = 32


def dot(a, b):
    return lax.dot_general(a, b, (((1,), (0,)), ((), ())), preferred_element_type=f32)


def dot_nt(a, b):
    return lax.dot_general(a, b, (((1,), (1,)), ((), ())), preferred_element_type=f32)


def dot_tn(a, b):
    return lax.dot_general(a, b, (((0,), (0,)), ((), ())), preferred_element_type=f32)


def shift(v, mask, by):
    rows = v.shape[0]
    moved = pltpu.roll(v, by % rows, 0)
    return masked(moved, mask)


def masked(v, mask):
    return (v.reshape(-1, mask.shape[0], v.shape[1]) * mask[None, :, : v.shape[1]]).reshape(v.shape)


def sigma(x):
    return 0.5 + 0.5 * jnp.tanh(0.5 * x)


def silu(x):
    return x * sigma(x)


def slope(x):
    s = sigma(x)
    return s * (1.0 + x * (1.0 - s))


def normed(z, n):
    return (z - n[0:1]) * n[1:2]


def scaled(hat, n):
    return hat * n[2:3] + n[3:4]


def acted(z, n):
    return scaled(normed(z, n), n)


def input_grad(e, hat, n, s_mean, s_cross):
    return ((n[2:3] * n[1:2]) * (e - s_mean - hat * s_cross)).astype(bf16)


def eighth(v):
    return jnp.sum(v.reshape(-1, 8, v.shape[1]), axis=0)


def clear_first(step, *refs):
    @pl.when(step == 0)
    def _():
        for ref in refs:
            ref[...] = jnp.zeros(ref.shape, ref.dtype)


def add_moments(step, acc, lo, z):
    hi = lo + z.shape[1]
    high = z.shape[0] // 8
    deep = z.reshape(high, 8, hi - lo)
    own = jnp.sum(deep, axis=0) * (1.0 / high)
    off = deep - own[None]
    spread_of = jnp.sum(off * off, axis=0)
    past = step.astype(f32)
    share = 1.0 / (past + 1.0)
    gap = own - acc[0, :, lo:hi]
    acc[0, :, lo:hi] += gap * share
    acc[1, :, lo:hi] += spread_of + gap * gap * (past * share * high)


def add_sums(step, acc, lo, parts):
    hi = lo + parts[0].shape[1]
    for k, part in enumerate(parts):
        acc[k, :, lo:hi] += part


def split_fours(raw, wide):
    rows = wide.shape[0]
    wide[...] = raw[...].astype(f32).reshape(rows, 128)
    return jnp.concatenate([wide[pl.ds(k, rows // 4, stride=4), :] for k in range(4)], axis=1)


def join_fours(value, wide, raw):
    rows = wide.shape[0]
    for k in range(4):
        wide[pl.ds(k, rows // 4, stride=4), :] = value[:, 128 * k : 128 * (k + 1)]
    raw[...] = wide[...].astype(bf16).reshape(raw.shape)


def clear(grid):
    grid[...] = jnp.zeros(grid.shape, grid.dtype)


def fill(grid, side, value, block):
    per = side // STEPS
    line = value.shape[0] // per
    frames = line // side
    for r in range(per):
        at = ((block * per + r + 1) * (side + 2) + 1) * frames
        grid[pl.ds(pl.multiple_of(at, 16), line), :] = value[r * line : (r + 1) * line]


def tap_columns(grid, side, step, rows, flip):
    per = side // STEPS
    line = rows // per
    frames = line // side
    lines = []
    for r in range(per):
        pieces = []
        for a in range(3):
            for b in range(3):
                ra, rb = (2 - a, 2 - b) if flip else (a, b)
                at = ((step * per + r + ra) * (side + 2) + rb) * frames
                pieces.append(grid[pl.ds(pl.multiple_of(at, 16), line), :])
        lines.append(jnp.concatenate(pieces, axis=1))
    return jnp.concatenate(lines, axis=0)


INNER = 8


def greet(n):
    me = lax.axis_index("fsdp")
    mi, mo, depth = lax.rem(me, INNER), lax.div(me, INNER), n // INNER
    barrier = pltpu.get_barrier_semaphore()
    for k in range(1, INNER):
        pl.semaphore_signal(barrier, inc=1, device_id=(mo * INNER + lax.rem(mi + k, INNER),), device_id_type=MESH)
    for k in range(1, depth):
        pl.semaphore_signal(barrier, inc=1, device_id=(lax.rem(mo + k, depth) * INNER + mi,), device_id_type=MESH)


def greeted(n):
    pl.semaphore_wait(pltpu.get_barrier_semaphore(), INNER - 1 + n // INNER - 1)


def total_of(n, centred, own, near, far, mid, near_send, near_recv, far_send, far_recv):
    me = lax.axis_index("fsdp")
    mi, mo, depth = lax.rem(me, INNER), lax.div(me, INNER), n // INNER

    def swap(src, slots, sends, recvs, mine, size, peer):
        copies = []
        for k in range(1, size):
            copy = pltpu.make_async_remote_copy(
                src_ref=src, dst_ref=slots.at[mine], send_sem=sends.at[k], recv_sem=recvs.at[k],
                device_id=(peer(k),), device_id_type=MESH)
            copy.start()
            copies.append(copy)
        slots[mine] = src[...]
        for copy in copies:
            copy.wait()

    def merge(slots, size):
        if not centred:
            return sum(slots[k] for k in range(1, size)) + slots[0]
        mean = sum(slots[k, 0:1] for k in range(size)) * (1.0 / size)
        off = [slots[k, 0:1] - mean for k in range(size)]
        return jnp.concatenate([mean, sum(slots[k, 1:2] + off[k] * off[k] for k in range(size)) * (1.0 / size)], axis=0)

    swap(own, near, near_send, near_recv, mi, INNER, lambda k: mo * INNER + lax.rem(mi + k, INNER))
    mid[...] = merge(near, INNER)
    if depth == 1:
        return mid[...]
    swap(mid, far, far_send, far_recv, mo, depth, lambda k: lax.rem(mo + k, depth) * INNER + mi)
    return merge(far, depth)


def over_groups(part, width):
    lanes = part.shape[1]
    if width < 128:
        wide = jnp.broadcast_to(part, (8, lanes))
        total = wide
        for k in range(1, lanes // width):
            total = total + pltpu.roll(wide, k * width, 1)
        return total[0:1]
    total = sum(part[:, k : k + width] for k in range(0, lanes, width))
    return jnp.concatenate([total] * (lanes // width), axis=1)


def norm_pack(total, pairs, out, folds):
    out[0:2] = total
    for lo, hi, width in folds:
        groups = width / (hi - lo)
        mean = over_groups(total[0:1, lo:hi], width) * groups
        off = total[0:1, lo:hi] - mean
        out[0:1, lo:hi] = mean
        out[1:2, lo:hi] = over_groups(total[1:2, lo:hi] + off * off, width) * groups
    out[1:2] = lax.rsqrt(out[1:2] + EPSILON)
    at = 0
    for pair, lo, hi in pairs:
        out[2:4, at : at + hi - lo] = pair[:, lo:hi]
        at += hi - lo


def sum_pack(total, out, folds):
    out[...] = total
    for lo, hi, width in folds:
        for k in range(out.shape[0]):
            out[k : k + 1, lo:hi] = over_groups(total[k : k + 1, lo:hi], width)


def swap_scratch(shape, n):
    DS, depth = pltpu.SemaphoreType.DMA, n // INNER
    return [pltpu.VMEM((INNER,) + shape, f32), pltpu.VMEM((depth,) + shape, f32), pltpu.VMEM(shape, f32),
        DS((INNER,)), DS((INNER,)), DS((depth,)), DS((depth,))]


def run(body, rows, ins, outs, scratch, n=1, swap=None, call=None, same=None):
    def spec(shape, how):
        if how == "any":
            return pl.BlockSpec(memory_space=pl.ANY)
        if how == "rows":
            return pl.BlockSpec((shape[0] // STEPS,) + tuple(shape[1:]), lambda i, d=len(shape): (i,) + (0,) * (d - 1))
        return pl.BlockSpec(tuple(shape), lambda i, d=len(shape): (0,) * d, pipeline_mode=pl.Buffered(1))
    def out_spec(shape, how):
        if how in ("rows", "any"):
            return spec(shape, how)
        return pl.BlockSpec(tuple(shape), lambda i, d=len(shape): (0,) * d)
    extra = {}
    if swap is not None:
        scratch = scratch + [pltpu.VMEM(swap, f32)]
    if n > 1 and swap is not None:
        scratch = scratch + swap_scratch(swap, n)
    if n > 1 and call is not None:
        extra = dict(collective_id=call, has_side_effects=True)
    return pl.pallas_call(
        body,
        grid=(STEPS,),
        in_specs=[spec(a.shape, how) for a, how in ins],
        out_specs=[out_spec(shape, how) for shape, _, how in outs],
        out_shape=[jax.ShapeDtypeStruct(shape, kind) for shape, kind, _ in outs],
        scratch_shapes=scratch,
        input_output_aliases=same or {},
        compiler_params=pltpu.CompilerParams(dimension_semantics=("arbitrary",), vmem_limit_bytes=58 * 1024 * 1024, **extra),
    )(*[a for a, _ in ins])


def close_moments(step, acc, pairs, out, count, folds, n, ticks, own, *links):
    @pl.when(step == STEPS - 1)
    def _():
        mean = jnp.mean(acc[0], axis=0, keepdims=True)
        off = acc[0] - mean
        own[0:1] = mean
        own[1:2] = jnp.sum(acc[1], axis=0, keepdims=True) * (1.0 / count) + jnp.mean(off * off, axis=0, keepdims=True)
        if n > 1:
            ticks[3]()
            norm_pack(total_of(n, True, own, *links), pairs, out, folds)
            ticks[4]()
        else:
            norm_pack(own[...], pairs, out, folds)


def close_sums(step, acc, out, folds, n, ticks, own, *links):
    if n > 1 and not ticks:
        @pl.when(step == 0)
        def _():
            greet(n)

    @pl.when(step == STEPS - 1)
    def _():
        for k in range(acc.shape[0]):
            own[k : k + 1] = jnp.sum(acc[k], axis=0, keepdims=True)
        if n > 1:
            if ticks:
                ticks[3]()
            else:
                greeted(n)
            sum_pack(total_of(n, False, own, *links), out, folds)
            if ticks:
                ticks[4]()
        else:
            sum_pack(own[...], out, folds)


def places():
    me = lax.axis_index("fsdp")
    return lax.div(me, 8), lax.rem(lax.div(me, 4), 2), lax.rem(lax.div(me, 2), 2), lax.rem(me, 2)


def flat(z, y, x, c):
    return ((z * 2 + y) * 2 + x) * 2 + c


def six(term, n):
    return term.reshape((n // 8, 2, 2, 2, term.shape[0] // n) + term.shape[1:])


def halves(width):
    if width < 256:
        return ((0, width),)
    middle = width // 256 * 128
    return ((0, middle), (middle, width))


def scatter_scratch(parts, n):
    depth, k, DS = n // 8, len(parts), pltpu.SemaphoreType.DMA
    def buf(lead):
        return [pltpu.VMEM(lead + part, bf16) for part in parts]
    return (buf((depth, 2, 2)) + buf((depth, 2, 2)) + buf((depth, 2)) + buf((depth,)) + buf((depth,))
        + [DS((k,)), DS((k, 2)), DS((k, 2, 2)), DS((k, 2, 2)), DS((k, depth)), DS((k, depth))])


def scatter_ticks(n, ins, outs, rest):
    k, depth = len(ins), n // 8
    half, r1, r2, r3, r4 = (rest[j * k : (j + 1) * k] for j in range(5))
    own_sem, c_sem, p_sem, q_sem, z_send, z_recv = rest[5 * k :]
    z, y, x, c = places()
    core, over_x, over_y = flat(z, y, x, 1 - c), flat(z, y, 1 - x, c), flat(z, 1 - y, x, c)
    line = [flat(lax.rem(z + s, depth), y, x, c) for s in range(depth)]
    spots = [lax.rem(z + s, depth) for s in range(depth)]

    def remote(src, dst, send, recv, peer):
        return pltpu.make_async_remote_copy(
            src_ref=src, dst_ref=dst, send_sem=send, recv_sem=recv, device_id=(peer,), device_id_type=MESH)
    def sides(i):
        return tuple(enumerate(halves(half[i].shape[-1])))
    def own(i):
        return pltpu.make_async_copy(ins[i].at[:, :, :, c], half[i], own_sem.at[i])
    def to_core(i):
        return remote(ins[i].at[:, :, :, 1 - c], r1[i], c_sem.at[i, 0], c_sem.at[i, 1], core)
    def to_first(i, t, lo, hi):
        src, peer = (half[i].at[:, :, 1 - x, :, lo:hi], over_x) if t == 0 else (half[i].at[:, 1 - y, :, :, lo:hi], over_y)
        return remote(src, r2[i].at[:, :, :, lo:hi], p_sem.at[i, t, 0], p_sem.at[i, t, 1], peer)
    def to_second(i, t, lo, hi):
        src, peer = (half[i].at[:, 1 - y, x, :, lo:hi], over_y) if t == 0 else (half[i].at[:, y, 1 - x, :, lo:hi], over_x)
        return remote(src, r3[i].at[:, :, lo:hi], q_sem.at[i, t, 0], q_sem.at[i, t, 1], peer)
    def to_line(i, s):
        return remote(half[i].at[spots[s], y, x], r4[i].at[s], z_send.at[i, s], z_recv.at[i, s], line[s])
    def add(target, other):
        target[...] = (target[...].astype(f32) + other[...].astype(f32)).astype(target.dtype)

    def begin():
        for i in range(k):
            own(i).start()
            to_core(i).start()
    def first():
        for i in range(k):
            own(i).wait()
            to_core(i).wait()
            @pl.loop(0, depth)
            def _(zz, i=i):
                for a in range(2):
                    for b in range(2):
                        add(half[i].at[zz, a, b], r1[i].at[zz, a, b])
            for t, (lo, hi) in sides(i):
                to_first(i, t, lo, hi).start()
    def second():
        for i in range(k):
            for t, (lo, hi) in sides(i):
                to_first(i, t, lo, hi).wait()
                @pl.loop(0, depth)
                def _(zz, i=i, t=t, lo=lo, hi=hi):
                    for o in range(2):
                        target = half[i].at[zz, o, x] if t == 0 else half[i].at[zz, y, o]
                        add(target.at[:, lo:hi], r2[i].at[zz, o, :, lo:hi])
                to_second(i, t, lo, hi).start()
    def third():
        for i in range(k):
            for t, (lo, hi) in sides(i):
                to_second(i, t, lo, hi).wait()
            @pl.loop(0, depth)
            def _(zz, i=i):
                add(half[i].at[zz, y, x], r3[i].at[zz])
            for s in range(1, depth):
                to_line(i, s).start()
    def finish():
        for i in range(k):
            outs[i][...] = half[i][z, y, x].astype(f32)
            for s in range(1, depth):
                to_line(i, s).wait()
                outs[i][...] += r4[i][s].astype(f32)
    return begin, first, second, third, finish


GATHER_SEMS = 9


def gather_scratch(k, n):
    DS, depth = pltpu.SemaphoreType.DMA, n // 8
    return [DS((1,)), DS((depth,)), DS((depth,)), DS((2, 2)), DS((2, 2)), DS((2, 3)), DS((2, 3)), DS((8,)), DS((8,))] * k


class Moves:
    def __init__(self, n, shard, whole, sems):
        self.n, self.shard, self.whole, self.sems = n, shard, whole, sems
        self.at = places()
        self.sides = tuple(enumerate(halves(whole.shape[-1])))

    def remote(self, src, dst, send, recv, *peer):
        return pltpu.make_async_remote_copy(
            src_ref=src, dst_ref=dst, send_sem=send, recv_sem=recv, device_id=(flat(*peer),), device_id_type=MESH)

    def part(self, name, t, lo, hi):
        z, y, x, c = self.at
        index = {
            "p": (slice(None), y, x, c),
            "q": (slice(None), y, slice(None), c) if t == 0 else (slice(None), slice(None), x, c),
            "c1": (slice(None), y, 1 - x, c) if t == 0 else (slice(None), 1 - y, x, c),
            "c2": (slice(None), 1 - y, slice(None), c) if t == 0 else (slice(None), slice(None), 1 - x, c),
        }["p" if name == "c0" else name]
        return self.whole.at[index + (slice(None), slice(lo, hi))]

    def copies(self, name):
        z, y, x, c = self.at
        own, z_send, z_recv, p, q, c_send, c_recv, d_send, d_recv = self.sems
        depth = self.n // 8
        if name == "z":
            mine = self.whole.at[z, y, x, c]
            return [pltpu.make_async_copy(self.shard, mine, own.at[0])] + [
                self.remote(self.shard, mine, z_send.at[s], z_recv.at[s], lax.rem(z + s, depth), y, x, c) for s in range(1, depth)]
        if name == "d":
            mine = self.whole.at[:, y, x, c]
            found = []
            for k in range(1, 8):
                other = lax.rem((y * 2 + x) * 2 + c + k, 8)
                found.append(self.remote(mine, mine, d_send.at[k], d_recv.at[k], z, 0, 0, other))
            return found
        found = []
        for t, (lo, hi) in self.sides:
            src = self.part(name, t, lo, hi)
            if name[0] == "c":
                j = int(name[1])
                found.append(self.remote(src, src, c_send.at[t, j], c_recv.at[t, j], z, y, x, 1 - c))
                continue
            sem = p if name == "p" else q
            peer = (z, y, 1 - x, c) if (t == 0) == (name == "p") else (z, 1 - y, x, c)
            found.append(self.remote(src, src, sem.at[t, 0], sem.at[t, 1], *peer))
        return found

    def start(self, *names):
        for name in names:
            for copy in self.copies(name):
                copy.start()

    def wait(self, *names):
        for name in names:
            for copy in self.copies(name):
                copy.wait()


def moves(n, shards, wholes, rest):
    return [Moves(n, shard, whole, rest[GATHER_SEMS * i : GATHER_SEMS * (i + 1)]) for i, (shard, whole) in enumerate(zip(shards, wholes))]


def spread_shapes(shards, n):
    return [((n // 8, 2, 2, 2) + v.shape, v.dtype, "any") for v in shards]


def whole_shapes(wholes):
    return [(v.shape, v.dtype, "any") for v in wholes]


def gathered(v, n):
    return v.reshape((n * v.shape[4],) + v.shape[5:])


def body0(n, *refs):
    lat, norms, first = moves(n, refs[:3], refs[3:6], refs[6:])
    greet(n)
    greeted(n)
    for m in (lat, norms, first):
        m.start("z")
    for m in (lat, norms):
        m.wait("z")
        m.start("d")
    first.wait("z")
    first.start("p", "c0")
    lat.wait("d")
    norms.wait("d")
    first.wait("p", "c0")


def stage0(shards, n):
    return pl.pallas_call(
        functools.partial(body0, n),
        in_specs=[pl.BlockSpec(memory_space=pl.ANY)] * len(shards),
        out_specs=[pl.BlockSpec(memory_space=pl.ANY)] * len(shards),
        out_shape=[jax.ShapeDtypeStruct(shape, kind) for shape, kind, _ in spread_shapes(shards, n)],
        scratch_shapes=gather_scratch(len(shards), n),
        compiler_params=pltpu.CompilerParams(collective_id=1, has_side_effects=True),
    )(*shards)


def run_ticks(step, n, ticks, at):
    @pl.when(step == 0)
    def _():
        greet(n)
    for j in range(3):
        @pl.when(step == at[j])
        def _(j=j):
            if j == 0:
                greeted(n)
            ticks[j]()


def strips(rows, width, body, init):
    return lax.fori_loop(0, rows // STRIP, lambda k, carry: body(pl.ds(pl.multiple_of(k * STRIP, STRIP), STRIP), carry), init, unroll=True)


FOLDS1 = ((256, 384, 32), (384, 896, 128))
FOLDS2 = ((256, 384, 32),)
FOLDS3 = ((256, 768, 128),)


def body1(n, raw, lat, band, fproj, mask, spair, fpair, held, *refs):
    shards, (fast4, lat_pre, fone_pre, n1), wholes, (wide, acc), rest = refs[:2], refs[2:6], refs[6:9], refs[9:11], refs[11:]
    step = pl.program_id(0)
    clear_first(step, acc)
    ticks, swap = (), rest
    if n > 1:
        first, *others = moves(n, (None,) + tuple(shards), wholes, rest)
        swap = rest[3 * GATHER_SEMS :]

        def begin():
            first.start("q", "c1")
            for m in others:
                m.start("z")
        def middle():
            first.wait("q")
            first.start("c2")
        def finish():
            first.wait("c1", "c2")
            for m in others:
                m.wait("z")
        ticks = (begin, middle, lambda: None, lambda: None, finish)
        run_ticks(step, n, ticks, (1, 4, 6))
    f = split_fours(raw, wide).astype(bf16)
    fast4[...] = f
    prev, nxt = mask[0], mask[1]
    z = dot_nt(f[:, :384], lat[:, 256:]) + shift(dot_nt(f[:, 256:], lat[:, :256]), prev, 1)
    lat_pre[...] = z
    add_moments(step, acc, 0, z)
    y = dot(f, band[...])
    z = y[:, :128] + shift(y[:, 128:256], prev, 1) + shift(y[:, 256:], nxt, -1)
    fone_pre[...] = z
    add_moments(step, acc, 256, z)
    z = jnp.concatenate([dot(f[:, :256], fproj[...]), dot(f[:, 256:], fproj[...])], axis=1)
    add_moments(step, acc, 384, z)
    close_moments(step, acc, ((spair, 0, 256), (fpair, 0, 128), (fpair, 768, 1280)), n1, f.shape[0] * STEPS, FOLDS1, n, ticks, *swap)


def stage1(raw, lat, band, fproj, mask, spair, fpair, held, shards_of, n):
    rows = raw.shape[0] * raw.shape[1] // 4
    return run(functools.partial(body1, n), rows,
        [(raw, "rows")] + [(v, "all") for v in (lat, band, fproj, mask, spair, fpair)] + [(v, "any") for v in (held,) + tuple(shards_of)],
        [((rows, 512), bf16, "rows"), ((rows, 256), f32, "rows"), ((rows, 128), f32, "rows"), ((4, 896), f32, "all")] + whole_shapes([held]) + spread_shapes(shards_of, n),
        [pltpu.VMEM((rows * 4 // STEPS, 128), f32), pltpu.VMEM((2, 8, 896), f32)] + (gather_scratch(3, n) if n > 1 else []), n, (2, 896), 2, {7: 4})


def body2(n, side, slow, lat_pre, fone_pre, n1, first, fmid, mask, spair, fpair, held_a, held_b, shard,
          lateral, one_pre, ftwo_pre, n2, whole_a, whole_b, whole_c, grid, acc, *rest):
    step = pl.program_id(0)
    rows = slow.shape[0]
    n_lat, n_fone = n1[:, :256], n1[:, 256:384]
    ticks, swap = (), rest
    if n > 1:
        middle, last, proj = moves(n, (None, None, shard), (whole_a, whole_b, whole_c), rest)
        swap = rest[3 * GATHER_SEMS :]

        def begin():
            middle.start("p", "c0")
            last.start("p", "c0")
            proj.start("z")
        def half():
            middle.wait("p")
            middle.start("q", "c1")
        def late():
            proj.wait("z")
            proj.start("p", "c0")
        def close():
            middle.wait("q")
            middle.start("c2")
        def finish():
            last.wait("p", "c0")
            proj.wait("p", "c0")
            middle.wait("c0", "c1", "c2")
        ticks = (begin, half, late, close, finish)
        run_ticks(step, n, ticks, (1, 3, 5))

    def put(block):
        part = fone_pre[pl.ds(pl.multiple_of(block * rows, 16), rows), :]
        fill(grid, side, silu(acted(part, n_fone)).astype(bf16), block)

    @pl.when(step == 0)
    def _():
        clear(grid)
        clear(acc)
        put(0)

    put(jnp.minimum(step + 1, STEPS - 1))
    lat = silu(acted(lat_pre[...], n_lat)).astype(bf16)
    lateral[...] = lat
    joined = jnp.concatenate([slow[...], lat], axis=1)
    z = dot(joined, first[1]) + shift(dot(joined, first[0]), mask[0], 1) + shift(dot(joined, first[2]), mask[1], -1)
    one_pre[...] = z
    add_moments(step, acc, 0, z)
    z = dot(tap_columns(grid, side, step, rows, False), fmid[...])
    ftwo_pre[...] = z
    add_moments(step, acc, 256, z)
    close_moments(step, acc, ((spair, 256, 512), (fpair, 128, 256)), n2, rows * STEPS, FOLDS2, n, ticks, *swap)


def stage2(slow, lat_pre, fone_pre, n1, first, fmid, mask, spair, fpair, held, shard, side, n):
    rows = slow.shape[0]
    frames = rows // side**2
    return run(functools.partial(body2, n, side), rows,
        [(slow, "rows"), (lat_pre, "rows")] + [(v, "all") for v in (fone_pre, n1, first, fmid, mask, spair, fpair)] + [(v, "any") for v in tuple(held) + (shard,)],
        [((rows, 256), bf16, "rows"), ((rows, 256), f32, "rows"), ((rows, 128), f32, "rows"), ((4, 384), f32, "all")] + whole_shapes(held) + spread_shapes([shard], n),
        [pltpu.VMEM(((side + 2) ** 2 * frames, 128), bf16), pltpu.VMEM((2, 8, 384), f32)] + (gather_scratch(3, n) if n > 1 else []), n, (2, 384), 3, {9: 4, 10: 5})


def body3(n, side, one_pre, ftwo_pre, n2, middle, flast, spair, fpair, held_a, held_b, two_pre, ftwo, n3, whole_a, whole_b, grid, acc, *rest):
    step = pl.program_id(0)
    rows = two_pre.shape[0]
    n_one, n_ftwo = n2[:, :256], n2[:, 256:]
    ticks, swap = (), rest
    if n > 1:
        both = moves(n, (None, None), (whole_a, whole_b), rest)
        swap = rest[2 * GATHER_SEMS :]

        def begin():
            for m in both:
                m.start("q", "c1")
        def half():
            for m in both:
                m.wait("q")
                m.start("c2")
        def finish():
            for m in both:
                m.wait("c1", "c2")
        ticks = (begin, half, lambda: None, lambda: None, finish)
        run_ticks(step, n, ticks, (1, 5, 6))

    def put(block):
        part = one_pre[pl.ds(pl.multiple_of(block * rows, 16), rows), :]
        fill(grid, side, silu(acted(part, n_one)).astype(bf16), block)

    @pl.when(step == 0)
    def _():
        clear(grid)
        clear(acc)
        put(0)

    put(jnp.minimum(step + 1, STEPS - 1))
    z = dot(tap_columns(grid, side, step, rows, False), middle[...])
    two_pre[...] = z
    add_moments(step, acc, 0, z)
    f = silu(acted(ftwo_pre[...], n_ftwo)).astype(bf16)
    ftwo[...] = f
    for k in range(2):
        add_moments(step, acc, 256 * (k + 1), dot(f, flast[:, 256 * k : 256 * (k + 1)]))
    close_moments(step, acc, ((spair, 512, 768), (fpair, 256, 768)), n3, rows * STEPS, FOLDS3, n, ticks, *swap)


def stage3(one_pre, ftwo_pre, n2, middle, flast, spair, fpair, held, side, n):
    rows = one_pre.shape[0]
    frames = rows // side**2
    return run(functools.partial(body3, n, side), rows,
        [(one_pre, "all"), (ftwo_pre, "rows")] + [(v, "all") for v in (n2, middle, flast, spair, fpair)] + [(v, "any") for v in held],
        [((rows, 256), f32, "rows"), ((rows, 128), bf16, "rows"), ((4, 768), f32, "all")] + whole_shapes(held),
        [pltpu.VMEM(((side + 2) ** 2 * frames, 256), bf16), pltpu.VMEM((2, 8, 768), f32)] + (gather_scratch(2, n) if n > 1 else []), n, (2, 768), 4, {7: 3, 8: 4})


def body4(n, two_pre, slow, lateral, n3, last, proj, spair, two, proj_pre, n4, acc, *swap):
    step = pl.program_id(0)
    clear_first(step, acc)
    v = silu(acted(two_pre[...], n3[:, :256])).astype(bf16)
    two[...] = v
    for k in range(4):
        add_moments(step, acc, 256 * k, dot(v, last[:, 256 * k : 256 * (k + 1)]))
    joined = jnp.concatenate([slow[...], lateral[...]], axis=1)
    for k in range(4):
        z = dot(joined, proj[:, 256 * k : 256 * (k + 1)])
        proj_pre[:, 256 * k : 256 * (k + 1)] = z.astype(proj_pre.dtype)
        add_moments(step, acc, 1024 + 256 * k, z)
    if n > 1:
        @pl.when(step == 0)
        def _():
            greet(n)
    close_moments(step, acc, ((spair, 768, 2816),), n4, v.shape[0] * STEPS, (), n,
        (None, None, None, lambda: greeted(n), lambda: None), *swap)


def stage4(two_pre, slow, lateral, n3, last, proj, spair, n):
    rows = two_pre.shape[0]
    return run(functools.partial(body4, n), rows,
        [(v, "rows") for v in (two_pre, slow, lateral)] + [(v, "all") for v in (n3, last, proj, spair)],
        [((rows, 256), bf16, "rows"), ((rows, 1024), f32, "rows"), ((4, 2048), f32, "all")], [pltpu.VMEM((2, 8, 2048), f32)], n, (2, 2048), 5)


def body5(two, proj_pre, cot, fast4, ftwo, fcot, n1, n3, n4, last, fproj, flast,
          slow_out, fast_out, delta, fdelta, sums, wide, three, fthree, fskip, fgrad, fout, acc):
    step = pl.program_id(0)
    rows = two.shape[0]
    clear_first(step, acc)
    fgrad[...] = split_fours(fcot, wide)
    three[...] = dot(two[...], last[...])
    fthree[...] = dot(ftwo[...], flast[...])
    for k in range(2):
        fskip[:, 256 * k : 256 * (k + 1)] = dot(fast4[:, 256 * k : 256 * (k + 1)], fproj[...])

    def side_of(za, zb, grad, na, nb, out, keep, lo, lanes):
        ga, gb, base = 0.5 * na[1:2] * na[2:3], 0.5 * nb[1:2] * nb[2:3], 0.5 * (na[3:4] + nb[3:4])
        ma, mb = na[0:1], nb[0:1]
        def one(at, carry):
            ha = za[at, lanes].astype(f32) - ma
            hb = zb[at, lanes].astype(f32) - mb
            h = ha * ga + hb * gb + base
            th = jnp.tanh(h)
            u = 1.0 + th
            out[at, lanes] = (h * u).astype(out.dtype)
            d = (0.5 * grad[at, lanes].astype(f32)) * (u * (1.0 + h * (1.0 - th)))
            keep[at, lanes] = d
            return carry[0] + eighth(d), carry[1] + eighth(d * ha), carry[2] + eighth(d * hb)
        zero = jnp.zeros((8, 256), f32)
        add_sums(step, acc, lo, strips(rows, 256, one, (zero, zero, zero)))

    for k in range(4):
        lanes = slice(256 * k, 256 * (k + 1))
        side_of(three, proj_pre, cot, n4[:, lanes], n4[:, 1024 + 256 * k : 1280 + 256 * k], slow_out, delta, 256 * k, lanes)
    for k in range(2):
        lanes = slice(256 * k, 256 * (k + 1))
        side_of(fthree, fskip, fgrad, n3[:, 256 + 256 * k : 512 + 256 * k], n1[:, 384 + 256 * k : 640 + 256 * k], fout, fdelta, 1024 + 256 * k, lanes)
    join_fours(fout[...], wide, fast_out)

    @pl.when(step == STEPS - 1)
    def _():
        scales = (1.0, jnp.concatenate([n4[1:2, :1024], n3[1:2, 256:]], axis=1), jnp.concatenate([n4[1:2, 1024:], n1[1:2, 384:]], axis=1))
        for k in range(3):
            sums[k : k + 1] = jnp.sum(acc[k], axis=0, keepdims=True) * scales[k]


def stage5(two, proj_pre, cot, fast4, ftwo, fcot, n1, n3, n4, last, fproj, flast):
    rows = two.shape[0]
    part = rows // STEPS
    return run(body5, rows,
        [(two, "rows"), (proj_pre, "rows"), (cot, "rows"), (fast4, "rows"), (ftwo, "rows"), (fcot, "rows"),
         (n1, "all"), (n3, "all"), (n4, "all"), (last, "all"), (fproj, "all"), (flast, "all")],
        [((rows, 1024), bf16, "rows"), (fcot.shape, bf16, "rows"), ((rows, 1024), f32, "rows"), ((rows, 512), f32, "rows"), ((3, 1536), f32, "all")],
        [pltpu.VMEM((part * 4, 128), f32), pltpu.VMEM((part, 1024), f32), pltpu.VMEM((part, 512), f32), pltpu.VMEM((part, 512), f32),
         pltpu.VMEM((part, 512), f32), pltpu.VMEM((part, 512), f32), pltpu.VMEM((3, 8, 1536), f32)])


def body5x(n, own, out, *links):
    greet(n)
    greeted(n)
    sum_pack(total_of(n, False, own, *links), out, ((1024, 1536, 128),))


def stage5x(sums, n):
    return pl.pallas_call(
        functools.partial(body5x, n),
        in_specs=[pl.BlockSpec(memory_space=pltpu.VMEM)],
        out_specs=pl.BlockSpec(memory_space=pltpu.VMEM),
        out_shape=jax.ShapeDtypeStruct(sums.shape, f32),
        scratch_shapes=swap_scratch(sums.shape, n),
        compiler_params=pltpu.CompilerParams(collective_id=6, has_side_effects=True),
    )(sums)


def body6(n, total, two, two_pre, proj_pre, slow, lateral, delta, fast4, ftwo, ftwo_pre, fdelta, n1, n2, n3, n4, s5, last, fproj, flast,
          d_proj, d_fproj, last_term, proj_term, flast_term, e_two, e_ftwo, sums,
          three, fthree, fskip, d_three, d_fthree, acc, last_acc, proj_acc, *swap):
    step = pl.program_id(0)
    rows = two.shape[0]
    clear_first(step, acc, last_acc, proj_acc, flast_term)
    three[...] = dot(two[...], last[...])
    fthree[...] = dot(ftwo[...], flast[...])
    for k in range(2):
        fskip[:, 256 * k : 256 * (k + 1)] = dot(fast4[:, 256 * k : 256 * (k + 1)], fproj[...])

    def side_of(za, zb, e, na, nb, s, da, db, lanes):
        pa, pb = na[2:3] * na[1:2], nb[2:3] * nb[1:2]
        qa, qb = pa * na[1:2] * s[1:2], pb * nb[1:2] * s[2:3]
        ma, mb, base = na[0:1], nb[0:1], s[0:1]
        def one(at, carry):
            d = e[at, lanes] - base
            da[at, lanes] = (d * pa - (za[at, lanes].astype(f32) - ma) * qa).astype(bf16)
            db[at, lanes] = (d * pb - (zb[at, lanes].astype(f32) - mb) * qb).astype(bf16)
            return carry
        strips(rows, 256, one, 0)

    for k in range(4):
        lanes = slice(256 * k, 256 * (k + 1))
        side_of(three, proj_pre, delta, n4[:, lanes], n4[:, 1024 + 256 * k : 1280 + 256 * k], s5[:, lanes] * (1.0 / total), d_three, d_proj, lanes)
    for k in range(2):
        lanes = slice(256 * k, 256 * (k + 1))
        side_of(fthree, fskip, fdelta, n3[:, 256 + 256 * k : 512 + 256 * k], n1[:, 384 + 256 * k : 640 + 256 * k],
                s5[:, 1024 + 256 * k : 1280 + 256 * k] * (0.25 / total), d_fthree, d_fproj, lanes)

    wide = slow.shape[1]
    last_acc[...] += dot_tn(two[...], d_three[...])
    proj_acc[:wide] += dot_tn(slow[...], d_proj[...])
    proj_acc[wide:] += dot_tn(lateral[...], d_proj[...])
    flast_term[...] += dot_tn(ftwo[...], d_fthree[...])
    h = normed(two_pre[...], n3[:, :256])
    e = dot_nt(d_three[...], last[...]) * slope(scaled(h, n3[:, :256]))
    e_two[...] = e
    add_sums(step, acc, 0, (eighth(e), eighth(e * h)))
    h = normed(ftwo_pre[...], n2[:, 256:])
    e = dot_nt(d_fthree[...], flast[...]) * slope(scaled(h, n2[:, 256:]))
    e_ftwo[...] = e
    add_sums(step, acc, 256, (eighth(e), eighth(e * h)))
    close_sums(step, acc, sums, ((256, 384, 32),), n, (), *swap)

    @pl.when(step == STEPS - 1)
    def _():
        last_term[...] = last_acc[...].astype(bf16)
        proj_term[...] = proj_acc[...].astype(bf16)


def stage6(total, two, two_pre, proj_pre, slow, lateral, delta, fast4, ftwo, ftwo_pre, fdelta, n1, n2, n3, n4, s5, last, fproj, flast, n):
    rows = two.shape[0]
    part = rows // STEPS
    return run(functools.partial(body6, n, total), rows,
        [(a, "rows") for a in (two, two_pre, proj_pre, slow, lateral, delta, fast4, ftwo, ftwo_pre, fdelta)]
        + [(a, "all") for a in (n1, n2, n3, n4, s5, last, fproj, flast)],
        [((rows, 1024), bf16, "rows"), ((rows, 512), bf16, "rows"), ((256, 1024), bf16, "all"), ((1280, 1024), bf16, "all"), ((128, 512), f32, "all"),
         ((rows, 256), f32, "rows"), ((rows, 128), f32, "rows"), ((2, 384), f32, "all")],
        [pltpu.VMEM((part, 1024), f32), pltpu.VMEM((part, 512), f32), pltpu.VMEM((part, 512), f32),
         pltpu.VMEM((part, 1024), bf16), pltpu.VMEM((part, 512), bf16), pltpu.VMEM((2, 8, 384), f32),
         pltpu.VMEM((256, 1024), f32), pltpu.VMEM((1280, 1024), f32)], n, (2, 384), 7)


def body7(n, side, total, one_pre, two_pre, e_two, fone_pre, ftwo_pre, e_ftwo, n1, n2, n3, s6, middle, fmid, proj_term,
          middleerm, fmid_term, e_one, e_fone, sums, proj_grad, grid, fgrid, acc, mid_acc, *rest):
    step = pl.program_id(0)
    ticks, swap = (), rest
    if n > 1:
        ticks = scatter_ticks(n, (proj_term,), (proj_grad,), rest[:11])
        swap = rest[11:]
        run_ticks(step, n, ticks, (1, 3, 5))
    rows = one_pre.shape[0]

    def put(block):
        at = pl.ds(pl.multiple_of(block * rows, 16), rows)
        p, s = n3[:, :256], s6[:, :256] * (1.0 / total)
        fill(grid, side, input_grad(e_two[at, :], normed(two_pre[at, :], p), p, s[0:1], s[1:2]), block)
        p, s = n2[:, 256:], s6[:, 256:] * (0.25 / total)
        fill(fgrid, side, input_grad(e_ftwo[at, :], normed(ftwo_pre[at, :], p), p, s[0:1], s[1:2]), block)

    @pl.when(step == 0)
    def _():
        clear(grid)
        clear(fgrid)
        clear(acc)
        put(0)
        mid_acc[...] = jnp.zeros_like(mid_acc)
        fmid_term[...] = jnp.zeros_like(fmid_term)

    put(jnp.minimum(step + 1, STEPS - 1))

    def one_side(pre, p, columns, weight, lo, term, e_out):
        h = normed(pre[...], p)
        act = scaled(h, p)
        s = sigma(act)
        mid = act * s
        term[...] += dot_tn(mid.astype(bf16), columns)
        width = weight.shape[1]
        turned = jnp.concatenate([weight[width * k : width * (k + 1)] for k in range(9)], axis=1)
        e = dot_nt(columns, turned) * (s + mid * (1.0 - s))
        e_out[...] = e
        add_sums(step, acc, lo, (eighth(e), eighth(e * h)))

    one_side(one_pre, n2[:, :256], tap_columns(grid, side, step, rows, True), middle, 0, mid_acc, e_one)
    one_side(fone_pre, n1[:, 256:384], tap_columns(fgrid, side, step, rows, True), fmid, 256, fmid_term, e_fone)
    close_sums(step, acc, sums, ((256, 384, 32),), n, ticks, *swap)

    @pl.when(step == STEPS - 1)
    def _():
        for k in range(9):
            middleerm[k] = mid_acc[:, 256 * k : 256 * (k + 1)].astype(bf16)


def stage7(total, one_pre, two_pre, e_two, fone_pre, ftwo_pre, e_ftwo, n1, n2, n3, s6, middle, fmid, proj_term, side, n):
    terms = [six(v, n) for v in (proj_term,)] if n > 1 else [proj_term]
    parts = [(v.shape[0] // n, v.shape[1]) for v in (proj_term,)]
    rows = one_pre.shape[0]
    frames = rows // side**2
    return run(functools.partial(body7, n, side, total), rows,
        [(one_pre, "rows"), (two_pre, "all"), (e_two, "all"), (fone_pre, "rows"), (ftwo_pre, "all"), (e_ftwo, "all")]
        + [(a, "all") for a in (n1, n2, n3, s6, middle, fmid)] + [(v, "any") for v in terms],
        [((9, 256, 256), bf16, "all"), ((128, 1152), f32, "all"), ((rows, 256), f32, "rows"), ((rows, 128), f32, "rows"), ((2, 384), f32, "all")] + [(part, f32, "all") for part in parts],
        [pltpu.VMEM(((side + 2) ** 2 * frames, 256), bf16), pltpu.VMEM(((side + 2) ** 2 * frames, 128), bf16),
         pltpu.VMEM((2, 8, 384), f32), pltpu.VMEM((256, 2304), f32)] + (scatter_scratch(parts, n) if n > 1 else []), n, (2, 384), 8)


def body8(n, total, slow, lateral, one_pre, e_one, n2, s7, mask, middleerm, first_term, pieces, middle_grad, first_acc, *rest):
    step = pl.program_id(0)
    if n > 1:
        ticks = scatter_ticks(n, (middleerm,), (middle_grad,), rest)
        run_ticks(step, n, ticks, (1, 2, 4))

        @pl.when(step == STEPS - 1)
        def _():
            ticks[3]()
    clear_first(step, first_acc)
    p, s = n2[:, :256], s7[:, :256] * (1.0 / total)
    d = input_grad(e_one[...], normed(one_pre[...], p), p, s[0:1], s[1:2])
    w = d.astype(f32)
    rows = w.shape[0]
    before = pltpu.roll(masked(w, mask[0]), rows - 1, 0).astype(bf16)
    after = pltpu.roll(masked(w, mask[1]), 1, 0).astype(bf16)
    columns = jnp.concatenate([before, d, after], axis=1)
    pieces[...] = columns
    wide = slow.shape[1]
    first_acc[:wide] += dot_tn(slow[...], columns)
    first_acc[wide:] += dot_tn(lateral[...], columns)

    @pl.when(step == STEPS - 1)
    def _():
        for k in range(3):
            first_term[k] = first_acc[:, 256 * k : 256 * (k + 1)].astype(bf16)
        if n > 1:
            ticks[4]()


def stage8(total, slow, lateral, one_pre, e_one, n2, s7, mask, middleerm, n):
    rows = slow.shape[0]
    part = (middleerm.shape[0] // n, middleerm.shape[1])
    return run(functools.partial(body8, n, total), rows,
        [(a, "rows") for a in (slow, lateral, one_pre, e_one)] + [(a, "all") for a in (n2, s7, mask)]
        + [(six(middleerm, n) if n > 1 else middleerm, "any")],
        [((3, 1280, 256), bf16, "all"), ((rows, 768), bf16, "rows"), (part, f32, "all")],
        [pltpu.VMEM((1280, 768), f32)] + (scatter_scratch([part], n) if n > 1 else []), n, None, 12)


def body8b(n, pieces, d_proj, lat_pre, n1, first, proj, last_term, first_term,
           slow_grad, e_lat, sums, last_grad, first_grad, acc, *rest):
    step = pl.program_id(0)
    ticks, swap = (), rest
    if n > 1:
        ticks = scatter_ticks(n, (last_term, first_term), (last_grad, first_grad), rest[:16])
        swap = rest[16:]
        run_ticks(step, n, ticks, (1, 3, 5))
    clear_first(step, acc)
    wide = proj.shape[0] - 256

    def back(lo, hi):
        part = dot_nt(d_proj[...], proj[lo:hi])
        for k in range(3):
            part += dot_nt(pieces[:, 256 * k : 256 * (k + 1)], first[k, lo:hi])
        return part

    for k in range(4):
        slow_grad[:, 256 * k : 256 * (k + 1)] = back(256 * k, 256 * (k + 1)).astype(bf16)
    h = normed(lat_pre[...], n1[:, :256])
    e = back(wide, wide + 256) * slope(scaled(h, n1[:, :256]))
    e_lat[...] = e
    add_sums(step, acc, 0, (eighth(e), eighth(e * h)))
    close_sums(step, acc, sums, (), n, ticks, *swap)


def stage8b(pieces, d_proj, lat_pre, n1, first, proj, last_term, first_term, n):
    rows = pieces.shape[0]
    terms = [six(v, n) if n > 1 else v for v in (last_term, first_term)]
    parts = [(v.shape[0] // n, v.shape[1]) for v in (last_term, first_term)]
    return run(functools.partial(body8b, n), rows,
        [(a, "rows") for a in (pieces, d_proj, lat_pre)] + [(a, "all") for a in (n1, first, proj)] + [(v, "any") for v in terms],
        [((rows, 1024), bf16, "rows"), ((rows, 256), f32, "rows"), ((2, 256), f32, "all")] + [(part, f32, "all") for part in parts],
        [pltpu.VMEM((2, 8, 256), f32)] + (scatter_scratch(parts, n) if n > 1 else []), n, (2, 256), 9)


def lanes_at(v, source, target):
    moved = pltpu.roll(v, (target - source) % 128, 1) if target != source else v
    lane = lax.broadcasted_iota(jnp.int32, v.shape, 1)
    return jnp.where((lane >= target) & (lane < target + 32), moved, 0.0)


def pack_fast(out, band, fproj, flast, fmid):
    places_of = (
        ((0, 0, 1), (0, 1, 2), (0, 2, 3), (1, 3, 0)),
        ((0, 0, 0), (0, 1, 1), (0, 2, 2), (0, 3, 3)),
        ((0, 1, 0), (0, 2, 1), (0, 3, 2), (2, 0, 3)),
    )
    for tap in range(3):
        out[32 * tap : 32 * (tap + 1)] = sum(
            band[128 * part + 32 * j : 128 * part + 32 * (j + 1), 128 * k : 128 * (k + 1)] for part, k, j in places_of[tap])
    out[96:224] = fproj[...]
    out[224:256] = sum(flast[32 * k : 32 * (k + 1), 128 * k : 128 * (k + 1)] for k in range(4))
    for group in range(3):
        total = None
        for tap in range(4 * group, min(4 * group + 4, 9)):
            for k in range(4):
                turned = fmid[:, 128 * tap : 128 * (tap + 1)].T
                v = lanes_at(turned[32 * k : 32 * (k + 1)], 32 * k, 32 * (tap % 4))
                total = v if total is None else total + v
        out[256 + 32 * group : 288 + 32 * group] = total
    out[352:384] = jnp.zeros((32, 128), f32)


def own_pair(out, sums, lo, hi, row):
    share = out.shape[1]
    back = lax.rem(hi - lo - lax.axis_index("fsdp") * share, hi - lo)
    for at, k in enumerate((row, 0)):
        wide = jnp.broadcast_to(sums[k : k + 1, lo:hi], (8, hi - lo))
        out[at : at + 1] = pltpu.roll(wide, back, 1)[0:1, :share]


def body9(n, total, fast4, lat_pre, e_lat, fone_pre, e_fone, d_fproj, ready, n1, s5, s6, s7, s8, lat, band, fproj, mask, flast_term, fmid_term,
          ready_first, ready_middle, ready_last, ready_proj, lat_term, packed, raw, slow_grad, lat_n, one_n, two_n, out_n, proj_n, mid_n, fout_n,
          first_grad, middle_grad, last_grad, proj_grad, wide, lat_acc, whole, band_term, fproj_term):
    step = pl.program_id(0)
    clear_first(step, lat_acc, band_term, fproj_term)
    slow_grad[...] = ready[...]
    rows = fast4.shape[0]
    def backward(e, pre, p, s):
        d = input_grad(e[...], normed(pre[...], p), p, s[0:1], s[1:2])
        w = d.astype(f32)
        return d, pltpu.roll(masked(w, mask[0]), rows - 1, 0).astype(bf16), pltpu.roll(masked(w, mask[1]), 1, 0).astype(bf16)
    d, before, _ = backward(e_lat, lat_pre, n1[:, :256], s8[...] * (1.0 / total))
    f, fbefore, fafter = backward(e_fone, fone_pre, n1[:, 256:384], s7[:, 256:] * (0.25 / total))
    narrow = jnp.concatenate([f, fbefore, fafter], axis=1)
    lat_acc[:, :256] += dot_tn(before, fast4[:, 256:])
    lat_acc[:, 256:] += dot_tn(d, fast4[:, :384])
    band_term[...] += dot_tn(narrow, fast4[...])
    for k in range(4):
        fproj_term[...] += dot_tn(fast4[:, 128 * k : 128 * (k + 1)], d_fproj[:, 128 * k : 128 * (k + 1)])
    base = dot_nt(narrow, band[...])
    skip = jnp.concatenate([dot_nt(d_fproj[:, 256 * k : 256 * (k + 1)], fproj[...]) for k in range(2)], axis=1)
    whole[...] = base + skip
    whole[:, :384] += dot(d, lat[:, 256:])
    whole[:, 256:] += dot(before, lat[:, :256])
    join_fours(whole[...], wide, raw)

    @pl.when(step == STEPS - 1)
    def _():
        lat_term[...] = lat_acc[...].astype(bf16)
        for grad, found in ((first_grad, ready_first), (middle_grad, ready_middle), (last_grad, ready_last), (proj_grad, ready_proj)):
            grad[...] = found[...]
        pack_fast(packed, band_term, fproj_term, flast_term, fmid_term)
        if n > 1:
            own_pair(lat_n, s8, 0, 256, 1)
            own_pair(one_n, s7, 0, 256, 1)
            own_pair(two_n, s6, 0, 256, 1)
            own_pair(out_n, s5, 0, 1024, 1)
            own_pair(proj_n, s5, 0, 1024, 2)
        for j, (sums, lo, row) in enumerate(((s7, 256, 1), (s6, 256, 1))):
            mid_n[j, 0:1] = sums[row : row + 1, lo : lo + 32]
            mid_n[j, 1:2] = sums[0:1, lo : lo + 32]
        for j in range(2):
            fout_n[j, 0:1] = s5[j + 1 : j + 2, 1024:1152]
            fout_n[j, 1:2] = s5[0:1, 1024:1152]


def stage9(total, fast4, lat_pre, e_lat, fone_pre, e_fone, d_fproj, ready, n1, s5, s6, s7, s8, lat, band, fproj, mask, flast_term, fmid_term, grads, n):
    rows = fast4.shape[0]
    part = rows // STEPS
    return run(functools.partial(body9, n, total), rows,
        [(a, "rows") for a in (fast4, lat_pre, e_lat, fone_pre, e_fone, d_fproj, ready)]
        + [(a, "all") for a in (n1, s5, s6, s7, s8, lat, band, fproj, mask, flast_term, fmid_term) + tuple(grads)],
        [((256, 640), bf16, "all"), ((384, 128), f32, "all"), ((rows // 16, 64, 128), bf16, "rows"), (ready.shape, bf16, "rows")]
        + [((2, 256 // n), f32, "all")] * 3 + [((2, 1024 // n), f32, "all")] * 2 + [((2, 2, 32), f32, "all"), ((2, 2, 128), f32, "all")] + [(v.shape, f32, "all") for v in grads],
        [pltpu.VMEM((part * 4, 128), f32), pltpu.VMEM((256, 640), f32), pltpu.VMEM((part, 512), f32),
         pltpu.VMEM((384, 512), f32), pltpu.VMEM((128, 128), f32)])


def body10(n, lat_term, packed, lat_grad, first_t, middle_t, last, proj, sums, slots, line, mine, lat_slots, lat_line, lat_mine,
           a_send, a_recv, b_send, b_recv, g_send, g_recv, l_send, l_recv, m_send, m_recv):
    me = lax.axis_index("fsdp")
    mi, mo, depth = lax.rem(me, INNER), lax.div(me, INNER), n // INNER
    peers = [mo * INNER + lax.rem(mi + k, INNER) for k in range(INNER)]
    spots = [lax.rem(mi + k, INNER) for k in range(INNER)]
    beyond = [lax.rem(mo + k, depth) for k in range(depth)]

    def remote(src, dst, send, recv, peer):
        copy = pltpu.make_async_remote_copy(
            src_ref=src, dst_ref=dst, send_sem=send, recv_sem=recv, device_id=(peer,), device_id_type=MESH)
        copy.start()
        return copy

    greet(n)
    greeted(n)
    fast = [remote(packed.at[spots[k]], slots.at[mi], a_send.at[k], a_recv.at[k], peers[k]) for k in range(1, INNER)]
    slow = [remote(lat_term.at[:, spots[k]], lat_slots.at[mi], l_send.at[k], l_recv.at[k], peers[k]) for k in range(1, INNER)]
    slots[mi] = packed[mi]
    lat_slots[mi] = lat_term[:, mi]
    for copy in fast:
        copy.wait()
    mine[...] = sum(slots[k] for k in range(1, INNER)) + slots[0]
    fast = [remote(mine, line.at[mo], b_send.at[k], b_recv.at[k], beyond[k] * INNER + mi) for k in range(1, depth)]
    line[mo] = mine[...]
    for copy in slow:
        copy.wait()
    lat_mine[...] = sum(lat_slots[k].astype(f32) for k in range(INNER)).astype(bf16)
    slow = [remote(lat_mine.at[beyond[k]], lat_line.at[mo], m_send.at[k], m_recv.at[k], beyond[k] * INNER + mi) for k in range(1, depth)]
    lat_line[mo] = lat_mine[mo]
    for copy in fast:
        copy.wait()
    sums[mi] = sum((line[k] for k in range(1, depth)), line[0])
    fast = [remote(sums.at[mi], sums.at[mi], g_send.at[k], g_recv.at[k], peers[k]) for k in range(1, INNER)]
    for copy in slow:
        copy.wait()
    lat_grad[...] = sum(lat_line[k].astype(f32) for k in range(depth))
    for copy in fast:
        copy.wait()

    high = sums.shape[1]
    def rows_of(lo, hi):
        found = []
        while lo < hi:
            top = min(hi, (lo // high + 1) * high)
            found.append(sums[lo // high, lo % high : lo % high + top - lo])
            lo = top
        return jnp.concatenate(found, axis=0) if len(found) > 1 else found[0]

    for k in range(3):
        first_t[:, 128 * k : 128 * (k + 1)] = rows_of(32 * k, 32 * (k + 1))
        wide = min(128, 288 - 128 * k)
        middle_t[:, 128 * k : 128 * k + wide] = rows_of(256 + 32 * k, 288 + 32 * k)[:, :wide]
    proj[...] = rows_of(96, 224)
    last[...] = rows_of(224, 256)


def stage10(lat_term, packed, n):
    depth, DS = n // INNER, pltpu.SemaphoreType.DMA
    packed = packed.reshape(INNER, -1, 128)
    chunk = packed.shape[1:]
    share = (lat_term.shape[0] // n, lat_term.shape[1])
    lat_grad, first_t, middle_t, last, proj = pl.pallas_call(
        functools.partial(body10, n),
        in_specs=[pl.BlockSpec(memory_space=pltpu.VMEM)] * 2,
        out_specs=[pl.BlockSpec(memory_space=pltpu.VMEM)] * 5,
        out_shape=[jax.ShapeDtypeStruct(shape, f32) for shape in (share, (32, 384), (32, 288), (32, 128), (128, 128))],
        scratch_shapes=[pltpu.VMEM((INNER,) + chunk, f32), pltpu.VMEM((INNER,) + chunk, f32), pltpu.VMEM((depth,) + chunk, f32), pltpu.VMEM(chunk, f32),
            pltpu.VMEM((INNER, depth) + share, bf16), pltpu.VMEM((depth,) + share, bf16), pltpu.VMEM((depth,) + share, bf16)]
        + [DS((INNER,)), DS((INNER,)), DS((depth,)), DS((depth,)), DS((INNER,)), DS((INNER,)), DS((INNER,)), DS((INNER,)), DS((depth,)), DS((depth,))],
        compiler_params=pltpu.CompilerParams(collective_id=10, has_side_effects=True),
    )(lat_term.reshape((depth, INNER) + share), packed)
    return lat_grad, (first_t.T, middle_t.T, last, proj)


def spread(weight, groups):
    eye = jnp.eye(groups, dtype=weight.dtype)
    r, c = weight.shape[-2:]
    wide = eye[:, None, :, None] * weight[..., None, :, None, :]
    return wide.reshape(weight.shape[:-2] + (groups * r, groups * c))


def banded(fast_first):
    table = np.zeros((3, 4, 3, 4), np.float32)
    for tap in range(3):
        for j in range(4):
            k = j + tap - 1
            part = 1 if k < 0 else 2 if k > 3 else 0
            table[tap, k % 4, part, j] = 1
    tap = fast_first.reshape(3, 128, 32)
    total = sum(table[k].astype(tap.dtype)[:, None, :, :, None] * tap[k][None, :, None, None, :] for k in range(3))
    return total.reshape(512, 384)


def shards(slow_in, fast_in, clip_ids, lateral_weight, first_weight, middle_weight, last_weight, proj_weight,
           lat_norm, one_norm, two_norm, out_norm, proj_norm, fast_first, fast_middle, fast_last, fast_proj,
           fast_mid_norm, fast_out_norm, slow_cot, fast_cot):
    n = lax.axis_size("fsdp")
    side = slow_in.shape[1]
    count = slow_in.shape[0] * side * side * n
    norms = jnp.concatenate([lat_norm, one_norm, two_norm, out_norm, proj_norm], axis=1).astype(f32)
    norms = jnp.pad(norms, ((0, 6), (0, 128 - norms.shape[1])))
    lat, norms_full, first = stage0([lateral_weight.T, norms, first_weight], n)
    lat = gathered(lat, n)
    norms_full = norms_full.reshape(n, 8, 128)
    gains, offset = [], 0
    for pair in (lat_norm, one_norm, two_norm, out_norm, proj_norm):
        width = pair.shape[1]
        gains.append(norms_full[:, :2, offset : offset + width].transpose(1, 0, 2).reshape(2, -1))
        offset += width
    spair = jnp.concatenate(gains, axis=1)
    fpair = jnp.concatenate(
        [jnp.tile(pair[k].astype(f32), (1, 4)) for pair in (fast_mid_norm, fast_out_norm) for k in range(2)], axis=1)
    band = banded(fast_first)
    fproj = spread(fast_proj, 2)
    fmid = spread(fast_middle.reshape(9, 32, 32), 4)
    fmid = fmid.reshape(-1, 128)
    flast = spread(fast_last, 4)

    same = (clip_ids[0, 1:] == clip_ids[0, :-1]).astype(f32)
    closed = jnp.zeros((1,), f32)
    mask = jnp.stack([jnp.concatenate([closed, same]), jnp.concatenate([same, closed])])
    mask = jnp.broadcast_to(mask[:, :, None], mask.shape + (256,))

    def rows(v):
        return v.transpose(1, 2, 0, 3).reshape(-1, v.shape[3])
    def unrows(v):
        return v.reshape(side, side, -1, v.shape[1]).transpose(2, 0, 1, 3)
    def raw(v):
        return v.transpose(1, 2, 0, 3).reshape(side * side, -1, v.shape[3])
    def unraw(v):
        return v.reshape((side, side) + v.shape[1:]).transpose(2, 0, 1, 3)

    slow = rows(slow_in)
    fast4, lat_pre, fone_pre, n1, first, *held = stage1(
        raw(fast_in), lat, band, fproj, mask, spair, fpair, first, (middle_weight, last_weight), n)
    first = gathered(first, n).reshape(3, -1, first_weight.shape[1])
    lateral, one_pre, ftwo_pre, n2, middle, last, proj = stage2(
        slow, lat_pre, fone_pre, n1, first, fmid, mask, spair, fpair, held, proj_weight, side, n)
    middle = gathered(middle, n)
    two_pre, ftwo, n3, last, proj = stage3(one_pre, ftwo_pre, n2, middle, flast, spair, fpair, (last, proj), side, n)
    last, proj = gathered(last, n), gathered(proj, n)
    two, proj_pre, n4 = stage4(two_pre, slow, lateral, n3, last, proj, spair, n)
    slow_out, fast_out, delta, fdelta, local = stage5(
        two, proj_pre, rows(slow_cot), fast4, ftwo, raw(fast_cot), n1, n3, n4, last, fproj, flast)
    s5 = stage5x(local, n)
    d_proj, d_fproj, last_term, proj_term, flast_term, e_two, e_ftwo, s6 = stage6(
        count, two, two_pre, proj_pre, slow, lateral, delta, fast4, ftwo, ftwo_pre, fdelta, n1, n2, n3, n4, s5, last, fproj, flast, n)
    middle_term, fmid_term, e_one, e_fone, s7, proj_grad = stage7(
        count, one_pre, two_pre, e_two, fone_pre, ftwo_pre, e_ftwo, n1, n2, n3, s6, middle, fmid, proj_term, side, n)
    first_term, pieces, middle_grad = stage8(count, slow, lateral, one_pre, e_one, n2, s7, mask, middle_term.reshape(-1, 256), n)
    slow_grad, e_lat, s8, last_grad, first_grad = stage8b(
        pieces, d_proj, lat_pre, n1, first, proj, last_term, first_term.reshape(-1, 256), n)
    lat_term, packed, fast_grad, slow_grad, *small = stage9(
        count, fast4, lat_pre, e_lat, fone_pre, e_fone, d_fproj, slow_grad, n1, s5, s6, s7, s8, lat, band, fproj, mask, flast_term, fmid_term,
        (first_grad, middle_grad, last_grad, proj_grad), n)
    lateral_grad, fast_grads = stage10(lat_term, packed, n)
    return (unrows(slow_out), unraw(fast_out), unrows(slow_grad), unraw(fast_grad),
            lateral_grad.T, *small[7:],
            *small[:5], *fast_grads, *small[5:7])


def solution(mesh):
    in_specs = (
        P("fsdp", None, None, None),
        P("fsdp", None, None, None),
        P("fsdp", None),
        P(None, "fsdp"),
        P("fsdp", None),
        P("fsdp", None),
        P("fsdp", None),
        P("fsdp", None),
        P(None, "fsdp"),
        P(None, "fsdp"),
        P(None, "fsdp"),
        P(None, "fsdp"),
        P(None, "fsdp"),
        P(),
        P(),
        P(),
        P(),
        P(),
        P(),
        P("fsdp", None, None, None),
        P("fsdp", None, None, None),
    )
    out_specs = (
        P("fsdp", None, None, None),
        P("fsdp", None, None, None),
        P("fsdp", None, None, None),
        P("fsdp", None, None, None),
        P(None, "fsdp"),
        P("fsdp", None),
        P("fsdp", None),
        P("fsdp", None),
        P("fsdp", None),
        P(None, "fsdp"),
        P(None, "fsdp"),
        P(None, "fsdp"),
        P(None, "fsdp"),
        P(None, "fsdp"),
        P(),
        P(),
        P(),
        P(),
        P(),
        P(),
    )
    return jax.shard_map(shards, mesh=mesh, in_specs=in_specs, out_specs=out_specs, check_vma=False)
```

time: 1950 us -> 351 us (0.18)
  blocking collectives: 713 us -> 0 us
  waiting for transfers between devices: 625 us -> 0 us
  Pallas kernels: 0 us -> 326 us
  matrix products: 249 us -> 0 us
  other arithmetic: 193 us -> 6.14 us
  local copies, waits for them, and re-layouts: 150 us -> 17.3 us
    reduce_scatter x4 -> x0, waiting for transfers between devices: 490 us -> none  [the longest x1 145 us: shards(): lax.psum_scatter(proj_term, 'fsdp', scatter_dimension=0, tiled=True)]
    psum x11 -> x0, blocking collectives: 439 us -> none  [the longest x4 164 us: gather_stats(): totals = lax.psum(local_sums, 'fsdp')]
    pallas_call x0 -> x13, Pallas kernels: none -> 326 us  [the longest x10 279 us: run(): pl.pallas_call(body, grid=(STEPS,), in_specs=[spec(a.shape, how) for a, h...]
    all_gather x7 -> x0, blocking collectives: 274 us -> none  [the longest x1 44.6 us: shards(): lax.all_gather(lateral_weight, 'fsdp', axis=1, tiled=True)]
    dot_general x27 -> x0, matrix products: 249 us -> none  [the longest x9 108 us: back_product(): jnp.einsum('fhwd,cd->fhwc', gradient, weight, preferred_element_type=jnp....]
    psum x1 -> x0, waiting for transfers between devices: 118 us -> none  [reduce_norms(): sum_all, cross_all = lax.psum((firsts, seconds), 'fsdp')]
    slice x16 -> x3, local copies, waits for them, and re-layouts: 97.1 us -> 3.02 us  [the longest x2 2.29 us: shards(): norms_full[:, :2, offset:offset + width].transpose(1, 0, 2).reshape(2, -1)]
    reduce_sum x14 -> x0, other arithmetic: 73.8 us -> none  [the longest x5 47.9 us: reduce_norms(): jnp.sum(grad_out, axis=(0, 1, 2))]
  transfers between devices with their start and end apart: 9 -> 0, of which waited for: 6 -> 0; matrix products, arithmetic and copies ran while one was open for 13% -> 0% of each run, Pallas kernels for 0% -> 0%
where the time goes in v2:
time: 351 us; the launch traced here: 350 us
  Pallas kernels  326 us (93%)
  local copies, waits for them, and re-layouts  17.3 us (5%)
  other arithmetic  6.14 us (2%)
    pallas_call x10, Pallas kernels, run(): pl.pallas_call(body, grid=(STEPS,), in_specs=[spec(a.shape, how) for a, h...  279 us
    pallas_call x1, Pallas kernels, stage0(): pl.pallas_call(functools.partial(body0, n), in_specs=[pl.BlockSpec(memory...  19.4 us
    pallas_call x1, Pallas kernels, stage10(): pl.pallas_call(functools.partial(body10, n), in_specs=[pl.BlockSpec(memor...  16.6 us
    pallas_call x1, Pallas kernels, stage5x(): pl.pallas_call(functools.partial(body5x, n), in_specs=[pl.BlockSpec(memor...  11.1 us
    unnamed x22, local copies, waits for them, and re-layouts  9.89 us

profile of v2, /device:TPU:0, one launch (start us, length us, event | category | flops | bytes accessed | tf_op | source)
XLA Modules:
  0.0 349.9 jit_solution(18322301591797708984)
XLA Ops:
  6.8 0.9 broadcast_multiply_fusion.2
  9.9 1.0 multiply_add_fusion
  11.0 0.9 copy.63.band
  12.5 1.3 mul.124.fmid
  13.8 19.4 %shard_map.383 = (bf16[4,2,2,2,8,640]{5,4,3,2,1,0:T(8,128)(2,1)}, f32[4,2,2,2,8,128]{5,4,3,2,1,0:T(8,128)}, bf16[4,2,2,2,120,256]{5,4,3,2,1,0:T(8,128)(2,1)}) custom-call(bf16[8,640]{1,0:T(8,128)(2,1)} %bitcast.137, f32[8,128]{1,0:T(8,128)} %pad_convert_fusion.refs_1_, bf16[120,256]{1,0:T(8,128)(2,1)} %refs_2_.1), custom_call_target="tpu_custom_call" | custom-call | tf_op jit(solution)/shard_map/pallas_call | solution.py:501
  33.2 1.1 fusion.2
  34.3 1.2 fusion.3
  36.7 23.6 %shard_map.384 = (bf16[3136,512]{1,0:T(8,128)(2,1)}, f32[3136,256]{1,0:T(8,128)}, f32[3136,128]{1,0:T(8,128)}, f32[4,896]{1,0:T(4,128)}, bf16[4,2,2,2,120,256]{5...) custom-call(bf16[196,64,128]{2,1,0:T(8,128)(2,1)} %bitcast.114, ...), custom_call_target="tpu_custom_call", output_to_operand_aliasing={{4}: (7, {})} | custom-call | tf_op jit(solution)/shard_map/pallas_call | solution.py:253
  60.2 26.0 %shard_map.385 = (bf16[3136,256]{1,0:T(8,128)(2,1)}, f32[3136,256]{1,0:T(8,128)}, f32[3136,128]{1,0:T(8,128)}, f32[4,384]{1,0:T(4,128)}, bf16[4,2,2,2,72,256]{5,...) custom-call(bf16[3136,1024]{1,0:T(8,128)(2,1)} %bitcast.95, ...), custom_call_target="tpu_custom_call", output_to_operand_aliasing={{4}: (9, {}), {5}: (10, {})} | custom-call | tf_op jit(solution)/shard_map/pallas_call | solution.py:253
  86.3 25.4 %shard_map.386 = (f32[3136,256]{1,0:T(8,128)}, bf16[3136,128]{1,0:T(8,128)(2,1)}, f32[4,768]{1,0:T(4,128)}, bf16[4,2,2,2,8,1024]{5,4,3,2,1,0:T(8,128)(2,1)}, bf16[4,2,2,2,40,1024]{5,4,3,2,1,0:T(8,128)(2,1)}) custom-call(f32[3136,256]{1,0:T(8,128)} %get-tuple-element.101.one_pre, ...), custom_call_target="tpu_custom_call", output_to_operand_aliasing={{3}: (7, {}), {4}: (8, {})} | custom-call | tf_op jit(solution)/shard_map/pallas_call | solution.py:253
  111.6 27.4 %shard_map.387 = (bf16[3136,256]{1,0:T(8,128)(2,1)}, f32[3136,1024]{1,0:T(8,128)}, f32[4,2048]{1,0:T(4,128)}) custom-call(f32[3136,256]{1,0:T(8,128)} %get-tuple-element.107.two_pre, bf16[3136,1024]{1,0:T(8,128)(2,1)} %bitcast.96, bf16[3136,256]{1,0:T(8,128)(2,1)} %get-tuple-element.108.lateral, f32[4,768]{1,0:T(4,128)} %get-tuple-element.109.n3, ...), custom_call_target="tpu_custom_call" | custom-call | tf_op jit(solution)/shard_map/pallas_call | solution.py:253
  139.1 27.2 %shard_map.388 = (bf16[3136,1024]{1,0:T(8,128)(2,1)}, bf16[196,64,128]{2,1,0:T(8,128)(2,1)}, f32[3136,1024]{1,0:T(8,128)}, f32[3136,512]{1,0:T(8,128)}, f32[3,1536]{1,0:T(4,128)}) custom-call(bf16[3136,256]{1,0:T(8,128)(2,1)} %get-tuple-element.112.two, f32[3136,1024]{1,0:T(8,128)} %get-tuple-element.113.proj_pre, bf16[3136,1024]{1,0:T(8,128)(2,1)} %bitcast.108, ...), custom_call_target="tpu_custom_call" | custom-call | tf_op jit(solution)/shard_map/pallas_call | solution.py:253
  166.3 11.1 %shard_map.389.s5 = f32[3,1536]{1,0:T(4,128)} custom-call(f32[3,1536]{1,0:T(4,128)} %get-tuple-element.121.own), custom_call_target="tpu_custom_call" | custom-call | tf_op jit(solution)/shard_map/pallas_call | solution.py:778
  177.4 40.8 %shard_map.390 = (bf16[3136,1024]{1,0:T(8,128)(2,1)}, bf16[3136,512]{1,0:T(8,128)(2,1)}, bf16[256,1024]{1,0:T(8,128)(2,1)}, bf16[1280,1024]{1,0:T(8,128)(2,1)}, ...) custom-call(bf16[3136,256]{1,0:T(8,128)(2,1)} %get-tuple-element.112.two, ...), custom_call_target="tpu_custom_call" | custom-call | tf_op jit(solution)/shard_map/pallas_call | solution.py:253
  218.2 36.1 %shard_map.391 = (bf16[9,256,256]{2,1,0:T(8,128)(2,1)}, f32[128,1152]{1,0:T(8,128)}, f32[3136,256]{1,0:T(8,128)}, f32[3136,128]{1,0:T(8,128)}, f32[2,384]{1,0:T(2,128)}, /*index=5*/f32[40,1024]{1,0:T(8,128)}) custom-call(f32[3136,256]{1,0:T(8,128)} %get-tuple-element.101.one_pre, f32[3136,256]{1,0:T(8,128)} %get-tuple-element.107.two_pre, ...), custom_call_target="tpu_custom_call" | custom-call | tf_op jit(solution)/shard_map/pallas_call | solution.py:253
  254.3 20.1 %shard_map.392 = (bf16[3,1280,256]{2,1,0:T(8,128)(2,1)}, bf16[3136,768]{1,0:T(8,128)(2,1)}, f32[72,256]{1,0:T(8,128)}) custom-call(bf16[3136,1024]{1,0:T(8,128)(2,1)} %bitcast.98, bf16[3136,256]{1,0:T(8,128)(2,1)} %get-tuple-element.108.lateral, f32[3136,256]{1,0:T(8,128)} %get-tuple-element.101.one_pre, f32[3136,256]{1,0:T(8,128)} %get-tuple-element.126.e_one, ...), custom_call_target="tpu_custom_call" | custom-call | tf_op jit(solution)/shard_map/pallas_call | solution.py:253
  274.5 33.6 %shard_map.393 = (bf16[3136,1024]{1,0:T(8,128)(2,1)}, f32[3136,256]{1,0:T(8,128)}, f32[2,256]{1,0:T(2,128)}, f32[8,1024]{1,0:T(8,128)}, f32[120,256]{1,0:T(8,128)}) custom-call(bf16[3136,768]{1,0:T(8,128)(2,1)} %get-tuple-element.129.pieces, bf16[3136,1024]{1,0:T(8,128)(2,1)} %get-tuple-element.130.d_proj, f32[3136,256]{1,0:T(8,128)} %get-tuple-element.95.lat_pre, ...), custom_call_target="tpu_custom_call" | custom-call | tf_op jit(solution)/shard_map/pallas_call | solution.py:253
  308.1 18.3 %shard_map.394 = (bf16[256,640]{1,0:T(8,128)(2,1)}, f32[384,128]{1,0:T(8,128)}, bf16[196,64,128]{2,1,0:T(8,128)(2,1)}, bf16[3136,1024]{1,0:T(8,128)(2,1)}, f32[2...) custom-call(bf16[3136,512]{1,0:T(8,128)(2,1)} %get-tuple-element.114, ...), custom_call_target="tpu_custom_call" | custom-call | tf_op jit(solution)/shard_map/pallas_call | solution.py:253
  326.4 16.6 %shard_map.395 = (f32[8,640]{1,0:T(8,128)}, f32[32,384]{1,0:T(8,128)}, f32[32,288]{1,0:T(8,128)}, f32[32,128]{1,0:T(8,128)}, f32[128,128]{1,0:T(8,128)}) custom-call(bf16[4,8,8,640]{3,2,1,0:T(8,128)(2,1)} %bitcast.128, f32[8,48,128]{2,1,0:T(8,128)} %bitcast.132), custom_call_target="tpu_custom_call" | custom-call | tf_op jit(solution)/shard_map/pallas_call | solution.py:1147
  343.0 1.3 copy.107
  344.3 1.4 copy.108
  345.7 1.4 copy.109
  347.2 1.3 copy.110
  348.5 1.5 copy.111
  (43 shorter events, 10.0 us)
Async XLA Ops:
  4.5 31.1 %copy-start.1 = (f32[2,1280]{1,0:T(2,128)}, f32[2,1280]{1,0:T(2,128)S(1)}, u32[]{:S(2)}) copy-start(f32[2,1280]{1,0:T(2,128)S(1)} %constant_dynamic-update-slice_fusion.5.fpair) | copy-start | bytes 30724
  36.0 0.6 copy-start

commit v3 on v2

--- a/solution.py
+++ b/solution.py
@@ -481,12 +481,91 @@
     return v.reshape((n * v.shape[4],) + v.shape[5:])
 
 
-def body0(n, *refs):
-    lat, norms, first = moves(n, refs[:3], refs[3:6], refs[6:])
+def at_lanes(v, offset):
+    rows, width = v.shape
+    wide = v if width == 128 else jnp.concatenate([v, jnp.zeros((rows, 128 - width), v.dtype)], axis=1)
+    return pltpu.roll(wide, offset, 1) if offset else wide
+
+
+def build_fast(first_t, middle_t, last, skip, mid_norm, out_norm, ids, band, fproj, fmid, flast, fpair, mask, lanes):
+    band[...] = jnp.zeros(band.shape, bf16)
+    fproj[...] = jnp.zeros(fproj.shape, bf16)
+    flast[...] = jnp.zeros(flast.shape, bf16)
+    none = jnp.zeros((96, 128), f32)
+    for tap in range(3):
+        block = jnp.concatenate([first_t[:, 128 * tap : 128 * (tap + 1)].astype(f32), none], axis=0).T
+        placed = [pltpu.roll(block, 32 * j, 1) if j else block for j in range(4)]
+        for part in range(3):
+            for k in range(4):
+                here = [j for j in range(4) if (j + tap - 1) % 4 == k and part == (1 if j + tap < 1 else 2 if j + tap > 4 else 0)]
+                if here:
+                    (j,) = here
+                    band[128 * k : 128 * (k + 1), 128 * part : 128 * (part + 1)] += placed[j].astype(bf16)
+    lanes[...] = jnp.zeros(lanes.shape, f32)
+    lanes[:, :288] = middle_t[...].astype(f32)
+    for group in range(3):
+        block = jnp.concatenate([lanes[:, 128 * group : 128 * (group + 1)], none], axis=0).T
+        for tap in range(4 * group, min(4 * group + 4, 9)):
+            part = block[32 * (tap % 4) : 32 * (tap % 4 + 1)]
+            for k in range(4):
+                fmid[128 * tap + 32 * k : 128 * tap + 32 * (k + 1)] = (pltpu.roll(part, 32 * k, 1) if k else part).astype(bf16)
+    for k in range(4):
+        flast[32 * k : 32 * (k + 1), 128 * k : 128 * (k + 1)] = last[...]
+    for k in range(2):
+        fproj[128 * k : 128 * (k + 1), 128 * k : 128 * (k + 1)] = skip[...]
+        narrow = at_lanes(mid_norm[k].astype(f32), 0)
+        wide = jnp.concatenate([narrow] * 4, axis=0)
+        fpair[:, 128 * k : 128 * (k + 1)] = sum(pltpu.roll(wide, 32 * j, 1) for j in range(1, 4))[:2] + narrow
+        for j in range(4):
+            fpair[:, 256 + 512 * k + 128 * j : 384 + 512 * k + 128 * j] = out_norm[k].astype(f32)
+    frames = mask.shape[1]
+    row = lax.broadcasted_iota(jnp.int32, (frames, frames), 0)
+    column = lax.broadcasted_iota(jnp.int32, (frames, frames), 1)
+    spread_ids = jnp.broadcast_to(ids[...].astype(f32), (frames, frames))
+    def pick(by):
+        return jnp.sum(jnp.where(column == row + by, spread_ids, 0.0), axis=1, keepdims=True)
+    at = lax.broadcasted_iota(jnp.int32, (frames, 1), 0)
+    here = pick(0)
+    prev = jnp.where((here == pick(-1)) & (at > 0), 1.0, 0.0)
+    after = jnp.where((here == pick(1)) & (at < frames - 1), 1.0, 0.0)
+    mask[0] = jnp.broadcast_to(prev, mask.shape[1:])
+    mask[1] = jnp.broadcast_to(after, mask.shape[1:])
+
+
+def pack_norms(pairs, out):
+    total, offset = None, 0
+    for pair in pairs:
+        v = at_lanes(jnp.concatenate([pair[...].astype(f32)] * 4, axis=0), offset)
+        total = v if total is None else total + v
+        offset += pair.shape[1]
+    out[...] = total
+
+
+def join_norms(gathered_of, shares, out):
+    n = gathered_of.shape[0]
+    offset, lo = 0, 0
+    for share in shares:
+        wide = share * n
+        pick = lax.broadcasted_iota(jnp.int32, (128, wide), 0) == offset + lax.broadcasted_iota(jnp.int32, (128, wide), 1) % share
+        pick = jnp.where(pick, 1.0, 0.0).astype(bf16)
+        mine = lax.broadcasted_iota(jnp.int32, (n, wide), 0) == lax.broadcasted_iota(jnp.int32, (n, wide), 1) // share
+        for row in range(2):
+            each = dot(gathered_of[:, row, :].astype(bf16), pick)
+            out[row : row + 1, lo : lo + wide] = jnp.sum(jnp.where(mine, each, 0.0), axis=0, keepdims=True)
+        offset += share
+        lo += wide
+
+
+def body0(n, lat_shard, first_shard, p_lat, p_one, p_two, p_out, p_proj, first_t, middle_t, last_w, skip, mid_norm, out_norm, ids,
+          lat_whole, first_whole, spair, band, fproj, fmid, flast, fpair, mask, own, norms_whole, lanes, *sems):
+    lat, norms, first = moves(n, (lat_shard, own, first_shard), (lat_whole, norms_whole, first_whole), sems)
+    pairs = (p_lat, p_one, p_two, p_out, p_proj)
     greet(n)
+    pack_norms(pairs, own)
     greeted(n)
     for m in (lat, norms, first):
         m.start("z")
+    build_fast(first_t, middle_t, last_w, skip, mid_norm, out_norm, ids, band, fproj, fmid, flast, fpair, mask, lanes)
     for m in (lat, norms):
         m.wait("z")
         m.start("d")
@@ -494,18 +573,25 @@
     first.start("p", "c0")
     lat.wait("d")
     norms.wait("d")
+    join_norms(norms_whole[...].reshape(n, 8, 128), [p.shape[1] for p in pairs], spair)
     first.wait("p", "c0")
 
 
-def stage0(shards, n):
+def stage0(lat_shard, first_shard, pairs, fast, ids, n):
+    VM, ANY = pl.BlockSpec(memory_space=pltpu.VMEM), pl.BlockSpec(memory_space=pl.ANY)
+    shape_of = lambda shape, kind: jax.ShapeDtypeStruct(shape, kind)
+    small = tuple(pairs) + tuple(fast) + (ids,)
+    width = sum(p.shape[1] for p in pairs) * n
     return pl.pallas_call(
         functools.partial(body0, n),
-        in_specs=[pl.BlockSpec(memory_space=pl.ANY)] * len(shards),
-        out_specs=[pl.BlockSpec(memory_space=pl.ANY)] * len(shards),
-        out_shape=[jax.ShapeDtypeStruct(shape, kind) for shape, kind, _ in spread_shapes(shards, n)],
-        scratch_shapes=gather_scratch(len(shards), n),
+        in_specs=[ANY, ANY] + [VM] * len(small),
+        out_specs=[ANY, ANY] + [VM] * 7,
+        out_shape=[shape_of(s, k) for s, k, _ in spread_shapes([lat_shard, first_shard], n)]
+        + [shape_of((2, width), f32), shape_of((512, 384), bf16), shape_of((256, 256), bf16), shape_of((1152, 128), bf16),
+           shape_of((128, 512), bf16), shape_of((2, 1280), f32), shape_of((2, ids.shape[1], 256), f32)],
+        scratch_shapes=[pltpu.VMEM((8, 128), f32), pltpu.VMEM((n // 8, 2, 2, 2, 8, 128), f32), pltpu.VMEM((32, 384), f32)] + gather_scratch(3, n),
         compiler_params=pltpu.CompilerParams(collective_id=1, has_side_effects=True),
-    )(*shards)
+    )(lat_shard, first_shard, *small)
 
 
 def run_ticks(step, n, ticks, at):
@@ -1154,26 +1240,24 @@
         + [DS((INNER,)), DS((INNER,)), DS((depth,)), DS((depth,)), DS((INNER,)), DS((INNER,)), DS((INNER,)), DS((INNER,)), DS((depth,)), DS((depth,))],
         compiler_params=pltpu.CompilerParams(collective_id=10, has_side_effects=True),
     )(lat_term.reshape((depth, INNER) + share), packed)
+    lat_grad, first_t, middle_t, last, proj = stage11((lat_grad, first_t, middle_t, last, proj))
     return lat_grad, (first_t.T, middle_t.T, last, proj)
 
 
-def spread(weight, groups):
-    eye = jnp.eye(groups, dtype=weight.dtype)
-    r, c = weight.shape[-2:]
-    wide = eye[:, None, :, None] * weight[..., None, :, None, :]
-    return wide.reshape(weight.shape[:-2] + (groups * r, groups * c))
-
-
-def banded(fast_first):
-    table = np.zeros((3, 4, 3, 4), np.float32)
-    for tap in range(3):
-        for j in range(4):
-            k = j + tap - 1
-            part = 1 if k < 0 else 2 if k > 3 else 0
-            table[tap, k % 4, part, j] = 1
-    tap = fast_first.reshape(3, 128, 32)
-    total = sum(table[k].astype(tap.dtype)[:, None, :, :, None] * tap[k][None, :, None, None, :] for k in range(3))
-    return total.reshape(512, 384)
+def body11(*refs):
+    half = len(refs) // 2
+    for source, target in zip(refs[:half], refs[half:]):
+        target[...] = source[...]
+
+
+def stage11(arrays):
+    VM = pl.BlockSpec(memory_space=pltpu.VMEM)
+    return pl.pallas_call(
+        body11,
+        in_specs=[VM] * len(arrays),
+        out_specs=[VM] * len(arrays),
+        out_shape=[jax.ShapeDtypeStruct(v.shape, v.dtype) for v in arrays],
+    )(*arrays)
 
 
 def shards(slow_in, fast_in, clip_ids, lateral_weight, first_weight, middle_weight, last_weight, proj_weight,
@@ -1182,29 +1266,10 @@
     n = lax.axis_size("fsdp")
     side = slow_in.shape[1]
     count = slow_in.shape[0] * side * side * n
-    norms = jnp.concatenate([lat_norm, one_norm, two_norm, out_norm, proj_norm], axis=1).astype(f32)
-    norms = jnp.pad(norms, ((0, 6), (0, 128 - norms.shape[1])))
-    lat, norms_full, first = stage0([lateral_weight.T, norms, first_weight], n)
+    lat, first, spair, band, fproj, fmid, flast, fpair, mask = stage0(
+        lateral_weight.T, first_weight, (lat_norm, one_norm, two_norm, out_norm, proj_norm),
+        (fast_first.T, fast_middle.T, fast_last, fast_proj, fast_mid_norm, fast_out_norm), clip_ids, n)
     lat = gathered(lat, n)
-    norms_full = norms_full.reshape(n, 8, 128)
-    gains, offset = [], 0
-    for pair in (lat_norm, one_norm, two_norm, out_norm, proj_norm):
-        width = pair.shape[1]
-        gains.append(norms_full[:, :2, offset : offset + width].transpose(1, 0, 2).reshape(2, -1))
-        offset += width
-    spair = jnp.concatenate(gains, axis=1)
-    fpair = jnp.concatenate(
-        [jnp.tile(pair[k].astype(f32), (1, 4)) for pair in (fast_mid_norm, fast_out_norm) for k in range(2)], axis=1)
-    band = banded(fast_first)
-    fproj = spread(fast_proj, 2)
-    fmid = spread(fast_middle.reshape(9, 32, 32), 4)
-    fmid = fmid.reshape(-1, 128)
-    flast = spread(fast_last, 4)
-
-    same = (clip_ids[0, 1:] == clip_ids[0, :-1]).astype(f32)
-    closed = jnp.zeros((1,), f32)
-    mask = jnp.stack([jnp.concatenate([closed, same]), jnp.concatenate([same, closed])])
-    mask = jnp.broadcast_to(mask[:, :, None], mask.shape + (256,))
 
     def rows(v):
         return v.transpose(1, 2, 0, 3).reshape(-1, v.shape[3])

time: 351 us -> 331 us (0.943)
  local copies, waits for them, and re-layouts: 17.3 us -> 0 us
  other arithmetic: 6.14 us -> 0 us
    unnamed x22 -> x0, local copies, waits for them, and re-layouts: 9.89 us -> none
    pallas_call x1 -> x2, Pallas kernels: 19.4 us -> 22.9 us  [the longest x1 21.3 us: stage0(): pl.pallas_call(functools.partial(body0, n), in_specs=[ANY, ANY] + [VM] *...]
where the time goes in v3:
time: 331 us; the launch traced here: 330 us
  Pallas kernels  329 us (99%)
    pallas_call x10, Pallas kernels, run(): pl.pallas_call(body, grid=(STEPS,), in_specs=[spec(a.shape, how) for a, h...  279 us
    pallas_call x1, Pallas kernels, stage0(): pl.pallas_call(functools.partial(body0, n), in_specs=[ANY, ANY] + [VM] *...  21.3 us
    pallas_call x1, Pallas kernels, stage10(): pl.pallas_call(functools.partial(body10, n), in_specs=[pl.BlockSpec(memor...  16.6 us
    pallas_call x1, Pallas kernels, stage5x(): pl.pallas_call(functools.partial(body5x, n), in_specs=[pl.BlockSpec(memor...  11.1 us

profile of v3, /device:TPU:0, one launch (start us, length us, event | category | flops | bytes accessed | tf_op | source)
XLA Modules:
  0.0 330.0 jit_solution(2210524932868610290)
XLA Ops:
  0.7 21.3 %shard_map.356 = (bf16[4,2,2,2,8,640]{5,4,3,2,1,0:T(8,128)(2,1)}, bf16[4,2,2,2,120,256]{5,4,3,2,1,0:T(8,128)(2,1)}, f32[2,2816]{1,0:T(2,128)}, bf16[512,384]{1,0...) custom-call(bf16[8,640]{1,0:T(8,128)(2,1)} %bitcast.67, ...), custom_call_target="tpu_custom_call" | custom-call | tf_op jit(solution)/shard_map/pallas_call | solution.py:585
  22.0 23.6 %shard_map.357 = (bf16[3136,512]{1,0:T(8,128)(2,1)}, f32[3136,256]{1,0:T(8,128)}, f32[3136,128]{1,0:T(8,128)}, f32[4,896]{1,0:T(4,128)}, bf16[4,2,2,2,120,256]{5...) custom-call(bf16[196,64,128]{2,1,0:T(8,128)(2,1)} %bitcast.56, ...), custom_call_target="tpu_custom_call", output_to_operand_aliasing={{4}: (7, {})} | custom-call | tf_op jit(solution)/shard_map/pallas_call | solution.py:253
  45.6 26.0 %shard_map.358 = (bf16[3136,256]{1,0:T(8,128)(2,1)}, f32[3136,256]{1,0:T(8,128)}, f32[3136,128]{1,0:T(8,128)}, f32[4,384]{1,0:T(4,128)}, bf16[4,2,2,2,72,256]{5,...) custom-call(bf16[3136,1024]{1,0:T(8,128)(2,1)} %bitcast.41, ...), custom_call_target="tpu_custom_call", output_to_operand_aliasing={{4}: (9, {}), {5}: (10, {})} | custom-call | tf_op jit(solution)/shard_map/pallas_call | solution.py:253
  71.6 25.4 %shard_map.359 = (f32[3136,256]{1,0:T(8,128)}, bf16[3136,128]{1,0:T(8,128)(2,1)}, f32[4,768]{1,0:T(4,128)}, bf16[4,2,2,2,8,1024]{5,4,3,2,1,0:T(8,128)(2,1)}, bf16[4,2,2,2,40,1024]{5,4,3,2,1,0:T(8,128)(2,1)}) custom-call(f32[3136,256]{1,0:T(8,128)} %get-tuple-element.117.one_pre, ...), custom_call_target="tpu_custom_call", output_to_operand_aliasing={{3}: (7, {}), {4}: (8, {})} | custom-call | tf_op jit(solution)/shard_map/pallas_call | solution.py:253
  97.0 27.4 %shard_map.360 = (bf16[3136,256]{1,0:T(8,128)(2,1)}, f32[3136,1024]{1,0:T(8,128)}, f32[4,2048]{1,0:T(4,128)}) custom-call(f32[3136,256]{1,0:T(8,128)} %get-tuple-element.124.two_pre, bf16[3136,1024]{1,0:T(8,128)(2,1)} %bitcast.42, bf16[3136,256]{1,0:T(8,128)(2,1)} %get-tuple-element.125.lateral, f32[4,768]{1,0:T(4,128)} %get-tuple-element.126.n3, ...), custom_call_target="tpu_custom_call" | custom-call | tf_op jit(solution)/shard_map/pallas_call | solution.py:253
  124.4 27.2 %shard_map.361 = (bf16[3136,1024]{1,0:T(8,128)(2,1)}, bf16[196,64,128]{2,1,0:T(8,128)(2,1)}, f32[3136,1024]{1,0:T(8,128)}, f32[3136,512]{1,0:T(8,128)}, f32[3,1536]{1,0:T(4,128)}) custom-call(bf16[3136,256]{1,0:T(8,128)(2,1)} %get-tuple-element.129.two, f32[3136,1024]{1,0:T(8,128)} %get-tuple-element.130.proj_pre, bf16[3136,1024]{1,0:T(8,128)(2,1)} %bitcast.54, ...), custom_call_target="tpu_custom_call" | custom-call | tf_op jit(solution)/shard_map/pallas_call | solution.py:253
  151.6 11.1 %shard_map.362.s5 = f32[3,1536]{1,0:T(4,128)} custom-call(f32[3,1536]{1,0:T(4,128)} %get-tuple-element.138.own), custom_call_target="tpu_custom_call" | custom-call | tf_op jit(solution)/shard_map/pallas_call | solution.py:864
  162.7 40.8 %shard_map.363 = (bf16[3136,1024]{1,0:T(8,128)(2,1)}, bf16[3136,512]{1,0:T(8,128)(2,1)}, bf16[256,1024]{1,0:T(8,128)(2,1)}, bf16[1280,1024]{1,0:T(8,128)(2,1)}, ...) custom-call(bf16[3136,256]{1,0:T(8,128)(2,1)} %get-tuple-element.129.two, ...), custom_call_target="tpu_custom_call" | custom-call | tf_op jit(solution)/shard_map/pallas_call | solution.py:253
  203.5 36.2 %shard_map.364 = (bf16[9,256,256]{2,1,0:T(8,128)(2,1)}, f32[128,1152]{1,0:T(8,128)}, f32[3136,256]{1,0:T(8,128)}, f32[3136,128]{1,0:T(8,128)}, f32[2,384]{1,0:T(2,128)}, /*index=5*/f32[40,1024]{1,0:T(8,128)}) custom-call(f32[3136,256]{1,0:T(8,128)} %get-tuple-element.117.one_pre, f32[3136,256]{1,0:T(8,128)} %get-tuple-element.124.two_pre, ...), custom_call_target="tpu_custom_call" | custom-call | tf_op jit(solution)/shard_map/pallas_call | solution.py:253
  239.7 20.1 %shard_map.365 = (bf16[3,1280,256]{2,1,0:T(8,128)(2,1)}, bf16[3136,768]{1,0:T(8,128)(2,1)}, f32[72,256]{1,0:T(8,128)}) custom-call(bf16[3136,1024]{1,0:T(8,128)(2,1)} %bitcast.44, bf16[3136,256]{1,0:T(8,128)(2,1)} %get-tuple-element.125.lateral, f32[3136,256]{1,0:T(8,128)} %get-tuple-element.117.one_pre, f32[3136,256]{1,0:T(8,128)} %get-tuple-element.143.e_one, ...), custom_call_target="tpu_custom_call" | custom-call | tf_op jit(solution)/shard_map/pallas_call | solution.py:253
  259.9 33.6 %shard_map.366 = (bf16[3136,1024]{1,0:T(8,128)(2,1)}, f32[3136,256]{1,0:T(8,128)}, f32[2,256]{1,0:T(2,128)}, f32[8,1024]{1,0:T(8,128)}, f32[120,256]{1,0:T(8,128)}) custom-call(bf16[3136,768]{1,0:T(8,128)(2,1)} %get-tuple-element.146.pieces, bf16[3136,1024]{1,0:T(8,128)(2,1)} %get-tuple-element.147.d_proj, f32[3136,256]{1,0:T(8,128)} %get-tuple-element.110.lat_pre, ...), custom_call_target="tpu_custom_call" | custom-call | tf_op jit(solution)/shard_map/pallas_call | solution.py:253
  293.4 18.3 %shard_map.367 = (bf16[256,640]{1,0:T(8,128)(2,1)}, f32[384,128]{1,0:T(8,128)}, bf16[196,64,128]{2,1,0:T(8,128)(2,1)}, bf16[3136,1024]{1,0:T(8,128)(2,1)}, f32[2...) custom-call(bf16[3136,512]{1,0:T(8,128)(2,1)} %get-tuple-element.131, ...), custom_call_target="tpu_custom_call" | custom-call | tf_op jit(solution)/shard_map/pallas_call | solution.py:253
  311.7 16.6 %shard_map.368 = (f32[8,640]{1,0:T(8,128)}, f32[32,384]{1,0:T(8,128)}, f32[32,288]{1,0:T(8,128)}, f32[32,128]{1,0:T(8,128)}, f32[128,128]{1,0:T(8,128)}) custom-call(bf16[4,8,8,640]{3,2,1,0:T(8,128)(2,1)} %bitcast.63, f32[8,48,128]{2,1,0:T(8,128)} %bitcast.64), custom_call_target="tpu_custom_call" | custom-call | tf_op jit(solution)/shard_map/pallas_call | solution.py:1233
  328.4 1.6 shard_map.369

commit v4 on v3

--- a/solution.py
+++ b/solution.py
@@ -598,12 +598,13 @@
     @pl.when(step == 0)
     def _():
         greet(n)
-    for j in range(3):
+    for j in range(len(at)):
         @pl.when(step == at[j])
         def _(j=j):
             if j == 0:
                 greeted(n)
             ticks[j]()
+    return tuple(ticks) if len(at) == 3 else tuple(ticks[:3]) + (lambda: None, ticks[4])
 
 
 def strips(rows, width, body, init):
@@ -636,7 +637,7 @@
             for m in others:
                 m.wait("z")
         ticks = (begin, middle, lambda: None, lambda: None, finish)
-        run_ticks(step, n, ticks, (1, 4, 6))
+        ticks = run_ticks(step, n, ticks, (0, 4, 6))
     f = split_fours(raw, wide).astype(bf16)
     fast4[...] = f
     prev, nxt = mask[0], mask[1]
@@ -688,7 +689,7 @@
             proj.wait("p", "c0")
             middle.wait("c0", "c1", "c2")
         ticks = (begin, half, late, close, finish)
-        run_ticks(step, n, ticks, (1, 3, 5))
+        ticks = run_ticks(step, n, ticks, (0, 2, 4, 6))
 
     def put(block):
         part = fone_pre[pl.ds(pl.multiple_of(block * rows, 16), rows), :]
@@ -742,7 +743,7 @@
             for m in both:
                 m.wait("c1", "c2")
         ticks = (begin, half, lambda: None, lambda: None, finish)
-        run_ticks(step, n, ticks, (1, 5, 6))
+        ticks = run_ticks(step, n, ticks, (0, 5, 6))
 
     def put(block):
         part = one_pre[pl.ds(pl.multiple_of(block * rows, 16), rows), :]
@@ -942,7 +943,7 @@
     if n > 1:
         ticks = scatter_ticks(n, (proj_term,), (proj_grad,), rest[:11])
         swap = rest[11:]
-        run_ticks(step, n, ticks, (1, 3, 5))
+        ticks = run_ticks(step, n, ticks, (0, 2, 4, 6))
     rows = one_pre.shape[0]
 
     def put(block):
@@ -1002,7 +1003,7 @@
     step = pl.program_id(0)
     if n > 1:
         ticks = scatter_ticks(n, (middleerm,), (middle_grad,), rest)
-        run_ticks(step, n, ticks, (1, 2, 4))
+        run_ticks(step, n, ticks, (0, 2, 4))
 
         @pl.when(step == STEPS - 1)
         def _():
@@ -1045,7 +1046,7 @@
     if n > 1:
         ticks = scatter_ticks(n, (last_term, first_term), (last_grad, first_grad), rest[:16])
         swap = rest[16:]
-        run_ticks(step, n, ticks, (1, 3, 5))
+        ticks = run_ticks(step, n, ticks, (0, 2, 4, 6))
     clear_first(step, acc)
     wide = proj.shape[0] - 256
 

time: 331 us -> 336 us (1.015)
  Pallas kernels: 329 us -> 335 us
    pallas_call x10, Pallas kernels: 279 us -> 284 us  [run(): pl.pallas_call(body, grid=(STEPS,), in_specs=[spec(a.shape, how) for a, h...]
where the time goes in v4:
time: 336 us; the launch traced here: 335 us
  Pallas kernels  335 us (100%)
    pallas_call x10, Pallas kernels, run(): pl.pallas_call(body, grid=(STEPS,), in_specs=[spec(a.shape, how) for a, h...  284 us
    pallas_call x1, Pallas kernels, stage0(): pl.pallas_call(functools.partial(body0, n), in_specs=[ANY, ANY] + [VM] *...  21.3 us
    pallas_call x1, Pallas kernels, stage10(): pl.pallas_call(functools.partial(body10, n), in_specs=[pl.BlockSpec(memor...  16.4 us
    pallas_call x1, Pallas kernels, stage5x(): pl.pallas_call(functools.partial(body5x, n), in_specs=[pl.BlockSpec(memor...  11.1 us

profile of v4, /device:TPU:0, one launch (start us, length us, event | category | flops | bytes accessed | tf_op | source)
XLA Modules:
  0.0 335.5 jit_solution(5546945270821113743)
XLA Ops:
  0.7 21.3 %shard_map.356 = (bf16[4,2,2,2,8,640]{5,4,3,2,1,0:T(8,128)(2,1)}, bf16[4,2,2,2,120,256]{5,4,3,2,1,0:T(8,128)(2,1)}, f32[2,2816]{1,0:T(2,128)}, bf16[512,384]{1,0...) custom-call(bf16[8,640]{1,0:T(8,128)(2,1)} %bitcast.67, ...), custom_call_target="tpu_custom_call" | custom-call | tf_op jit(solution)/shard_map/pallas_call | solution.py:585
  22.0 23.6 %shard_map.357 = (bf16[3136,512]{1,0:T(8,128)(2,1)}, f32[3136,256]{1,0:T(8,128)}, f32[3136,128]{1,0:T(8,128)}, f32[4,896]{1,0:T(4,128)}, bf16[4,2,2,2,120,256]{5...) custom-call(bf16[196,64,128]{2,1,0:T(8,128)(2,1)} %bitcast.56, ...), custom_call_target="tpu_custom_call", output_to_operand_aliasing={{4}: (7, {})} | custom-call | tf_op jit(solution)/shard_map/pallas_call | solution.py:253
  45.6 27.6 %shard_map.358 = (bf16[3136,256]{1,0:T(8,128)(2,1)}, f32[3136,256]{1,0:T(8,128)}, f32[3136,128]{1,0:T(8,128)}, f32[4,384]{1,0:T(4,128)}, bf16[4,2,2,2,72,256]{5,...) custom-call(bf16[3136,1024]{1,0:T(8,128)(2,1)} %bitcast.41, ...), custom_call_target="tpu_custom_call", output_to_operand_aliasing={{4}: (9, {}), {5}: (10, {})} | custom-call | tf_op jit(solution)/shard_map/pallas_call | solution.py:253
  73.2 25.3 %shard_map.359 = (f32[3136,256]{1,0:T(8,128)}, bf16[3136,128]{1,0:T(8,128)(2,1)}, f32[4,768]{1,0:T(4,128)}, bf16[4,2,2,2,8,1024]{5,4,3,2,1,0:T(8,128)(2,1)}, bf16[4,2,2,2,40,1024]{5,4,3,2,1,0:T(8,128)(2,1)}) custom-call(f32[3136,256]{1,0:T(8,128)} %get-tuple-element.117.one_pre, ...), custom_call_target="tpu_custom_call", output_to_operand_aliasing={{3}: (7, {}), {4}: (8, {})} | custom-call | tf_op jit(solution)/shard_map/pallas_call | solution.py:253
  98.6 27.4 %shard_map.360 = (bf16[3136,256]{1,0:T(8,128)(2,1)}, f32[3136,1024]{1,0:T(8,128)}, f32[4,2048]{1,0:T(4,128)}) custom-call(f32[3136,256]{1,0:T(8,128)} %get-tuple-element.124.two_pre, bf16[3136,1024]{1,0:T(8,128)(2,1)} %bitcast.42, bf16[3136,256]{1,0:T(8,128)(2,1)} %get-tuple-element.125.lateral, f32[4,768]{1,0:T(4,128)} %get-tuple-element.126.n3, ...), custom_call_target="tpu_custom_call" | custom-call | tf_op jit(solution)/shard_map/pallas_call | solution.py:253
  126.0 27.2 %shard_map.361 = (bf16[3136,1024]{1,0:T(8,128)(2,1)}, bf16[196,64,128]{2,1,0:T(8,128)(2,1)}, f32[3136,1024]{1,0:T(8,128)}, f32[3136,512]{1,0:T(8,128)}, f32[3,1536]{1,0:T(4,128)}) custom-call(bf16[3136,256]{1,0:T(8,128)(2,1)} %get-tuple-element.129.two, f32[3136,1024]{1,0:T(8,128)} %get-tuple-element.130.proj_pre, bf16[3136,1024]{1,0:T(8,128)(2,1)} %bitcast.54, ...), custom_call_target="tpu_custom_call" | custom-call | tf_op jit(solution)/shard_map/pallas_call | solution.py:253
  153.2 11.1 %shard_map.362.s5 = f32[3,1536]{1,0:T(4,128)} custom-call(f32[3,1536]{1,0:T(4,128)} %get-tuple-element.138.own), custom_call_target="tpu_custom_call" | custom-call | tf_op jit(solution)/shard_map/pallas_call | solution.py:865
  164.4 40.8 %shard_map.363 = (bf16[3136,1024]{1,0:T(8,128)(2,1)}, bf16[3136,512]{1,0:T(8,128)(2,1)}, bf16[256,1024]{1,0:T(8,128)(2,1)}, bf16[1280,1024]{1,0:T(8,128)(2,1)}, ...) custom-call(bf16[3136,256]{1,0:T(8,128)(2,1)} %get-tuple-element.129.two, ...), custom_call_target="tpu_custom_call" | custom-call | tf_op jit(solution)/shard_map/pallas_call | solution.py:253
  205.2 36.5 %shard_map.364 = (bf16[9,256,256]{2,1,0:T(8,128)(2,1)}, f32[128,1152]{1,0:T(8,128)}, f32[3136,256]{1,0:T(8,128)}, f32[3136,128]{1,0:T(8,128)}, f32[2,384]{1,0:T(2,128)}, /*index=5*/f32[40,1024]{1,0:T(8,128)}) custom-call(f32[3136,256]{1,0:T(8,128)} %get-tuple-element.117.one_pre, f32[3136,256]{1,0:T(8,128)} %get-tuple-element.124.two_pre, ...), custom_call_target="tpu_custom_call" | custom-call | tf_op jit(solution)/shard_map/pallas_call | solution.py:253
  241.7 21.9 %shard_map.365 = (bf16[3,1280,256]{2,1,0:T(8,128)(2,1)}, bf16[3136,768]{1,0:T(8,128)(2,1)}, f32[72,256]{1,0:T(8,128)}) custom-call(bf16[3136,1024]{1,0:T(8,128)(2,1)} %bitcast.44, bf16[3136,256]{1,0:T(8,128)(2,1)} %get-tuple-element.125.lateral, f32[3136,256]{1,0:T(8,128)} %get-tuple-element.117.one_pre, f32[3136,256]{1,0:T(8,128)} %get-tuple-element.143.e_one, ...), custom_call_target="tpu_custom_call" | custom-call | tf_op jit(solution)/shard_map/pallas_call | solution.py:253
  263.6 35.5 %shard_map.366 = (bf16[3136,1024]{1,0:T(8,128)(2,1)}, f32[3136,256]{1,0:T(8,128)}, f32[2,256]{1,0:T(2,128)}, f32[8,1024]{1,0:T(8,128)}, f32[120,256]{1,0:T(8,128)}) custom-call(bf16[3136,768]{1,0:T(8,128)(2,1)} %get-tuple-element.146.pieces, bf16[3136,1024]{1,0:T(8,128)(2,1)} %get-tuple-element.147.d_proj, f32[3136,256]{1,0:T(8,128)} %get-tuple-element.110.lat_pre, ...), custom_call_target="tpu_custom_call" | custom-call | tf_op jit(solution)/shard_map/pallas_call | solution.py:253
  299.2 18.3 %shard_map.367 = (bf16[256,640]{1,0:T(8,128)(2,1)}, f32[384,128]{1,0:T(8,128)}, bf16[196,64,128]{2,1,0:T(8,128)(2,1)}, bf16[3136,1024]{1,0:T(8,128)(2,1)}, f32[2...) custom-call(bf16[3136,512]{1,0:T(8,128)(2,1)} %get-tuple-element.131, ...), custom_call_target="tpu_custom_call" | custom-call | tf_op jit(solution)/shard_map/pallas_call | solution.py:253
  317.4 16.4 %shard_map.368 = (f32[8,640]{1,0:T(8,128)}, f32[32,384]{1,0:T(8,128)}, f32[32,288]{1,0:T(8,128)}, f32[32,128]{1,0:T(8,128)}, f32[128,128]{1,0:T(8,128)}) custom-call(bf16[4,8,8,640]{3,2,1,0:T(8,128)(2,1)} %bitcast.63, f32[8,48,128]{2,1,0:T(8,128)} %bitcast.64), custom_call_target="tpu_custom_call" | custom-call | tf_op jit(solution)/shard_map/pallas_call | solution.py:1234
  333.9 1.6 shard_map.369

commit v5 on v3

--- a/solution.py
+++ b/solution.py
@@ -854,27 +854,24 @@
          pltpu.VMEM((part, 512), f32), pltpu.VMEM((part, 512), f32), pltpu.VMEM((3, 8, 1536), f32)])
 
 
-def body5x(n, own, out, *links):
-    greet(n)
-    greeted(n)
-    sum_pack(total_of(n, False, own, *links), out, ((1024, 1536, 128),))
-
-
-def stage5x(sums, n):
-    return pl.pallas_call(
-        functools.partial(body5x, n),
-        in_specs=[pl.BlockSpec(memory_space=pltpu.VMEM)],
-        out_specs=pl.BlockSpec(memory_space=pltpu.VMEM),
-        out_shape=jax.ShapeDtypeStruct(sums.shape, f32),
-        scratch_shapes=swap_scratch(sums.shape, n),
-        compiler_params=pltpu.CompilerParams(collective_id=6, has_side_effects=True),
-    )(sums)
-
-
-def body6(n, total, two, two_pre, proj_pre, slow, lateral, delta, fast4, ftwo, ftwo_pre, fdelta, n1, n2, n3, n4, s5, last, fproj, flast,
-          d_proj, d_fproj, last_term, proj_term, flast_term, e_two, e_ftwo, sums,
+def body6(n, total, two, two_pre, proj_pre, slow, lateral, delta, fast4, ftwo, ftwo_pre, fdelta, n1, n2, n3, n4, sums5, last, fproj, flast,
+          d_proj, d_fproj, last_term, proj_term, flast_term, e_two, e_ftwo, sums, s5,
           three, fthree, fskip, d_three, d_fthree, acc, last_acc, proj_acc, *swap):
     step = pl.program_id(0)
+    ticks = ()
+    if n > 1:
+        early, swap = swap[:7], swap[7:]
+        ticks = (None, None, None, lambda: None, lambda: None)
+
+    @pl.when(step == 0)
+    def _():
+        if n > 1:
+            greet(n)
+            greeted(n)
+            sum_pack(total_of(n, False, sums5, *early), s5, ((1024, 1536, 128),))
+        else:
+            sum_pack(sums5[...], s5, ((1024, 1536, 128),))
+
     rows = two.shape[0]
     clear_first(step, acc, last_acc, proj_acc, flast_term)
     three[...] = dot(two[...], last[...])
@@ -914,7 +911,7 @@
     e = dot_nt(d_fthree[...], flast[...]) * slope(scaled(h, n2[:, 256:]))
     e_ftwo[...] = e
     add_sums(step, acc, 256, (eighth(e), eighth(e * h)))
-    close_sums(step, acc, sums, ((256, 384, 32),), n, (), *swap)
+    close_sums(step, acc, sums, ((256, 384, 32),), n, ticks, *swap)
 
     @pl.when(step == STEPS - 1)
     def _():
@@ -922,17 +919,17 @@
         proj_term[...] = proj_acc[...].astype(bf16)
 
 
-def stage6(total, two, two_pre, proj_pre, slow, lateral, delta, fast4, ftwo, ftwo_pre, fdelta, n1, n2, n3, n4, s5, last, fproj, flast, n):
+def stage6(total, two, two_pre, proj_pre, slow, lateral, delta, fast4, ftwo, ftwo_pre, fdelta, n1, n2, n3, n4, sums5, last, fproj, flast, n):
     rows = two.shape[0]
     part = rows // STEPS
     return run(functools.partial(body6, n, total), rows,
         [(a, "rows") for a in (two, two_pre, proj_pre, slow, lateral, delta, fast4, ftwo, ftwo_pre, fdelta)]
-        + [(a, "all") for a in (n1, n2, n3, n4, s5, last, fproj, flast)],
+        + [(a, "all") for a in (n1, n2, n3, n4, sums5, last, fproj, flast)],
         [((rows, 1024), bf16, "rows"), ((rows, 512), bf16, "rows"), ((256, 1024), bf16, "all"), ((1280, 1024), bf16, "all"), ((128, 512), f32, "all"),
-         ((rows, 256), f32, "rows"), ((rows, 128), f32, "rows"), ((2, 384), f32, "all")],
+         ((rows, 256), f32, "rows"), ((rows, 128), f32, "rows"), ((2, 384), f32, "all"), (sums5.shape, f32, "all")],
         [pltpu.VMEM((part, 1024), f32), pltpu.VMEM((part, 512), f32), pltpu.VMEM((part, 512), f32),
          pltpu.VMEM((part, 1024), bf16), pltpu.VMEM((part, 512), bf16), pltpu.VMEM((2, 8, 384), f32),
-         pltpu.VMEM((256, 1024), f32), pltpu.VMEM((1280, 1024), f32)], n, (2, 384), 7)
+         pltpu.VMEM((256, 1024), f32), pltpu.VMEM((1280, 1024), f32)] + (swap_scratch(sums5.shape, n) if n > 1 else []), n, (2, 384), 7)
 
 
 def body7(n, side, total, one_pre, two_pre, e_two, fone_pre, ftwo_pre, e_ftwo, n1, n2, n3, s6, middle, fmid, proj_term,
@@ -942,7 +939,7 @@
     if n > 1:
         ticks = scatter_ticks(n, (proj_term,), (proj_grad,), rest[:11])
         swap = rest[11:]
-        run_ticks(step, n, ticks, (1, 3, 5))
+        run_ticks(step, n, ticks, (1, 4, 6))
     rows = one_pre.shape[0]
 
     def put(block):
@@ -1002,7 +999,7 @@
     step = pl.program_id(0)
     if n > 1:
         ticks = scatter_ticks(n, (middleerm,), (middle_grad,), rest)
-        run_ticks(step, n, ticks, (1, 2, 4))
+        run_ticks(step, n, ticks, (1, 3, 5))
 
         @pl.when(step == STEPS - 1)
         def _():
@@ -1045,7 +1042,7 @@
     if n > 1:
         ticks = scatter_ticks(n, (last_term, first_term), (last_grad, first_grad), rest[:16])
         swap = rest[16:]
-        run_ticks(step, n, ticks, (1, 3, 5))
+        run_ticks(step, n, ticks, (1, 4, 6))
     clear_first(step, acc)
     wide = proj.shape[0] - 256
 
@@ -1292,9 +1289,8 @@
     two, proj_pre, n4 = stage4(two_pre, slow, lateral, n3, last, proj, spair, n)
     slow_out, fast_out, delta, fdelta, local = stage5(
         two, proj_pre, rows(slow_cot), fast4, ftwo, raw(fast_cot), n1, n3, n4, last, fproj, flast)
-    s5 = stage5x(local, n)
-    d_proj, d_fproj, last_term, proj_term, flast_term, e_two, e_ftwo, s6 = stage6(
-        count, two, two_pre, proj_pre, slow, lateral, delta, fast4, ftwo, ftwo_pre, fdelta, n1, n2, n3, n4, s5, last, fproj, flast, n)
+    d_proj, d_fproj, last_term, proj_term, flast_term, e_two, e_ftwo, s6, s5 = stage6(
+        count, two, two_pre, proj_pre, slow, lateral, delta, fast4, ftwo, ftwo_pre, fdelta, n1, n2, n3, n4, local, last, fproj, flast, n)
     middle_term, fmid_term, e_one, e_fone, s7, proj_grad = stage7(
         count, one_pre, two_pre, e_two, fone_pre, ftwo_pre, e_ftwo, n1, n2, n3, s6, middle, fmid, proj_term, side, n)
     first_term, pieces, middle_grad = stage8(count, slow, lateral, one_pre, e_one, n2, s7, mask, middle_term.reshape(-1, 256), n)

time: 331 us -> 334 us (level)
  Pallas kernels: 329 us -> 333 us
    pallas_call x10, Pallas kernels: 279 us -> 293 us  [run(): pl.pallas_call(body, grid=(STEPS,), in_specs=[spec(a.shape, how) for a, h...]
    pallas_call x1 -> x0, Pallas kernels: 11.1 us -> none  [stage5x(): pl.pallas_call(functools.partial(body5x, n), in_specs=[pl.BlockSpec(memor...]
where the time goes in v5:
time: 334 us
  Pallas kernels  333 us (100%)
    pallas_call x10, Pallas kernels, run(): pl.pallas_call(body, grid=(STEPS,), in_specs=[spec(a.shape, how) for a, h...  293 us
    pallas_call x1, Pallas kernels, stage0(): pl.pallas_call(functools.partial(body0, n), in_specs=[ANY, ANY] + [VM] *...  21.3 us
    pallas_call x1, Pallas kernels, stage10(): pl.pallas_call(functools.partial(body10, n), in_specs=[pl.BlockSpec(memor...  16.6 us

profile of v5, /device:TPU:0, one launch (start us, length us, event | category | flops | bytes accessed | tf_op | source)
XLA Modules:
  0.0 333.6 jit_solution(5888802747830505352)
XLA Ops:
  0.7 21.3 %shard_map.356 = (bf16[4,2,2,2,8,640]{5,4,3,2,1,0:T(8,128)(2,1)}, bf16[4,2,2,2,120,256]{5,4,3,2,1,0:T(8,128)(2,1)}, f32[2,2816]{1,0:T(2,128)}, bf16[512,384]{1,0...) custom-call(bf16[8,640]{1,0:T(8,128)(2,1)} %bitcast.67, ...), custom_call_target="tpu_custom_call" | custom-call | tf_op jit(solution)/shard_map/pallas_call | solution.py:585
  22.0 23.6 %shard_map.357 = (bf16[3136,512]{1,0:T(8,128)(2,1)}, f32[3136,256]{1,0:T(8,128)}, f32[3136,128]{1,0:T(8,128)}, f32[4,896]{1,0:T(4,128)}, bf16[4,2,2,2,120,256]{5...) custom-call(bf16[196,64,128]{2,1,0:T(8,128)(2,1)} %bitcast.56, ...), custom_call_target="tpu_custom_call", output_to_operand_aliasing={{4}: (7, {})} | custom-call | tf_op jit(solution)/shard_map/pallas_call | solution.py:253
  45.6 26.0 %shard_map.358 = (bf16[3136,256]{1,0:T(8,128)(2,1)}, f32[3136,256]{1,0:T(8,128)}, f32[3136,128]{1,0:T(8,128)}, f32[4,384]{1,0:T(4,128)}, bf16[4,2,2,2,72,256]{5,...) custom-call(bf16[3136,1024]{1,0:T(8,128)(2,1)} %bitcast.41, ...), custom_call_target="tpu_custom_call", output_to_operand_aliasing={{4}: (9, {}), {5}: (10, {})} | custom-call | tf_op jit(solution)/shard_map/pallas_call | solution.py:253
  71.6 25.4 %shard_map.359 = (f32[3136,256]{1,0:T(8,128)}, bf16[3136,128]{1,0:T(8,128)(2,1)}, f32[4,768]{1,0:T(4,128)}, bf16[4,2,2,2,8,1024]{5,4,3,2,1,0:T(8,128)(2,1)}, bf16[4,2,2,2,40,1024]{5,4,3,2,1,0:T(8,128)(2,1)}) custom-call(f32[3136,256]{1,0:T(8,128)} %get-tuple-element.118.one_pre, ...), custom_call_target="tpu_custom_call", output_to_operand_aliasing={{3}: (7, {}), {4}: (8, {})} | custom-call | tf_op jit(solution)/shard_map/pallas_call | solution.py:253
  97.0 27.4 %shard_map.360 = (bf16[3136,256]{1,0:T(8,128)(2,1)}, f32[3136,1024]{1,0:T(8,128)}, f32[4,2048]{1,0:T(4,128)}) custom-call(f32[3136,256]{1,0:T(8,128)} %get-tuple-element.125.two_pre, bf16[3136,1024]{1,0:T(8,128)(2,1)} %bitcast.42, bf16[3136,256]{1,0:T(8,128)(2,1)} %get-tuple-element.126.lateral, f32[4,768]{1,0:T(4,128)} %get-tuple-element.127.n3, ...), custom_call_target="tpu_custom_call" | custom-call | tf_op jit(solution)/shard_map/pallas_call | solution.py:253
  124.4 27.2 %shard_map.361 = (bf16[3136,1024]{1,0:T(8,128)(2,1)}, bf16[196,64,128]{2,1,0:T(8,128)(2,1)}, f32[3136,1024]{1,0:T(8,128)}, f32[3136,512]{1,0:T(8,128)}, f32[3,1536]{1,0:T(4,128)}) custom-call(bf16[3136,256]{1,0:T(8,128)(2,1)} %get-tuple-element.130.two, f32[3136,1024]{1,0:T(8,128)} %get-tuple-element.131.proj_pre, bf16[3136,1024]{1,0:T(8,128)(2,1)} %bitcast.54, ...), custom_call_target="tpu_custom_call" | custom-call | tf_op jit(solution)/shard_map/pallas_call | solution.py:253
  151.6 52.1 %shard_map.362 = (bf16[3136,1024]{1,0:T(8,128)(2,1)}, bf16[3136,512]{1,0:T(8,128)(2,1)}, bf16[256,1024]{1,0:T(8,128)(2,1)}, bf16[1280,1024]{1,0:T(8,128)(2,1)}, ...) custom-call(bf16[3136,256]{1,0:T(8,128)(2,1)} %get-tuple-element.130, ...), custom_call_target="tpu_custom_call" | custom-call | tf_op jit(solution)/shard_map/pallas_call | solution.py:253
  203.7 37.2 %shard_map.363 = (bf16[9,256,256]{2,1,0:T(8,128)(2,1)}, f32[128,1152]{1,0:T(8,128)}, f32[3136,256]{1,0:T(8,128)}, f32[3136,128]{1,0:T(8,128)}, f32[2,384]{1,0:T(2,128)}, /*index=5*/f32[40,1024]{1,0:T(8,128)}) custom-call(f32[3136,256]{1,0:T(8,128)} %get-tuple-element.118.one_pre, f32[3136,256]{1,0:T(8,128)} %get-tuple-element.125.two_pre, ...), custom_call_target="tpu_custom_call" | custom-call | tf_op jit(solution)/shard_map/pallas_call | solution.py:253
  240.9 20.5 %shard_map.364 = (bf16[3,1280,256]{2,1,0:T(8,128)(2,1)}, bf16[3136,768]{1,0:T(8,128)(2,1)}, f32[72,256]{1,0:T(8,128)}) custom-call(bf16[3136,1024]{1,0:T(8,128)(2,1)} %bitcast.44, bf16[3136,256]{1,0:T(8,128)(2,1)} %get-tuple-element.126.lateral, f32[3136,256]{1,0:T(8,128)} %get-tuple-element.118.one_pre, f32[3136,256]{1,0:T(8,128)} %get-tuple-element.144.e_one, ...), custom_call_target="tpu_custom_call" | custom-call | tf_op jit(solution)/shard_map/pallas_call | solution.py:253
  261.4 35.7 %shard_map.365 = (bf16[3136,1024]{1,0:T(8,128)(2,1)}, f32[3136,256]{1,0:T(8,128)}, f32[2,256]{1,0:T(2,128)}, f32[8,1024]{1,0:T(8,128)}, f32[120,256]{1,0:T(8,128)}) custom-call(bf16[3136,768]{1,0:T(8,128)(2,1)} %get-tuple-element.147.pieces, bf16[3136,1024]{1,0:T(8,128)(2,1)} %get-tuple-element.148.d_proj, f32[3136,256]{1,0:T(8,128)} %get-tuple-element.111.lat_pre, ...), custom_call_target="tpu_custom_call" | custom-call | tf_op jit(solution)/shard_map/pallas_call | solution.py:253
  297.1 18.3 %shard_map.366 = (bf16[256,640]{1,0:T(8,128)(2,1)}, f32[384,128]{1,0:T(8,128)}, bf16[196,64,128]{2,1,0:T(8,128)(2,1)}, bf16[3136,1024]{1,0:T(8,128)(2,1)}, f32[2...) custom-call(bf16[3136,512]{1,0:T(8,128)(2,1)} %get-tuple-element.132, ...), custom_call_target="tpu_custom_call" | custom-call | tf_op jit(solution)/shard_map/pallas_call | solution.py:253
  315.4 16.6 %shard_map.367 = (f32[8,640]{1,0:T(8,128)}, f32[32,384]{1,0:T(8,128)}, f32[32,288]{1,0:T(8,128)}, f32[32,128]{1,0:T(8,128)}, f32[128,128]{1,0:T(8,128)}) custom-call(bf16[4,8,8,640]{3,2,1,0:T(8,128)(2,1)} %bitcast.63, f32[8,48,128]{2,1,0:T(8,128)} %bitcast.64), custom_call_target="tpu_custom_call" | custom-call | tf_op jit(solution)/shard_map/pallas_call | solution.py:1230
  332.0 1.6 shard_map.368

commit v6 on v3

--- a/solution.py
+++ b/solution.py
@@ -570,11 +570,9 @@
         m.wait("z")
         m.start("d")
     first.wait("z")
-    first.start("p", "c0")
     lat.wait("d")
     norms.wait("d")
     join_norms(norms_whole[...].reshape(n, 8, 128), [p.shape[1] for p in pairs], spair)
-    first.wait("p", "c0")
 
 
 def stage0(lat_shard, first_shard, pairs, fast, ids, n):
@@ -625,17 +623,20 @@
         swap = rest[3 * GATHER_SEMS :]
 
         def begin():
-            first.start("q", "c1")
+            first.start("p", "c0")
             for m in others:
                 m.start("z")
         def middle():
+            first.wait("p")
+            first.start("q", "c1")
+        def late():
             first.wait("q")
             first.start("c2")
         def finish():
-            first.wait("c1", "c2")
+            first.wait("c0", "c1", "c2")
             for m in others:
                 m.wait("z")
-        ticks = (begin, middle, lambda: None, lambda: None, finish)
+        ticks = (begin, middle, lambda: None, late, finish)
         run_ticks(step, n, ticks, (1, 4, 6))
     f = split_fours(raw, wide).astype(bf16)
     fast4[...] = f

time: 331 us -> 329 us (level)
  no operation moved by 1% of the time
where the time goes in v6:
time: 329 us; the launch traced here: 328 us
  Pallas kernels  328 us (100%)
    pallas_call x10, Pallas kernels, run(): pl.pallas_call(body, grid=(STEPS,), in_specs=[spec(a.shape, how) for a, h...  279 us
    pallas_call x1, Pallas kernels, stage0(): pl.pallas_call(functools.partial(body0, n), in_specs=[ANY, ANY] + [VM] *...  19.4 us
    pallas_call x1, Pallas kernels, stage10(): pl.pallas_call(functools.partial(body10, n), in_specs=[pl.BlockSpec(memor...  16.4 us
    pallas_call x1, Pallas kernels, stage5x(): pl.pallas_call(functools.partial(body5x, n), in_specs=[pl.BlockSpec(memor...  10.9 us

profile of v6, /device:TPU:0, one launch (start us, length us, event | category | flops | bytes accessed | tf_op | source)
XLA Modules:
  0.0 328.5 jit_solution(10789153095902676007)
XLA Ops:
  0.7 19.4 %shard_map.356 = (bf16[4,2,2,2,8,640]{5,4,3,2,1,0:T(8,128)(2,1)}, bf16[4,2,2,2,120,256]{5,4,3,2,1,0:T(8,128)(2,1)}, f32[2,2816]{1,0:T(2,128)}, bf16[512,384]{1,0...) custom-call(bf16[8,640]{1,0:T(8,128)(2,1)} %bitcast.67, ...), custom_call_target="tpu_custom_call" | custom-call | tf_op jit(solution)/shard_map/pallas_call | solution.py:583
  20.1 24.0 %shard_map.357 = (bf16[3136,512]{1,0:T(8,128)(2,1)}, f32[3136,256]{1,0:T(8,128)}, f32[3136,128]{1,0:T(8,128)}, f32[4,896]{1,0:T(4,128)}, bf16[4,2,2,2,120,256]{5...) custom-call(bf16[196,64,128]{2,1,0:T(8,128)(2,1)} %bitcast.56, ...), custom_call_target="tpu_custom_call", output_to_operand_aliasing={{4}: (7, {})} | custom-call | tf_op jit(solution)/shard_map/pallas_call | solution.py:253
  44.1 25.9 %shard_map.358 = (bf16[3136,256]{1,0:T(8,128)(2,1)}, f32[3136,256]{1,0:T(8,128)}, f32[3136,128]{1,0:T(8,128)}, f32[4,384]{1,0:T(4,128)}, bf16[4,2,2,2,72,256]{5,...) custom-call(bf16[3136,1024]{1,0:T(8,128)(2,1)} %bitcast.41, ...), custom_call_target="tpu_custom_call", output_to_operand_aliasing={{4}: (9, {}), {5}: (10, {})} | custom-call | tf_op jit(solution)/shard_map/pallas_call | solution.py:253
  70.0 25.6 %shard_map.359 = (f32[3136,256]{1,0:T(8,128)}, bf16[3136,128]{1,0:T(8,128)(2,1)}, f32[4,768]{1,0:T(4,128)}, bf16[4,2,2,2,8,1024]{5,4,3,2,1,0:T(8,128)(2,1)}, bf16[4,2,2,2,40,1024]{5,4,3,2,1,0:T(8,128)(2,1)}) custom-call(f32[3136,256]{1,0:T(8,128)} %get-tuple-element.117.one_pre, ...), custom_call_target="tpu_custom_call", output_to_operand_aliasing={{3}: (7, {}), {4}: (8, {})} | custom-call | tf_op jit(solution)/shard_map/pallas_call | solution.py:253
  95.6 27.5 %shard_map.360 = (bf16[3136,256]{1,0:T(8,128)(2,1)}, f32[3136,1024]{1,0:T(8,128)}, f32[4,2048]{1,0:T(4,128)}) custom-call(f32[3136,256]{1,0:T(8,128)} %get-tuple-element.124.two_pre, bf16[3136,1024]{1,0:T(8,128)(2,1)} %bitcast.42, bf16[3136,256]{1,0:T(8,128)(2,1)} %get-tuple-element.125.lateral, f32[4,768]{1,0:T(4,128)} %get-tuple-element.126.n3, ...), custom_call_target="tpu_custom_call" | custom-call | tf_op jit(solution)/shard_map/pallas_call | solution.py:253
  123.1 27.2 %shard_map.361 = (bf16[3136,1024]{1,0:T(8,128)(2,1)}, bf16[196,64,128]{2,1,0:T(8,128)(2,1)}, f32[3136,1024]{1,0:T(8,128)}, f32[3136,512]{1,0:T(8,128)}, f32[3,1536]{1,0:T(4,128)}) custom-call(bf16[3136,256]{1,0:T(8,128)(2,1)} %get-tuple-element.129.two, f32[3136,1024]{1,0:T(8,128)} %get-tuple-element.130.proj_pre, bf16[3136,1024]{1,0:T(8,128)(2,1)} %bitcast.54, ...), custom_call_target="tpu_custom_call" | custom-call | tf_op jit(solution)/shard_map/pallas_call | solution.py:253
  150.3 10.9 %shard_map.362.s5 = f32[3,1536]{1,0:T(4,128)} custom-call(f32[3,1536]{1,0:T(4,128)} %get-tuple-element.138.own), custom_call_target="tpu_custom_call" | custom-call | tf_op jit(solution)/shard_map/pallas_call | solution.py:865
  161.3 41.2 %shard_map.363 = (bf16[3136,1024]{1,0:T(8,128)(2,1)}, bf16[3136,512]{1,0:T(8,128)(2,1)}, bf16[256,1024]{1,0:T(8,128)(2,1)}, bf16[1280,1024]{1,0:T(8,128)(2,1)}, ...) custom-call(bf16[3136,256]{1,0:T(8,128)(2,1)} %get-tuple-element.129.two, ...), custom_call_target="tpu_custom_call" | custom-call | tf_op jit(solution)/shard_map/pallas_call | solution.py:253
  202.5 35.6 %shard_map.364 = (bf16[9,256,256]{2,1,0:T(8,128)(2,1)}, f32[128,1152]{1,0:T(8,128)}, f32[3136,256]{1,0:T(8,128)}, f32[3136,128]{1,0:T(8,128)}, f32[2,384]{1,0:T(2,128)}, /*index=5*/f32[40,1024]{1,0:T(8,128)}) custom-call(f32[3136,256]{1,0:T(8,128)} %get-tuple-element.117.one_pre, f32[3136,256]{1,0:T(8,128)} %get-tuple-element.124.two_pre, ...), custom_call_target="tpu_custom_call" | custom-call | tf_op jit(solution)/shard_map/pallas_call | solution.py:253
  238.1 20.3 %shard_map.365 = (bf16[3,1280,256]{2,1,0:T(8,128)(2,1)}, bf16[3136,768]{1,0:T(8,128)(2,1)}, f32[72,256]{1,0:T(8,128)}) custom-call(bf16[3136,1024]{1,0:T(8,128)(2,1)} %bitcast.44, bf16[3136,256]{1,0:T(8,128)(2,1)} %get-tuple-element.125.lateral, f32[3136,256]{1,0:T(8,128)} %get-tuple-element.117.one_pre, f32[3136,256]{1,0:T(8,128)} %get-tuple-element.143.e_one, ...), custom_call_target="tpu_custom_call" | custom-call | tf_op jit(solution)/shard_map/pallas_call | solution.py:253
  258.5 33.6 %shard_map.366 = (bf16[3136,1024]{1,0:T(8,128)(2,1)}, f32[3136,256]{1,0:T(8,128)}, f32[2,256]{1,0:T(2,128)}, f32[8,1024]{1,0:T(8,128)}, f32[120,256]{1,0:T(8,128)}) custom-call(bf16[3136,768]{1,0:T(8,128)(2,1)} %get-tuple-element.146.pieces, bf16[3136,1024]{1,0:T(8,128)(2,1)} %get-tuple-element.147.d_proj, f32[3136,256]{1,0:T(8,128)} %get-tuple-element.110.lat_pre, ...), custom_call_target="tpu_custom_call" | custom-call | tf_op jit(solution)/shard_map/pallas_call | solution.py:253
  292.1 18.3 %shard_map.367 = (bf16[256,640]{1,0:T(8,128)(2,1)}, f32[384,128]{1,0:T(8,128)}, bf16[196,64,128]{2,1,0:T(8,128)(2,1)}, bf16[3136,1024]{1,0:T(8,128)(2,1)}, f32[2...) custom-call(bf16[3136,512]{1,0:T(8,128)(2,1)} %get-tuple-element.131, ...), custom_call_target="tpu_custom_call" | custom-call | tf_op jit(solution)/shard_map/pallas_call | solution.py:253
  310.4 16.4 %shard_map.368 = (f32[8,640]{1,0:T(8,128)}, f32[32,384]{1,0:T(8,128)}, f32[32,288]{1,0:T(8,128)}, f32[32,128]{1,0:T(8,128)}, f32[128,128]{1,0:T(8,128)}) custom-call(bf16[4,8,8,640]{3,2,1,0:T(8,128)(2,1)} %bitcast.63, f32[8,48,128]{2,1,0:T(8,128)} %bitcast.64), custom_call_target="tpu_custom_call" | custom-call | tf_op jit(solution)/shard_map/pallas_call | solution.py:1234
  326.8 1.6 shard_map.369
